TPU v7x, 128 devices: a whole 4x4x4 slice. The times are simulated.
128 devices in a mesh: dp: 16 (over z, y_hi, core), tensor: 8 (over y_lo, x).
Axes of the slice: x: 4, y: 4 (y_hi: 2, y_lo: 2; y = y_hi * 2 + y_lo), z: 4, core: 2. Of those that a mesh axis runs over, the one named last changes fastest.
Arguments:
- streams: bfloat16 [2048, 4, 2048], P('dp'), may hold values from -6 to 6
- placement: int32 [16], replicated, may hold values from 0 to 15, as said below
- w_query: bfloat16 [2048, 2048], P(None, 'tensor')
- w_key: bfloat16 [2048, 2048], P(None, 'tensor')
- w_value: bfloat16 [2048, 2048], P(None, 'tensor'), may hold values from -0.125 to 0.125
- w_output: bfloat16 [2048, 2048], P('tensor'), may hold values from -0.5 to 0.5
- w_gate: bfloat16 [2048, 8192], P(None, 'tensor'), may hold values from -0.125 to 0.125
- w_up: bfloat16 [2048, 8192], P(None, 'tensor'), may hold values from -0.125 to 0.125
- w_down: bfloat16 [8192, 2048], P('tensor'), may hold values from -0.0625 to 0.0625
- mix_dynamic: float32 [2, 2048, 6], replicated, may hold values from -0.125 to 0.125
- mix_static: float32 [2, 4, 6], replicated, may hold values from -0.3 to 1.5, as said below
- cotangent: bfloat16 [2048, 4, 2048], P('dp'), may hold values from -6 to 6
Outputs:
- streams_out: bfloat16 [2048, 4, 2048], P('dp')
- grad_streams: bfloat16 [2048, 4, 2048], P('dp')
- grad_w_query: float32 [2048, 2048], P('dp', 'tensor')
- grad_w_key: float32 [2048, 2048], P('dp', 'tensor')
- grad_w_value: float32 [2048, 2048], P('dp', 'tensor')
- grad_w_output: float32 [2048, 2048], P('tensor', 'dp')
- grad_w_gate: float32 [2048, 8192], P('dp', 'tensor')
- grad_w_up: float32 [2048, 8192], P('dp', 'tensor')
- grad_w_down: float32 [8192, 2048], P('tensor', 'dp')
- grad_mix_dynamic: float32 [2, 2048, 6], P(None, 'dp')
- grad_mix_static: float32 [2, 4, 6], replicated
Inputs may be any that keep to these rules, and one draw needn't show every extreme that they name: placement is a permutation: placement[a] is the segment held by index a of dp; the first and the last index of dp always hold prompt spans. `mix_static`: columns 0 and 5 are positive; columns 1 to 4 form a matrix near the identity.
All inputs are finite; a program needn't handle non-finite values.
Results may differ from a plain program's by a relative error of at most 0.018.
Values may be sent and summed in bfloat16 or wider, within the bound.
No kernel may reach another device: no remote copies, remote signals or barrier semaphores. Data moves between devices by JAX's collectives and lax.ppermute only.
A program may use at most 192 MiB of HBM per device.

v0:
```python
import functools

import jax
import jax.numpy as jnp
import numpy as np
from jax import lax
from jax.experimental import pallas as pl
from jax.experimental.pallas import tpu as pltpu
from jax.sharding import Mesh
from jax.sharding import PartitionSpec as P

HEAD = 128
EPS = 1e-05
THETA = 10000.0
BF = jnp.bfloat16
F32 = jnp.float32
K = 4
DP = ("z", "yh", "core")
TP = ("yl", "x")
SMEM = pl.BlockSpec(memory_space=pltpu.SMEM)
NT = (((1,), (1,)), ((), ()))
TN = (((0,), (0,)), ((), ()))
NN = (((1,), (0,)), ((), ()))


def dot(a, b, dims=NN):
    return lax.dot_general(a, b, dims, preferred_element_type=F32)


def lmean(v):
    return jnp.mean(v, -1, keepdims=True)


def lsum(v):
    return jnp.sum(v, -1, keepdims=True)


def norm_parts(v):
    ctr = v - lmean(v)
    rstd = lax.rsqrt(lmean(ctr * ctr) + EPS)
    return ctr * rstd, rstd


def norm_back(g, xhat, rstd):
    return rstd * (g - lmean(g) - xhat * lmean(g * xhat))


def three(v):
    hi = v.astype(BF)
    rest = v - hi.astype(F32)
    mid = rest.astype(BF)
    low = (rest - mid.astype(F32)).astype(BF)
    return hi, mid, low


def lanes(rows, pairs, start=None):
    lane = lax.broadcasted_iota(jnp.int32, (rows, 128), 1)
    out = jnp.zeros((rows, 128), F32) if start is None else start
    for at, v in pairs:
        out = jnp.where(lane == at, v, out)
    return out


def fold_parts(z):
    return z + pltpu.roll(z, 120, 1) + pltpu.roll(z, 112, 1)


def turn(v, cos, sin):
    return v * cos + pltpu.roll(v, 64, 1) * sin


def params(limit, **kw):
    return pltpu.CompilerParams(vmem_limit_bytes=60 * 2**20, **kw)


def whole(shape):
    n = len(shape)
    return pl.BlockSpec(shape, lambda *_: (0,) * n)


def like(*shapes):
    return tuple(jax.ShapeDtypeStruct(s, d) for s, d in shapes)


def iota(shape, dim):
    return lax.broadcasted_iota(jnp.int32, shape, dim)


def order(rows, to_planes):
    count = rows // K
    a, b = iota((rows, rows), 0), iota((rows, rows), 1)
    if not to_planes:
        a, b = b, a
    return (a == (b % K) * count + b // K).astype(BF)


def planes(block):
    rows, _, width = block.shape
    v = dot(order(K * rows, True), block.reshape(K * rows, width))
    return [v[k * rows : (k + 1) * rows] for k in range(K)]


def unplanes(parts):
    rows, width = parts[0].shape
    v = dot(order(K * rows, False), jnp.concatenate(parts, 0))
    return v.reshape(rows, K, width).astype(BF)


def stream_coefs(ref, rows):
    return [ref[pl.ds(k, rows, stride=K), :] for k in range(K)]


def static_rows(st_ref, layer, rows):
    row, lane = iota((rows, 128), 0) % K, iota((rows, 128), 1)
    out = jnp.zeros((rows, 128), F32)
    for k in range(K):
        for c in range(K + 2):
            out = jnp.where((row == k) & (lane == c), st_ref[layer, k, c], out)
    return out


def static_row(st_ref, layer, k):
    lane = iota((1, 128), 1)
    out = jnp.zeros((1, 128), F32)
    for c in range(K + 2):
        out = jnp.where(lane == c, st_ref[layer, k, c], out)
    return out


def fill_parts(m, wide_ref, mp_ref):
    cols = m.shape[0]
    wide_ref[...] = jnp.zeros_like(wide_ref)
    for i, v in enumerate(three(m)):
        wide_ref[8 * i : 8 * i + cols, :] = v.astype(F32)
    wide_ref[24:25, :] = jnp.ones((1, m.shape[1]), F32)
    mp_ref[...] = jnp.zeros_like(mp_ref)
    mp_ref[0:32, :] = wide_ref[...].astype(BF)


def device_index():
    core = lax.axis_index("core")
    return (lax.axis_index("z") * 2 + lax.axis_index("yh")) * 2 + core, core


def first_kernel(place_ref, st_ref, freq_ref, s_ref, m_ref, wq_ref, wk_ref, wv_ref,
                 n_ref, c_ref, qkv_ref, trig_ref, wide_ref, mp_ref):
    rows, _, width = s_ref.shape
    fill_parts(m_ref[0], wide_ref, mp_ref)
    sums = fold_parts(dot(jnp.ones((16, width), BF), mp_ref[...], NT))[0:1]
    step = 32
    part = K * step
    static = static_rows(st_ref, 0, part)
    row, lane = iota((part, 128), 0), iota((part, 128), 1)
    mine = (lane % step) == row // K

    def body(i, carry):
        r = pl.multiple_of(i * step, step)
        low = s_ref[pl.ds(r, step)].reshape(part, width)
        z = dot(low, mp_ref[...], NT)
        s = low.astype(F32)
        mean = z[:, 24:25] * (1.0 / width)
        ctr = s - mean
        rstd = lax.rsqrt(lmean(ctr * ctr) + EPS)
        c = static + jnp.tanh(rstd * (fold_parts(z) - mean * sums))
        c_ref[pl.ds(pl.multiple_of(i * part, part), part), :] = lanes(part, ((8, mean), (9, rstd)), c)
        a, b, d = (v.astype(F32) for v in three(c[:, 0:1]))
        take = jnp.where(lane < step, a, jnp.where(lane < 2 * step, b, d))
        take = jnp.where(mine & (lane < 3 * step), take, 0.0).astype(BF)
        w = dot(take, low, TN)
        taken = w[0:step] + w[step : 2 * step] + w[2 * step : 3 * step]
        n_ref[pl.ds(r, step), :] = norm_parts(taken)[0].astype(BF)
        return carry

    lax.fori_loop(0, rows // step, body, 0)
    me, _ = device_index()
    prompts = place_ref.shape[0] // 2
    start = jnp.minimum(place_ref[me], prompts) * rows
    angle = (start + iota((rows, HEAD), 0)).astype(F32) * freq_ref[...]
    cos = jnp.cos(angle)
    sin = jnp.where(iota((rows, HEAD), 1) < HEAD // 2, -1.0, 1.0) * jnp.sin(angle)
    trig_ref[0] = cos
    trig_ref[1] = sin
    normed = n_ref[...]
    q = dot(normed, wq_ref[...])
    k = dot(normed, wk_ref[...])
    heads = q.shape[1] // HEAD
    for h in range(heads):
        cut = slice(h * HEAD, (h + 1) * HEAD)
        qkv_ref[:, cut] = turn(q[:, cut], cos, sin).astype(BF)
        kcut = slice((heads + h) * HEAD, (heads + h + 1) * HEAD)
        qkv_ref[:, kcut] = turn(k[:, cut], cos, sin).astype(BF)
    qkv_ref[:, 2 * heads * HEAD :] = dot(normed, wv_ref[...]).astype(BF)


def first(place, st, streams, mt, wq, wk, wv):
    rows, _, width = streams.shape
    cols = wq.shape[1]
    half = HEAD // 2
    freq = np.float32(THETA) ** (-np.arange(half, dtype=np.float32) / np.float32(half))
    freq = jnp.asarray(np.concatenate([freq, freq])[None].astype(np.float32))
    outs = (
        ((rows, width), BF),
        ((K * rows, 128), F32),
        ((rows, 3 * cols), BF),
        ((2, rows, HEAD), F32),
    )
    return pl.pallas_call(
        first_kernel,
        grid=(1,),
        out_shape=like(*outs),
        in_specs=[SMEM, SMEM, whole(freq.shape), whole(streams.shape),
                  pl.BlockSpec((1, *mt.shape[1:]), lambda i: (0, 0, 0)),
                  whole(wq.shape), whole(wk.shape), whole(wv.shape)],
        out_specs=[whole(s) for s, _ in outs],
        scratch_shapes=[pltpu.VMEM((32, width), F32), pltpu.VMEM((128, width), BF)],
        compiler_params=params(26),
        name="first",
    )(place, st, freq, streams, mt, wq, wk, wv)


def own_blocks(place_ref, own_ref, same_ref, other_ref):
    me, core = device_index()
    own = place_ref[me]
    count = place_ref.shape[0]
    prompts = count // 2
    is_cont = own >= prompts
    blocks = []
    for s in range(prompts):
        d = jnp.int32(0)
        for a in range(count):
            d = jnp.where(place_ref[a] == s, a, d)
        block = jnp.where((d % 2) == core, same_ref[d // 2], other_ref[d // 2])
        reach = jnp.where(is_cont | (s < own), 4096, jnp.where(s == own, 0, -4096))
        blocks.append((block, reach))
    blocks.append((own_ref[...], jnp.where(is_cont, 0, -4096)))
    return blocks


def key_after_query(keys, queries):
    return iota((keys, queries), 0) - iota((keys, queries), 1)


def vector_rows(*vectors):
    row = iota((16, vectors[0].shape[1]), 0)
    out = jnp.zeros(row.shape, F32)
    for i, v in enumerate(vectors):
        for n, p in enumerate(three(v)):
            out = jnp.where(row == 3 * i + n, p.astype(F32), out)
    return out


def vector_of(rows16, i):
    v = rows16.astype(F32)
    return v[3 * i : 3 * i + 1] + v[3 * i + 1 : 3 * i + 2] + v[3 * i + 2 : 3 * i + 3]


def head_cuts(cols, h):
    return [slice(i * cols + h * HEAD, i * cols + (h + 1) * HEAD) for i in range(3)]


def attend_kernel(place_ref, own_ref, same_ref, other_ref, wo_ref, at_ref, log_ref, part_ref):
    rows, cols = at_ref.shape
    heads = cols // HEAD
    scale = HEAD ** (-0.5)
    blocks = own_blocks(place_ref, own_ref, same_ref, other_ref)
    lag = key_after_query(rows, rows)
    logs = []
    for h in range(heads):
        cut, kcut, vcut = head_cuts(cols, h)
        q = own_ref[:, cut]
        scores = [
            jnp.where(lag <= reach, dot(b[:, kcut], q, NT) * scale, -1e30) for b, reach in blocks
        ]
        top = functools.reduce(jnp.maximum, [jnp.max(s, 0, keepdims=True) for s in scores])
        terms = [jnp.exp(s - top) for s in scores]
        total = functools.reduce(jnp.add, [jnp.sum(e, 0, keepdims=True) for e in terms])
        inv = 1.0 / total
        out = None
        for e, (b, _) in zip(terms, blocks):
            o = dot((e * inv).astype(BF), b[:, vcut], TN)
            out = o if out is None else out + o
        at_ref[:, cut] = out.astype(BF)
        logs.append(top + jnp.log(total))
    log_ref[...] = jnp.concatenate(logs, 1)
    part_ref[...] = dot(at_ref[...], wo_ref[...]).astype(BF)


def attend(place, own, same, other, wo):
    rows = own.shape[0]
    cols = wo.shape[0]
    args = (own, same, other, wo)
    outs = (((rows, cols), BF), ((1, cols), F32), ((rows, wo.shape[1]), BF))
    return pl.pallas_call(
        attend_kernel,
        grid=(1,),
        out_shape=like(*outs),
        in_specs=[SMEM] + [whole(v.shape) for v in args],
        out_specs=[whole(s) for s, _ in outs],
        compiler_params=params(16),
        name="attend",
    )(place, *args)


def middle_kernel(t_ref, st_ref, parts_ref, s_ref, c_ref, m_ref, s1_ref, b1_ref, c2_ref, pay_ref,
                  wide_ref, mp_ref, split_ref):
    fill_parts(m_ref[0], wide_ref, mp_ref)
    b1 = jnp.sum(parts_ref[...].astype(F32), 0)
    b1_ref[...] = b1
    rows, width = b1.shape
    s0 = planes(s_ref[...])
    c1 = stream_coefs(c_ref, rows)
    stats = []
    for j in range(K):
        v = c1[j][:, 5:6] * b1
        for k in range(K):
            v = v + c1[k][:, 1 + j : 2 + j] * s0[k]
        s1_ref[j] = v
        mean = lmean(v)
        ctr = v - mean
        stats.append((mean, lax.rsqrt(lmean(ctr * ctr) + EPS)))
        hi = ctr.astype(BF)
        split_ref[j * rows : (j + 1) * rows, :] = hi
        split_ref[(K + j) * rows : (K + j + 1) * rows, :] = (ctr - hi.astype(F32)).astype(BF)
    z = dot(split_ref[...], mp_ref[...], NT)
    taken, gives = None, []
    for j in range(K):
        mean, rstd = stats[j]
        zj = z[j * rows : (j + 1) * rows] + z[(K + j) * rows : (K + j + 1) * rows]
        c = static_row(st_ref, 1, j) + jnp.tanh(rstd * fold_parts(zj))
        c2_ref[j] = lanes(rows, ((8, mean), (9, rstd)), c)
        part = c[:, 0:1] * s1_ref[j]
        taken = part if taken is None else taken + part
        gives += [(4 * i + j, v.astype(F32)) for i, v in enumerate(three(c[:, 5:6]))]
    pay_ref[:, 0:width] = norm_parts(taken)[0].astype(BF)
    pay_ref[:, width:] = lanes(rows, gives).astype(BF)


def token_call(kernel, name, t, tables, args, outs, scratch, limit):
    in_specs = [SMEM] * len(tables)
    for v, block in args:
        if block is None:
            in_specs.append(pl.BlockSpec(v.shape, lambda i, t, n=v.ndim: (0,) * n))
        else:
            in_specs.append(pl.BlockSpec(block, lambda i, t, n=v.ndim: (t[0],) + (0,) * (n - 1)))
    return pl.pallas_call(
        kernel,
        grid_spec=pltpu.PrefetchScalarGridSpec(
            num_scalar_prefetch=1,
            grid=(1,),
            in_specs=in_specs,
            out_specs=[pl.BlockSpec(s, lambda i, t, n=len(s): (0,) * n) for s, _ in outs],
            scratch_shapes=scratch,
        ),
        out_shape=like(*outs),
        compiler_params=params(limit),
        name=name,
    )(t, *tables, *[v for v, _ in args])


def middle(t, st, parts, streams, c1, mt_two):
    _, rows, width = parts.shape
    return token_call(
        middle_kernel,
        "middle",
        t,
        (st,),
        (
            (parts, None),
            (streams, (rows, K, width)),
            (c1, (K * rows, 128)),
            (mt_two, None),
        ),
        (
            ((K, rows, width), F32),
            ((rows, width), F32),
            ((K, rows, 128), F32),
            ((rows, width + 128), BF),
        ),
        [
            pltpu.VMEM((32, width), F32),
            pltpu.VMEM((128, width), BF),
            pltpu.VMEM((2 * K * rows, width), BF),
        ],
        12,
    )


def columns_for(step, count, piece):
    at = lax.rem(lax.axis_index("z") + step, count) * piece
    return pl.ds(pl.multiple_of(at, piece), piece)


def feed_kernel(pay_ref, cot_ref, wg_ref, wu_ref, wd_ref, *refs):
    *xy_refs, acts_ref, out_ref, gb_ref, b_ref, l_ref = refs
    step, steps = pl.program_id(0), pl.num_programs(0)
    rows, width = gb_ref.shape
    piece = width // len(xy_refs)

    @pl.when(step == 0)
    def _():
        chunk = 32
        row, lane = iota((chunk, K * chunk), 0), iota((chunk, K * chunk), 1)

        def body(i, carry):
            r = pl.multiple_of(i * chunk, chunk)
            give = pay_ref[pl.ds(r, chunk), width:].astype(F32)
            block = cot_ref[pl.ds(r, chunk)].reshape(K * chunk, width)
            total = None
            for n in range(3):
                w = jnp.zeros((chunk, K * chunk), F32)
                for j in range(K):
                    w = jnp.where(lane == K * row + j, give[:, K * n + j : K * n + j + 1], w)
                part = dot(w.astype(BF), block)
                total = part if total is None else total + part
            gb_ref[pl.ds(r, chunk), :] = total.astype(BF)
            return carry

        lax.fori_loop(0, rows // chunk, body, 0)
        for i, ref in enumerate(xy_refs):
            at = columns_for(i, len(xy_refs), piece)
            ref[:, 0:piece] = pay_ref[:, at]
            ref[:, piece:] = gb_ref[:, at]
        b_ref[...] = jnp.zeros_like(b_ref)
        l_ref[...] = jnp.zeros_like(l_ref)

    normed = pay_ref[:, 0:width]
    gate = dot(normed, wg_ref[...])
    up = dot(normed, wu_ref[...])
    sig = 1.0 / (1.0 + jnp.exp(-gate))
    silu = gate * sig
    hidden = (silu * up).astype(BF)
    grad = dot(gb_ref[...], wd_ref[...], NT)
    grad_gate = (grad * up * (sig * (1.0 + gate * (1.0 - sig)))).astype(BF)
    grad_up = (grad * silu).astype(BF)
    tile = hidden.shape[1]
    acts_ref[:, 0:tile] = grad_gate
    acts_ref[:, tile : 2 * tile] = grad_up
    acts_ref[:, 2 * tile :] = hidden
    b_ref[...] += dot(hidden, wd_ref[...])
    l_ref[...] += dot(grad_gate, wg_ref[...], NT) + dot(grad_up, wu_ref[...], NT)

    @pl.when(step == steps - 1)
    def _():
        out_ref[:, 0:width] = b_ref[...].astype(BF)
        out_ref[:, width:] = l_ref[...].astype(BF)


FEED_TILE = 256


def feed(pay, cotangent, wg, wu, wd, count):
    rows, _, width = cotangent.shape
    hidden = wg.shape[1]
    tile = FEED_TILE
    xy = (rows, 2 * width // count)
    return pl.pallas_call(
        feed_kernel,
        grid=(hidden // tile,),
        in_specs=[
            whole(pay.shape),
            whole(cotangent.shape),
            pl.BlockSpec((width, tile), lambda f: (0, f)),
            pl.BlockSpec((width, tile), lambda f: (0, f)),
            pl.BlockSpec((tile, width), lambda f: (f, 0)),
        ],
        out_specs=[
            *[whole(xy)] * count,
            pl.BlockSpec((rows, 3 * tile), lambda f: (0, f)),
            whole((rows, 2 * width)),
        ],
        out_shape=like(
            *[(xy, BF)] * count,
            ((rows, 3 * hidden), BF),
            ((rows, 2 * width), BF),
        ),
        scratch_shapes=[
            pltpu.VMEM((rows, width), BF),
            pltpu.VMEM((rows, width), F32),
            pltpu.VMEM((rows, width), F32),
        ],
        compiler_params=params(30),
        name="feed",
    )(pay, cotangent, wg, wu, wd)


def coef_back(grads, coefs, st_ref, layer, m, xhats, dm_ref, ds_ref, columns):
    rows = xhats[0].shape[0]
    dzs, statics = [], []
    for k in range(K):
        g = lanes(rows, grads[k].items())
        th = coefs[k] - static_row(st_ref, layer, k)
        dzs.append(g * (1.0 - th * th))
        statics.append(jnp.sum(g, 0, keepdims=True))
    ds_ref[layer] = jnp.concatenate(statics + [jnp.zeros((8 - K, 128), F32)], 0)
    for c in range(8):
        if c in columns:
            v = None
            for k in range(K):
                part = dzs[k][:, c : c + 1] * xhats[k]
                v = part if v is None else v + part
            dm_ref[layer, c : c + 1, :] = jnp.sum(v, 0, keepdims=True)
        else:
            dm_ref[layer, c : c + 1, :] = jnp.zeros((1, xhats[0].shape[1]), F32)
    out = []
    for k in range(K):
        v = None
        for c in columns:
            part = dzs[k][:, c : c + 1] * m[c : c + 1, :]
            v = part if v is None else v + part
        out.append(v)
    return out


def turn_kernel(t_ref, st_ref, parts_ref, s1_ref, c2_ref, cot_ref, s_ref, c1_ref, b1_ref, m_ref,
                s2_ref, gb1_ref, base_ref, dm_ref, ds_ref):
    rows, width = b1_ref.shape
    both = jnp.sum(parts_ref[...].astype(F32), 0)
    b2, gn = both[:, 0:width], both[:, width:]
    s1 = [s1_ref[k] for k in range(K)]
    c2 = [c2_ref[k] for k in range(K)]
    g2 = planes(cot_ref[...])
    grads = [dict() for _ in range(K)]
    taken, s2 = None, []
    for j in range(K):
        v = c2[j][:, 5:6] * b2
        for k in range(K):
            v = v + c2[k][:, 1 + j : 2 + j] * s1[k]
        s2.append(v.astype(BF))
        grads[j][5] = lsum(g2[j] * b2)
        for k in range(K):
            grads[k][1 + j] = lsum(g2[j] * s1[k])
        part = c2[j][:, 0:1] * s1[j]
        taken = part if taken is None else taken + part
    s2_ref[...] = unplanes(s2)
    normed, rstd = norm_parts(taken)
    gt = norm_back(gn, normed, rstd)
    for k in range(K):
        grads[k][0] = lsum(gt * s1[k])
    xhats = [(s1[k] - c2[k][:, 8:9]) * c2[k][:, 9:10] for k in range(K)]
    gx = coef_back(grads, c2, st_ref, 1, m_ref[1], xhats, dm_ref, ds_ref, range(6))
    g1 = []
    for k in range(K):
        v = c2[k][:, 0:1] * gt + norm_back(gx[k], xhats[k], c2[k][:, 9:10])
        for j in range(K):
            v = v + c2[k][:, 1 + j : 2 + j] * g2[j]
        g1.append(v)
    c1 = stream_coefs(c1_ref, rows)
    b1 = b1_ref[...]
    s0 = planes(s_ref[...])
    gb1 = None
    grads = [dict() for _ in range(K)]
    for j in range(K):
        part = c1[j][:, 5:6] * g1[j]
        gb1 = part if gb1 is None else gb1 + part
        grads[j][5] = lsum(g1[j] * b1)
        for k in range(K):
            grads[k][1 + j] = lsum(g1[j] * s0[k])
    gb1_ref[...] = gb1.astype(BF)
    xhats = [(s0[k] - c1[k][:, 8:9]) * c1[k][:, 9:10] for k in range(K)]
    gx = coef_back(grads, c1, st_ref, 0, m_ref[0], xhats, dm_ref, ds_ref, range(1, 6))
    base = []
    for k in range(K):
        v = norm_back(gx[k], xhats[k], c1[k][:, 9:10])
        for j in range(K):
            v = v + c1[k][:, 1 + j : 2 + j] * g1[j]
        base.append(v.astype(BF))
    base_ref[...] = unplanes(base)


def turn_back(t, st, parts, s1, c2, cotangent, streams, c1, b1, mt):
    rows, width = b1.shape
    block = (rows, K, width)
    return token_call(
        turn_kernel,
        "turn",
        t,
        (st,),
        (
            (parts, None),
            (s1, None),
            (c2, None),
            (cotangent, block),
            (streams, block),
            (c1, (K * rows, 128)),
            (b1, None),
            (mt, None),
        ),
        (
            (block, BF),
            ((rows, width), BF),
            (block, BF),
            ((2, 8, width), F32),
            ((2, 8, 128), F32),
        ),
        [],
        20,
    )


def query_kernel(place_ref, gb_ref, wo_ref, own_ref, log_ref, same_ref, other_ref, trig_ref,
                 at_ref, n_ref, do_ref, gq_ref, *ship_refs):
    rows, cols = gq_ref.shape
    heads = cols // HEAD
    scale = HEAD ** (-0.5)
    piece = gb_ref.shape[1] // len(ship_refs)
    grad = dot(gb_ref[...], wo_ref[...], NT).astype(BF)
    do_ref[0:rows, :] = grad
    blocks = own_blocks(place_ref, own_ref, same_ref, other_ref)
    lag = key_after_query(rows, rows)
    inners, logs = [], []
    for h in range(heads):
        cut, kcut, vcut = head_cuts(cols, h)
        q, do = own_ref[:, cut], grad[:, cut]
        log = log_ref[:, cut]
        logs.append(log)
        probs, gps, inner = [], [], None
        for b, reach in blocks:
            s = jnp.where(lag <= reach, dot(b[:, kcut], q, NT) * scale, -1e30)
            p = jnp.exp(s - log)
            gp = dot(b[:, vcut], do, NT)
            part = jnp.sum(p * gp, 0, keepdims=True)
            inner = part if inner is None else inner + part
            probs.append(p)
            gps.append(gp)
        gq = None
        for p, gp, (b, _) in zip(probs, gps, blocks):
            part = dot((p * (gp - inner)).astype(BF), b[:, kcut], TN)
            gq = part if gq is None else gq + part
        gq_ref[:, cut] = turn(gq * scale, trig_ref[0], -trig_ref[1]).astype(BF)
        inners.append(inner)
    do_ref[rows:, :] = jnp.concatenate(
        [vector_rows(i, log) for i, log in zip(inners, logs)], 1
    ).astype(BF)
    for i, ref in enumerate(ship_refs):
        at = columns_for(i, len(ship_refs), piece)
        ref[:, 0:piece] = gb_ref[:, at]
        ref[:, piece : 2 * piece] = n_ref[:, at]
        ref[:, 2 * piece :] = at_ref[...]


def query_back(place, gb1, wo, own, log, same, other, trig, attended, normed, count):
    rows, cols = attended.shape
    ship = ((rows, 2 * normed.shape[1] // count + cols), BF)
    args = (gb1, wo, own, log, same, other, trig, attended, normed)
    outs = (((rows + 16, cols), BF), ((rows, cols), BF), *[ship] * count)
    return pl.pallas_call(
        query_kernel,
        grid=(1,),
        out_shape=like(*outs),
        in_specs=[SMEM] + [whole(v.shape) for v in args],
        out_specs=[whole(s) for s, _ in outs],
        compiler_params=params(24),
        name="query_back",
    )(place, *args)


def key_kernel(place_ref, own_ref, qsame_ref, qother_ref, same_ref, other_ref, gq_ref, trig_ref,
               wq_ref, wk_ref, wv_ref, small_ref, part_ref):
    rows, cols = gq_ref.shape
    heads = cols // HEAD
    scale = HEAD ** (-0.5)
    me, core = device_index()
    own = place_ref[me]
    count = place_ref.shape[0]
    prompts = count // 2
    groups = [(g, rel) for g in range(count // 2) for rel in range(2)]
    reach = []
    for g, rel in groups:
        seg = place_ref[2 * g + (core + rel) % 2]
        full = (own < prompts) & (seg > own)
        value = jnp.where(full, 4096, jnp.where(seg == own, 0, -4096))
        reach.append(jnp.zeros((1, rows), jnp.int32) + value)
    reach = jnp.concatenate(reach, 1)
    lag = key_after_query(rows, rows)
    seen = jnp.concatenate([lag] * count, 1) <= reach
    for h in range(heads):
        cut, kcut, vcut = head_cuts(cols, h)
        k, v = own_ref[:, kcut], own_ref[:, vcut]
        qs, dos, logs, inners = [], [], [], []
        for g, rel in groups:
            src = same_ref if rel == 0 else other_ref
            qs.append((qsame_ref if rel == 0 else qother_ref)[g, :, cut])
            dos.append(src[g, 0:rows, cut])
            inners.append(vector_of(src[g, rows:, cut], 0))
            logs.append(vector_of(src[g, rows:, cut], 1))
        qs, dos = jnp.concatenate(qs, 0), jnp.concatenate(dos, 0)
        logs, inners = jnp.concatenate(logs, 1), jnp.concatenate(inners, 1)
        s = jnp.where(seen, dot(k, qs, NT) * scale, -1e30)
        p = jnp.exp(s - logs)
        gp = dot(v, dos, NT)
        ds = (p * (gp - inners)).astype(BF)
        gv = dot(p.astype(BF), dos)
        gk = dot(ds, qs) * scale
        small_ref[:, kcut] = turn(gk, trig_ref[0], -trig_ref[1]).astype(BF)
        small_ref[:, vcut] = gv.astype(BF)
    small_ref[:, 0:cols] = gq_ref[...]
    part = dot(gq_ref[...], wq_ref[...], NT)
    part += dot(small_ref[:, cols : 2 * cols], wk_ref[...], NT)
    part += dot(small_ref[:, 2 * cols :], wv_ref[...], NT)
    part_ref[...] = part.astype(BF)


def key_back(place, own, qsame, qother, same, other, gq, trig, wq, wk, wv):
    rows, cols = gq.shape
    args = (own, qsame, qother, same, other, gq, trig, wq, wk, wv)
    queries = pl.BlockSpec((*qsame.shape[:2], cols), lambda i: (0, 0, 0))
    specs = [whole(v.shape) for v in args]
    specs[1] = specs[2] = queries
    outs = (((rows, 3 * cols), BF), ((rows, wq.shape[0]), BF))
    return pl.pallas_call(
        key_kernel,
        grid=(1,),
        out_shape=like(*outs),
        in_specs=[SMEM] + specs,
        out_specs=[whole(s) for s, _ in outs],
        compiler_params=params(32),
        name="key_back",
    )(place, *args)


def last_kernel(t_ref, st_ref, parts_ref, s_ref, c_ref, dmin_ref, dsin_ref, gt_ref, dm_ref, ds_ref):
    gn = jnp.sum(parts_ref[...].astype(F32), 0)
    rows, width = gn.shape
    s0 = planes(s_ref[...])
    c1 = stream_coefs(c_ref, rows)
    taken = None
    for k in range(K):
        part = c1[k][:, 0:1] * s0[k]
        taken = part if taken is None else taken + part
    normed, rstd = norm_parts(taken)
    gt = norm_back(gn, normed, rstd)
    gt_ref[...] = gt.astype(BF)
    dm_ref[...] = dmin_ref[...]
    ds_ref[...] = dsin_ref[...]
    total = None
    lane = iota((1, 128), 1)
    for k in range(K):
        g = lsum(gt * s0[k])
        th = c1[k][:, 0:1] - st_ref[0, k, 0]
        part = g * (1.0 - th * th) * ((s0[k] - c1[k][:, 8:9]) * c1[k][:, 9:10])
        total = part if total is None else total + part
        ds_ref[0, k : k + 1, :] += jnp.where(lane == 0, jnp.sum(g, 0, keepdims=True), 0.0)
    dm_ref[0, 0:1, :] = jnp.sum(total, 0, keepdims=True)


def last(t, st, parts, streams, c1, dm, ds):
    _, rows, width = parts.shape
    return token_call(
        last_kernel,
        "last",
        t,
        (st,),
        (
            (parts, None),
            (streams, (rows, K, width)),
            (c1, (K * rows, 128)),
            (dm, None),
            (ds, None),
        ),
        (((rows, width), BF), (dm.shape, F32), (ds.shape, F32)),
        [],
        12,
    )


def final_kernel(st_ref, gt_ref, base_ref, s_ref, c_ref, m_ref, out_ref):
    rows, _, width = s_ref.shape
    part = K * rows
    spread = (iota((part, rows), 0) // K == iota((part, rows), 1)).astype(BF)
    gt = dot(spread, gt_ref[...])
    s0 = s_ref[...].reshape(part, width).astype(F32)
    c = c_ref[...]
    g = lsum(gt * s0)
    th = (c - static_rows(st_ref, 0, part))[:, 0:1]
    rstd = c[:, 9:10]
    xhat = (s0 - c[:, 8:9]) * rstd
    m = m_ref[0, 0:1, :]
    back = (m - lmean(m)) - xhat * lmean(m * xhat)
    v = base_ref[...].reshape(part, width).astype(F32) + c[:, 0:1] * gt
    v = v + (rstd * g * (1.0 - th * th)) * back
    out_ref[...] = v.astype(BF).reshape(rows, K, width)


def final(st, gt, base, streams, c1, mt):
    rows, _, width = streams.shape
    step = 32
    block = pl.BlockSpec((step, K, width), lambda i: (i, 0, 0))
    return pl.pallas_call(
        final_kernel,
        grid=(rows // step,),
        out_shape=jax.ShapeDtypeStruct(streams.shape, BF),
        in_specs=[
            SMEM,
            pl.BlockSpec((step, width), lambda i: (i, 0)),
            block,
            block,
            pl.BlockSpec((K * step, 128), lambda i: (i, 0)),
            whole(mt.shape),
        ],
        out_specs=block,
        compiler_params=params(20),
        name="final",
    )(st, gt, base, streams, c1, mt)


def weight_kernel(picks, tile, count, gathered, *refs):
    *lefts, keep_ref, give_ref, hold_ref = refs
    rights = lefts[-1:] if gathered else lefts[-count:]
    lefts = lefts[: -len(rights)]
    core, z = lax.axis_index("core"), lax.axis_index("z")
    mats = [
        jnp.concatenate([r[...] for r in lefts[i : i + count]], 0)
        for i in range(0, len(lefts), count)
    ]
    part = mats[0].shape[1] // 2
    for u, pick in enumerate(picks):
        cut = slice(u * tile, (u + 1) * tile)
        if gathered:
            right = [rights[0][lax.rem(z - i + count, count), :, cut] for i in range(count)]
        else:
            right = [r[:, cut] for r in rights]
        hold_ref[...] = dot(mats[pick], jnp.concatenate(right, 0), TN)
        keep_ref[0, u] = hold_ref[pl.ds(pl.multiple_of(core * part, part), part), :]
        give_ref[0, u] = hold_ref[pl.ds(pl.multiple_of((1 - core) * part, part), part), :].astype(BF)


def weight_part(left, offsets, right, right_at, tiles, picks, tile, name):
    count = len(left)
    rows = left[0].shape[0]
    units = len(picks)
    gathered = not isinstance(right, (list, tuple))
    shape = (2, units, 128, tiles * tile)
    out = pl.BlockSpec((1, units, 128, tile), lambda f, y: (y, 0, 0, f))
    specs = [
        pl.BlockSpec((rows, 256), lambda f, y, o=o: (0, o + y)) for o in offsets for _ in left
    ]
    if gathered:
        specs.append(pl.BlockSpec((count, rows, units * tile), lambda f, y: (0, 0, right_at + f)))
        right = [right]
    else:
        specs += [pl.BlockSpec((rows, units * tile), lambda f, y: (0, right_at + f))] * count
    return pl.pallas_call(
        functools.partial(weight_kernel, picks, tile, count, gathered),
        grid=(tiles, 2),
        in_specs=specs,
        out_specs=[out, out],
        out_shape=like((shape, F32), (shape, BF)),
        scratch_shapes=[pltpu.VMEM((256, tile), F32)],
        compiler_params=params(16),
        name=name,
    )(*[v for _ in offsets for v in left], *right)


def to_all(shard, axes):
    copies = jnp.broadcast_to(shard, (lax.axis_size(axes), *shard.shape))
    return lax.all_to_all(copies, axes, 0, 0, tiled=True)


def exchange(blocks, axes):
    return lax.all_to_all(blocks, axes, 0, 0, tiled=True)


def scatter_parts(partial, axes):
    n = lax.axis_size(axes)
    return exchange(partial.reshape(n, partial.shape[0] // n, partial.shape[1]), axes)


def swap(v, axis):
    return lax.ppermute(v, axis, [(0, 1), (1, 0)])


def over_chips(shard):
    same = to_all(shard, ("z", "yh"))
    return same, swap(same, "core")


def along_z(pieces):
    n = lax.axis_size("z")
    return [pieces[0]] + [
        lax.ppermute(pieces[i], "z", [(a, (a + i) % n) for a in range(n)]) for i in range(1, n)
    ]


def pick(v, at):
    return lax.dynamic_index_in_dim(v, at, 0, keepdims=False)


def over_yh(kept, got):
    yh = lax.axis_index("yh")
    give = pick(kept, 1 - yh) + pick(got, 1 - yh).astype(F32)
    return pick(kept, yh) + pick(got, yh).astype(F32) + swap(give.astype(BF), "yh").astype(F32)


def per_device(streams, placement, w_query, w_key, w_value, w_output, w_gate, w_up, w_down,
               mix_dynamic, mix_static, cotangent):
    rows, _, width = streams.shape
    groups = placement.shape[0]
    t = lax.axis_index(TP).astype(jnp.int32)[None]
    nz = lax.axis_size("z")
    mt = jnp.transpose(mix_dynamic, (0, 2, 1))

    normed_one, c1, own, trig = first(placement, mix_static, streams, mt, w_query, w_key, w_value)
    same, other = over_chips(own)
    attended, log, part_one = attend(placement, own, same, other, w_output)
    s1, b1, c2, pay = middle(t, mix_static, scatter_parts(part_one, TP), streams, c1, mt[1:2])
    pay = to_all(pay, TP).reshape(rows, width + 128)
    *xy, acts, part_two = feed(pay, cotangent, w_gate, w_up, w_down, nz)
    acts = lax.all_gather(acts, "z", axis=0)
    xy = along_z(xy)
    parts = scatter_parts(part_two, TP)
    s2, gb1, base, dm, ds = turn_back(t, mix_static, parts, s1, c2, cotangent, streams, c1, b1, mt)
    gb1 = to_all(gb1, TP).reshape(rows, width)
    base = lax.all_gather(base, TP, axis=0, tiled=True)
    streams_out = lax.all_gather(s2, TP, axis=0, tiled=True)
    do, gq, *ship = query_back(
        placement, gb1, w_output, own, log, same, other, trig, attended, normed_one, nz
    )
    ship = along_z(ship)
    do_same, do_other = over_chips(do)
    small, part_three = key_back(
        placement, own, same, other, do_same, do_other, gq, trig, w_query, w_key, w_value
    )
    small = along_z([small] * nz)
    parts = scatter_parts(part_three, TP)
    gt, dm, ds = last(t, mix_static, parts, streams, c1, dm, ds)
    gt = to_all(gt, TP).reshape(rows, width)
    grad_streams = final(mix_static, gt, base, streams, c1, mt)

    tiles = w_gate.shape[1] // FEED_TILE
    keep, give = weight_part(xy, (0, 2), acts, 0, tiles, (0, 0, 1), FEED_TILE, "feed_weights")
    ff = over_yh(keep, swap(give, "core"))
    keep, give = weight_part(ship, (0,), ship, 4, 1, (0,), 256, "output_weights")
    out = over_yh(keep, swap(give, "core"))
    keep, give = weight_part(ship, (2,), small, 0, 1, (0, 0, 0), 256, "qkv_weights")
    qkv = over_yh(keep, swap(give, "core"))

    spread = jnp.transpose(dm.reshape(16, groups, width // groups), (1, 0, 2))
    statics = jnp.broadcast_to(ds.reshape(1, 16, 128), (groups, 16, 128))
    packed = jnp.concatenate([spread, statics], 1)
    packed = jnp.sum(exchange(packed, DP), 0)
    packed = jnp.sum(to_all(packed, TP), 0)
    grad_dynamic = jnp.transpose(packed[:16].reshape(2, 8, -1)[:, :6], (0, 2, 1))
    grad_static = packed[16:].reshape(2, 8, 128)[:, :4, :6]
    return (
        streams_out,
        grad_streams,
        qkv[0],
        qkv[1],
        qkv[2],
        jnp.transpose(out[0]),
        ff[0],
        ff[1],
        jnp.transpose(ff[2]),
        grad_dynamic,
        grad_static,
    )


def solution(mesh):
    fine = Mesh(mesh.devices.reshape(4, 2, 2, 2, 4), ("z", "yh", "core", "yl", "x"))
    placed = (
        P(DP, None, None),
        P(),
        P(None, TP),
        P(None, TP),
        P(None, TP),
        P(TP, None),
        P(None, TP),
        P(None, TP),
        P(TP, None),
        P(),
        P(),
        P(DP, None, None),
    )
    return jax.shard_map(
        per_device,
        mesh=fine,
        in_specs=placed,
        out_specs=(
            P(DP, None, None),
            P(DP, None, None),
            P(DP, TP),
            P(DP, TP),
            P(DP, TP),
            P(TP, DP),
            P(DP, TP),
            P(DP, TP),
            P(TP, DP),
            P(None, DP, None),
            P(),
        ),
        check_vma=False,
    )
```

profile of v0, /device:TPU:0, one launch (start us, length us, event | category | flops | bytes accessed | tf_op | source)
XLA Modules:
  0.0 297.4 jit_solution(16546387235633336412)
XLA Ops:
  7.2 1.6 copy.45
  8.8 10.3 %first.1 = (bf16[128,2048]{1,0:T(8,128)(2,1)}, f32[512,128]{1,0:T(8,128)}, bf16[128,768]{1,0:T(8,128)(2,1)}, f32[2,128,128]{2,1,0:T(8,128)}) custom-call(s32[16]{0:T(128)} %place_ref.7, f32[2,4,6]{2,1,0:T(4,128)} %st_ref.9, f32[1,128]{1,0:T(1,128)} %constant.61.clone.freq_ref, bf16[128,4,2048]{2,1,0:T(4,128)(2,1)} %s_ref.9, f32[2,6,2048]{2,1,0:T(8,128)} %bitcast.57, ...), custom_call_target="tpu_custom_call" | custom-call | tf_op jit(solution)/shard_map/first/pallas_call | solution.py:207
  19.1 1.0 broadcast_in_dim.29
  20.1 30.6 %all_to_all.50.same_ref.qsame_ref = bf16[8,128,768]{2,1,0:T(8,128)(2,1)S(1)} all-to-all(bf16[8,128,768]{2,1,0:T(8,128)(2,1)S(1)} %broadcast_in_dim.29), channel_id=1, replica_groups=mesh['z'=4,'yh'=2,'core'=2,'yl'=2,'x'=4] {'z','yh'}, dimensions={0} | all-to-all | bytes 3145728 | tf_op jit(solution)/shard_map/all_to_all | solution.py:856
  50.8 3.4 %collective-permute-done.other_ref.qother_ref = bf16[8,128,768]{2,1,0:T(8,128)(2,1)S(1)} collective-permute-done((bf16[8,128,768]{2,1,0:T(8,128)(2,1)S(1)}, bf16[8,128,768]{2,1,0:T(8,128)(2,1)S(1)}, u32[]{:S(2)}, u32[]{:S(2)}) %collective-permute-start) | collective-permute-done | bytes 1572896 | tf_op jit(solution)/shard_map/ppermute | solution.py:869
  54.2 1.1 copy-done.1
  55.3 4.7 %attend.1 = (bf16[128,256]{1,0:T(8,128)(2,1)}, f32[1,256]{1,0:T(1,128)}, bf16[128,2048]{1,0:T(8,128)(2,1)}) custom-call(s32[16]{0:T(128)} %place_ref.7, bf16[128,768]{1,0:T(8,128)(2,1)} %get-tuple-element.50.own_ref, bf16[8,128,768]{2,1,0:T(8,128)(2,1)} %copy-done, bf16[8,128,768]{2,1,0:T(8,128)(2,1)} %copy-done.1, bf16[256,2048]{1,0:T(8,128)(2,1)} %wo_ref.3), custom_call_target="tpu_custom_call" | custom-call | tf_op jit(solution)/shard_map/attend/pallas_call | solution.py:293
  60.0 4.6 %all-to-all-start.1 = ((bf16[8,16,2048]{2,1,0:T(8,128)(2,1)}), bf16[8,16,2048]{2,1,0:T(8,128)(2,1)S(1)}, u32[]{:S(2)}, u32[]{:S(2)}) async-start(bf16[8,16,2048]{2,1,0:T(8,128)(2,1)} %bitcast.65), calls=%async_computation.1 | async-start | bytes 1048576 | tf_op jit(solution)/shard_map/all_to_all | solution.py:860
  65.3 9.7 %all-to-all-done.1.parts_ref = bf16[8,16,2048]{2,1,0:T(8,128)(2,1)S(1)} async-done(((bf16[8,16,2048]{2,1,0:T(8,128)(2,1)}), bf16[8,16,2048]{2,1,0:T(8,128)(2,1)S(1)}, u32[]{:S(2)}, u32[]{:S(2)}) %all-to-all-start.1) | async-done | bytes 524320 | tf_op jit(solution)/shard_map/all_to_all | solution.py:860
  75.0 0.8 copy-done.9
  75.8 2.9 middle.1
  78.7 0.9 broadcast_in_dim.30
  79.6 13.9 %all_to_all.51 = bf16[8,16,2176]{2,1,0:T(8,128)(2,1)} all-to-all(bf16[8,16,2176]{2,1,0:T(8,128)(2,1)S(1)} %broadcast_in_dim.30), channel_id=1, replica_groups=mesh['z'=4,'yh'=2,'core'=2,'yl'=2,'x'=4] {'yl','x'}, dimensions={0} | all-to-all | bytes 1114112 | tf_op jit(solution)/shard_map/all_to_all | solution.py:856
  93.5 13.9 %feed.1 = (bf16[128,1024]{1,0:T(8,128)(2,1)}, bf16[128,1024]{1,0:T(8,128)(2,1)}, bf16[128,1024]{1,0:T(8,128)(2,1)}, bf16[128,1024]{1,0:T(8,128)(2,1)}, bf16[128,...) custom-call(bf16[128,2176]{1,0:T(8,128)(2,1)} %bitcast.61, bf16[128,4,2048]{2,1,0:T(4,128)(2,1)} %cot_ref.3, ...), custom_call_target="tpu_custom_call" | custom-call | tf_op jit(solution)/shard_map/feed/pallas_call | solution.py:456
  107.4 18.9 %all_to_all.52.parts_ref = bf16[8,16,4096]{2,1,0:T(8,128)(2,1)} all-to-all(bf16[8,16,4096]{2,1,0:T(8,128)(2,1)} %bitcast.63), channel_id=1, replica_groups=mesh['z'=4,'yh'=2,'core'=2,'yl'=2,'x'=4] {'yl','x'}, dimensions={0} | all-to-all | bytes 2097152 | tf_op jit(solution)/shard_map/all_to_all | solution.py:860
  126.4 5.6 %turn.1 = (bf16[16,4,2048]{2,1,0:T(4,128)(2,1)}, bf16[16,2048]{1,0:T(8,128)(2,1)}, bf16[16,4,2048]{2,1,0:T(4,128)(2,1)}, f32[2,8,2048]{2,1,0:T(8,128)}, f32[2,8,128]{2,1,0:T(8,128)}) custom-call(s32[1]{0:T(128)} %bitcast.t_ref, f32[2,4,6]{2,1,0:T(4,128)} %st_ref.9, bf16[8,16,4096]{2,1,0:T(8,128)(2,1)} %all_to_all.52.parts_ref, ...), custom_call_target="tpu_custom_call" | custom-call | tf_op jit(solution)/shard_map/turn/pallas_call | solution.py:345
  132.8 0.9 broadcast_in_dim.31
  133.6 11.9 %all_to_all.53 = bf16[8,16,2048]{2,1,0:T(8,128)(2,1)} all-to-all(bf16[8,16,2048]{2,1,0:T(8,128)(2,1)S(1)} %broadcast_in_dim.31), channel_id=1, replica_groups=mesh['z'=4,'yh'=2,'core'=2,'yl'=2,'x'=4] {'yl','x'}, dimensions={0} | all-to-all | bytes 1048576 | tf_op jit(solution)/shard_map/all_to_all | solution.py:856
  145.6 6.1 %query_back.1 = (bf16[144,256]{1,0:T(8,128)(2,1)}, bf16[128,256]{1,0:T(8,128)(2,1)}, bf16[128,1280]{1,0:T(8,128)(2,1)}, bf16[128,1280]{1,0:T(8,128)(2,1)}, bf16[...) custom-call(s32[16]{0:T(128)} %place_ref.7, bf16[128,2048]{1,0:T(8,128)(2,1)} %bitcast.62, bf16[256,2048]{1,0:T(8,128)(2,1)} %wo_ref.3, ...), custom_call_target="tpu_custom_call" | custom-call | tf_op jit(solution)/shard_map/query_back/pallas_call | solution.py:646
  151.7 1.8 broadcast_in_dim.32
  153.5 3.5 %all-to-all-start.5 = ((bf16[8,144,256]{2,1,0:T(8,128)(2,1)}), bf16[8,144,256]{2,1,0:T(8,128)(2,1)S(1)}, u32[]{:S(2)}, u32[]{:S(2)}) async-start(bf16[8,144,256]{2,1,0:T(8,128)(2,1)} %broadcast_in_dim.32), calls=%async_computation.5 | async-start | bytes 1179648 | tf_op jit(solution)/shard_map/all_to_all | solution.py:856
  157.1 1.9 collective-permute-start.12
  159.0 2.7 collective-permute-start.13
  161.7 1.4 collective-permute-start.14
  163.2 7.6 %collective-permute-done.12.refs_1_.refs_5_ = bf16[128,1024]{1,0:T(8,128)(2,1)S(1)} collective-permute-done((bf16[128,1024]{1,0:T(8,128)(2,1)S(1)}, bf16[128,1024]{1,0:T(8,128)(2,1)S(1)}, u32[]{:S(2)}, u32[]{:S(2)}) %collective-permute-start.12) | collective-permute-done | bytes 262176 | tf_op jit(solution)/shard_map/ppermute | solution.py:880
  170.8 3.3 %collective-permute-done.13.refs_2_.refs_6_ = bf16[128,1024]{1,0:T(8,128)(2,1)S(1)} collective-permute-done((bf16[128,1024]{1,0:T(8,128)(2,1)S(1)}, bf16[128,1024]{1,0:T(8,128)(2,1)S(1)}, u32[]{:S(2)}, u32[]{:S(2)}) %collective-permute-start.13) | collective-permute-done | bytes 262176 | tf_op jit(solution)/shard_map/ppermute | solution.py:880
  174.9 10.5 %feed_weights.1 = (f32[2,3,128,1024]{3,2,1,0:T(8,128)}, bf16[2,3,128,1024]{3,2,1,0:T(8,128)(2,1)}) custom-call(bf16[128,1024]{1,0:T(8,128)(2,1)} %get-tuple-element.80.refs_0_.refs_4_, bf16[128,1024]{1,0:T(8,128)(2,1)} %copy-done.11, bf16[128,1024]{1,0:T(8,128)(2,1)} %copy-done.12, bf16[128,1024]{1,0:T(8,128)(2,1)} %copy-done.13, ...), custom_call_target="tpu_custom_call" | custom-call | tf_op jit(solution)/shard_map/feed_weights/pallas_call | solution.py:842
  186.0 1.0 collective-permute-start.2
  187.0 2.1 collective-permute-start.3
  189.1 1.9 collective-permute-start.4
  191.0 0.8 copy-done.15
  191.8 6.2 %key_back.1 = (bf16[128,768]{1,0:T(8,128)(2,1)}, bf16[128,2048]{1,0:T(8,128)(2,1)}) custom-call(s32[16]{0:T(128)} %place_ref.7, bf16[128,768]{1,0:T(8,128)(2,1)} %get-tuple-element.50.own_ref, bf16[8,128,768]{2,1,0:T(8,128)(2,1)} %copy-done, bf16[8,128,768]{2,1,0:T(8,128)(2,1)} %copy-done.1, bf16[8,144,256]{2,1,0:T(8,128)(2,1)} %copy-done.7, ...), custom_call_target="tpu_custom_call" | custom-call | tf_op jit(solution)/shard_map/key_back/pallas_call | solution.py:710
  198.2 5.0 %collective-permute-done.2.refs_1_.refs_5_ = bf16[128,1280]{1,0:T(8,128)(2,1)S(1)} collective-permute-done((bf16[128,1280]{1,0:T(8,128)(2,1)S(1)}, bf16[128,1280]{1,0:T(8,128)(2,1)S(1)}, u32[]{:S(2)}, u32[]{:S(2)}) %collective-permute-start.2) | collective-permute-done | bytes 327712 | tf_op jit(solution)/shard_map/ppermute | solution.py:880
  203.2 1.5 collective-permute-done.3.refs_2_.refs_6_
  204.7 4.2 %all-to-all-start.6 = ((bf16[8,16,2048]{2,1,0:T(8,128)(2,1)}), bf16[8,16,2048]{2,1,0:T(8,128)(2,1)S(1)}, u32[]{:S(2)}, u32[]{:S(2)}) async-start(bf16[8,16,2048]{2,1,0:T(8,128)(2,1)} %bitcast.64), calls=%async_computation.6 | async-start | bytes 1048576 | tf_op jit(solution)/shard_map/all_to_all | solution.py:860
  209.0 3.4 %collective-permute-done.6.refs_6_ = bf16[128,768]{1,0:T(8,128)(2,1)S(1)} collective-permute-done((bf16[128,768]{1,0:T(8,128)(2,1)}, bf16[128,768]{1,0:T(8,128)(2,1)S(1)}, u32[]{:S(2)}, u32[]{:S(2)}) %collective-permute-start.6) | collective-permute-done | bytes 196640 | tf_op jit(solution)/shard_map/ppermute | solution.py:880
  213.7 3.2 %qkv_weights.1 = (f32[2,3,128,256]{3,2,1,0:T(8,128)}, bf16[2,3,128,256]{3,2,1,0:T(8,128)(2,1)}) custom-call(bf16[128,1280]{1,0:T(8,128)(2,1)} %get-tuple-element.71.refs_0_.refs_4_, bf16[128,1280]{1,0:T(8,128)(2,1)} %copy-done.3, bf16[128,1280]{1,0:T(8,128)(2,1)} %copy-done.4, bf16[128,1280]{1,0:T(8,128)(2,1)} %copy-done.5, ...), custom_call_target="tpu_custom_call" | custom-call | tf_op jit(solution)/shard_map/qkv_weights/pallas_call | solution.py:842
  216.9 2.5 output_weights.1
  219.9 1.2 collective-permute-done.10
  221.1 1.0 fusion.3
  222.1 4.4 %collective-permute-start.11 = (bf16[1,128,256]{2,1,0:T(8,128)(2,1)S(1)}, bf16[1,128,256]{2,1,0:T(8,128)(2,1)}, u32[]{:S(2)}, u32[]{:S(2)}) collective-permute-start(bf16[1,128,256]{2,1,0:T(8,128)(2,1)S(1)} %fusion.3), channel_id=1, source_target_pairs={{0,16},{16,0},{1,17},{17,1},{2,18},{18,2},{3,19},{19,3},{4,20},{20... | collective-permute-start | bytes 196616 | tf_op jit(solution)/shard_map/ppermute | solution.py:869
  226.5 0.8 copy-done.8
  227.3 2.6 last.1
  229.9 0.9 copy.41
  232.3 4.0 %all-to-all-start.8 = ((f32[16,32,128]{2,1,0:T(8,128)}), f32[16,32,128]{2,1,0:T(8,128)S(1)}, u32[]{:S(2)}, u32[]{:S(2)}) async-start(f32[16,32,128]{2,1,0:T(8,128)} %pad_maximum_fusion), calls=%async_computation.8 | async-start | bytes 524288 | tf_op jit(solution)/shard_map/all_to_all | solution.py:860
  236.4 1.8 fusion.1
  238.1 3.4 %collective-permute-start.9 = (bf16[3,128,256]{2,1,0:T(8,128)(2,1)}, bf16[3,128,256]{2,1,0:T(8,128)(2,1)}, u32[]{:S(2)}, u32[]{:S(2)}) collective-permute-start(bf16[3,128,256]{2,1,0:T(8,128)(2,1)} %fusion.1), channel_id=1, source_target_pairs={{0,16},{16,0},{1,17},{17,1},{2,18},{18,2},{3,19},{19,3},{4,20},{20... | collective-permute-start | bytes 589832 | tf_op jit(solution)/shard_map/ppermute | solution.py:869
  241.6 1.0 fusion.2
  242.5 0.8 copy.38
  243.3 3.1 %all-to-all-done.8 = f32[16,32,128]{2,1,0:T(8,128)S(1)} async-done(((f32[16,32,128]{2,1,0:T(8,128)}), f32[16,32,128]{2,1,0:T(8,128)S(1)}, u32[]{:S(2)}, u32[]{:S(2)}) %all-to-all-start.8) | async-done | bytes 262176 | tf_op jit(solution)/shard_map/all_to_all | solution.py:860
  247.1 4.2 %all-to-all-start.9 = ((f32[8,32,128]{2,1,0:T(8,128)}), f32[8,32,128]{2,1,0:T(8,128)}, u32[]{:S(2)}, u32[]{:S(2)}) async-start(f32[8,32,128]{2,1,0:T(8,128)} %broadcast_in_dim.36), calls=%async_computation.9 | async-start | bytes 262144 | tf_op jit(solution)/shard_map/all_to_all | solution.py:856
  251.3 2.3 fusion
  253.9 1.1 bitcast_add_fusion.1
  255.0 2.7 all-to-all-done.9
  257.7 1.7 broadcast_in_dim.33
  259.4 4.2 %all-to-all-start.7 = ((bf16[8,16,2048]{2,1,0:T(8,128)(2,1)}), bf16[8,16,2048]{2,1,0:T(8,128)(2,1)}, u32[]{:S(2)}, u32[]{:S(2)}) async-start(bf16[8,16,2048]{2,1,0:T(8,128)(2,1)} %broadcast_in_dim.33), calls=%async_computation.7 | async-start | bytes 1048576 | tf_op jit(solution)/shard_map/all_to_all | solution.py:856
  263.5 0.8 slice_bitcast_fusion.3
  264.3 0.9 reduce_sum.19
  266.4 12.4 %all-to-all-done.7 = bf16[8,16,2048]{2,1,0:T(8,128)(2,1)} async-done(((bf16[8,16,2048]{2,1,0:T(8,128)(2,1)}), bf16[8,16,2048]{2,1,0:T(8,128)(2,1)}, u32[]{:S(2)}, u32[]{:S(2)}) %all-to-all-start.7) | async-done | bytes 524320 | tf_op jit(solution)/shard_map/all_to_all | solution.py:856
  278.8 7.0 %final.1 = bf16[128,4,2048]{2,1,0:T(4,128)(2,1)} custom-call(f32[2,4,6]{2,1,0:T(4,128)} %st_ref.9, bf16[128,2048]{1,0:T(8,128)(2,1)} %bitcast.7.gt_ref, bf16[128,4,2048]{2,1,0:T(4,128)(2,1)} %all-gather.7.cloned.1.call-done.base_ref, bf16[128,4,2048]{2,1,0:T(4,128)(2,1)} %s_ref.9, f32[512,128]{1,0:T(8,128)} %get-tuple-element.52.c_ref.c1_ref, ...), custom_call_target="tpu_custom_call" | custom-call | tf_op jit(solution)/shard_map/final/pallas_call | solution.py:788
  285.8 1.7 bitcast_add_fusion
  287.5 1.1 slice_bitcast_fusion
  288.6 1.0 copy.39
  289.6 1.3 copy.47
  (88 shorter events, 8.6 us)
Async XLA Ops:
  50.7 3.4 %copy-start = (bf16[8,128,768]{2,1,0:T(8,128)(2,1)}, bf16[8,128,768]{2,1,0:T(8,128)(2,1)S(1)}, u32[]{:S(2)}) copy-start(bf16[8,128,768]{2,1,0:T(8,128)(2,1)S(1)} %all_to_all.50.same_ref.qsame_ref) | copy-start | bytes 4718596
  50.7 13.9 %copy-start.6 = (f32[2,2048,6]{1,2,0:T(8,128)S(1)}, f32[2,2048,6]{1,2,0:T(8,128)}, u32[]{:S(2)}) copy-start(f32[2,2048,6]{1,2,0:T(8,128)} %copy.45) | copy-start | bytes 294916
  50.8 3.4 %collective-permute-start = (bf16[8,128,768]{2,1,0:T(8,128)(2,1)S(1)}, bf16[8,128,768]{2,1,0:T(8,128)(2,1)S(1)}, u32[]{:S(2)}, u32[]{:S(2)}) collective-permute-start(bf16[8,128,768]{2,1,0:T(8,128)(2,1)S(1)} %all_to_all.50.same_ref.qsame_ref), channel_id=1, source_target_pairs={{0,8},{8,0},{1,9},{9,1},{2,10},{10,2},{3,11},{11,3},{4,12},{12,4},... | collective-permute-start | bytes 4718600 | tf_op jit(solution)/shard_map/ppermute | solution.py:869
  54.2 1.1 copy-start.1
  60.0 15.0 %all-to-all-start.1 = ((bf16[8,16,2048]{2,1,0:T(8,128)(2,1)}), bf16[8,16,2048]{2,1,0:T(8,128)(2,1)S(1)}, u32[]{:S(2)}, u32[]{:S(2)}) async-start(bf16[8,16,2048]{2,1,0:T(8,128)(2,1)} %bitcast.65), calls=%async_computation.1 | async-start | bytes 1048576 | tf_op jit(solution)/shard_map/all_to_all | solution.py:860
  64.6 109.5 %all-gather.9.cloned.1.call-start = ((), (), s32[]{:S(2)}) async-start(), calls=%async_computation.12 | async-start | bytes 3932160 | tf_op jit(solution)/shard_map/all_gather | solution.py:908
  75.0 0.8 copy-start.9
  107.4 159.0 %all-gather.5.cloned.1.call-start = ((), (), s32[]{:S(2)}) async-start(), calls=%async_computation.10 | async-start | bytes 2359296 | tf_op jit(solution)/shard_map/all_gather | solution.py:914
  132.0 146.7 %all-gather.7.cloned.1.call-start = ((), (), s32[]{:S(2)}) async-start(), calls=%async_computation.11 | async-start | bytes 2359296 | tf_op jit(solution)/shard_map/all_gather | solution.py:913
  151.7 5.4 %copy-start.25 = (bf16[128,1024]{1,0:T(8,128)(2,1)S(1)}, bf16[128,1024]{1,0:T(8,128)(2,1)}, u32[]{:S(2)}) copy-start(bf16[128,1024]{1,0:T(8,128)(2,1)} %get-tuple-element.81) | copy-start | bytes 786436
  151.7 7.3 %copy-start.24 = (bf16[128,1024]{1,0:T(8,128)(2,1)S(1)}, bf16[128,1024]{1,0:T(8,128)(2,1)}, u32[]{:S(2)}) copy-start(bf16[128,1024]{1,0:T(8,128)(2,1)} %get-tuple-element.82) | copy-start | bytes 786436
  151.7 10.0 %copy-start.23 = (bf16[128,1024]{1,0:T(8,128)(2,1)S(1)}, bf16[128,1024]{1,0:T(8,128)(2,1)}, u32[]{:S(2)}) copy-start(bf16[128,1024]{1,0:T(8,128)(2,1)} %get-tuple-element.83) | copy-start | bytes 786436
  153.5 32.0 %all-to-all-start.5 = ((bf16[8,144,256]{2,1,0:T(8,128)(2,1)}), bf16[8,144,256]{2,1,0:T(8,128)(2,1)S(1)}, u32[]{:S(2)}, u32[]{:S(2)}) async-start(bf16[8,144,256]{2,1,0:T(8,128)(2,1)} %broadcast_in_dim.32), calls=%async_computation.5 | async-start | bytes 1179648 | tf_op jit(solution)/shard_map/all_to_all | solution.py:856
  157.1 13.7 %collective-permute-start.12 = (bf16[128,1024]{1,0:T(8,128)(2,1)S(1)}, bf16[128,1024]{1,0:T(8,128)(2,1)S(1)}, u32[]{:S(2)}, u32[]{:S(2)}) collective-permute-start(bf16[128,1024]{1,0:T(8,128)(2,1)S(1)} %copy-done.25), channel_id=1, source_target_pairs={{0,32},{32,64},{64,96},{96,0},{1,33},{33,65},{65,97},{97,1},{2,34}... | collective-permute-start | bytes 786440 | tf_op jit(solution)/shard_map/ppermute | solution.py:880
  159.0 15.1 %collective-permute-start.13 = (bf16[128,1024]{1,0:T(8,128)(2,1)S(1)}, bf16[128,1024]{1,0:T(8,128)(2,1)S(1)}, u32[]{:S(2)}, u32[]{:S(2)}) collective-permute-start(bf16[128,1024]{1,0:T(8,128)(2,1)S(1)} %copy-done.24), channel_id=1, source_target_pairs={{0,64},{32,96},{64,0},{96,32},{1,65},{33,97},{65,1},{97,33},{2,66}... | collective-permute-start | bytes 786440 | tf_op jit(solution)/shard_map/ppermute | solution.py:880
  161.7 12.4 %collective-permute-start.14 = (bf16[128,1024]{1,0:T(8,128)(2,1)S(1)}, bf16[128,1024]{1,0:T(8,128)(2,1)S(1)}, u32[]{:S(2)}, u32[]{:S(2)}) collective-permute-start(bf16[128,1024]{1,0:T(8,128)(2,1)S(1)} %copy-done.23), channel_id=1, source_target_pairs={{0,96},{32,0},{64,32},{96,64},{1,97},{33,1},{65,33},{97,65},{2,98}... | collective-permute-start | bytes 786440 | tf_op jit(solution)/shard_map/ppermute | solution.py:880
  170.8 3.3 %copy-start.11 = (bf16[128,1024]{1,0:T(8,128)(2,1)}, bf16[128,1024]{1,0:T(8,128)(2,1)S(1)}, u32[]{:S(2)}) copy-start(bf16[128,1024]{1,0:T(8,128)(2,1)S(1)} %collective-permute-done.12.refs_1_.refs_5_) | copy-start | bytes 786436
  174.1 0.7 copy-start.12
  174.1 0.8 copy-start.13
  174.9 11.1 %copy-start.22 = (bf16[128,1280]{1,0:T(8,128)(2,1)S(1)}, bf16[128,1280]{1,0:T(8,128)(2,1)}, u32[]{:S(2)}) copy-start(bf16[128,1280]{1,0:T(8,128)(2,1)} %get-tuple-element.72) | copy-start | bytes 983044
  174.9 12.1 %copy-start.21 = (bf16[128,1280]{1,0:T(8,128)(2,1)S(1)}, bf16[128,1280]{1,0:T(8,128)(2,1)}, u32[]{:S(2)}) copy-start(bf16[128,1280]{1,0:T(8,128)(2,1)} %get-tuple-element.73) | copy-start | bytes 983044
  174.9 14.2 %copy-start.20 = (bf16[128,1280]{1,0:T(8,128)(2,1)S(1)}, bf16[128,1280]{1,0:T(8,128)(2,1)}, u32[]{:S(2)}) copy-start(bf16[128,1280]{1,0:T(8,128)(2,1)} %get-tuple-element.74) | copy-start | bytes 983044
  185.4 65.9 %collective-permute-start.15 = (bf16[2,3,128,1024]{3,2,1,0:T(8,128)(2,1)}, bf16[2,3,128,1024]{3,2,1,0:T(8,128)(2,1)}, u32[]{:S(2)}, u32[]{:S(2)}) collective-permute-start(bf16[2,3,128,1024]{3,2,1,0:T(8,128)(2,1)} %get-tuple-element.86), channel_id=1, source_target_pairs={{0,8},{8,0},{1,9},{9,1},{2,10},{10,2},{3,11},{11,3},{4,12},{12,4},... | collective-permute-start | bytes 4718600 | tf_op jit(solution)/shard_map/ppermute | solution.py:869
  185.6 5.4 %copy-start.7 = (bf16[8,144,256]{2,1,0:T(8,128)(2,1)}, bf16[8,144,256]{2,1,0:T(8,128)(2,1)S(1)}, u32[]{:S(2)}) copy-start(bf16[8,144,256]{2,1,0:T(8,128)(2,1)S(1)} %all-to-all-done.5.same_ref) | copy-start | bytes 1769476
  185.6 5.4 %collective-permute-start.1 = (bf16[8,144,256]{2,1,0:T(8,128)(2,1)S(1)}, bf16[8,144,256]{2,1,0:T(8,128)(2,1)S(1)}, u32[]{:S(2)}, u32[]{:S(2)}) collective-permute-start(bf16[8,144,256]{2,1,0:T(8,128)(2,1)S(1)} %all-to-all-done.5.same_ref), channel_id=1, source_target_pairs={{0,8},{8,0},{1,9},{9,1},{2,10},{10,2},{3,11},{11,3},{4,12},{12,4},... | collective-permute-start | bytes 1769480 | tf_op jit(solution)/shard_map/ppermute | solution.py:869
  186.0 17.2 %collective-permute-start.2 = (bf16[128,1280]{1,0:T(8,128)(2,1)S(1)}, bf16[128,1280]{1,0:T(8,128)(2,1)S(1)}, u32[]{:S(2)}, u32[]{:S(2)}) collective-permute-start(bf16[128,1280]{1,0:T(8,128)(2,1)S(1)} %copy-done.22), channel_id=1, source_target_pairs={{0,32},{32,64},{64,96},{96,0},{1,33},{33,65},{65,97},{97,1},{2,34}... | collective-permute-start | bytes 983048 | tf_op jit(solution)/shard_map/ppermute | solution.py:880
  187.0 17.7 %collective-permute-start.3 = (bf16[128,1280]{1,0:T(8,128)(2,1)S(1)}, bf16[128,1280]{1,0:T(8,128)(2,1)S(1)}, u32[]{:S(2)}, u32[]{:S(2)}) collective-permute-start(bf16[128,1280]{1,0:T(8,128)(2,1)S(1)} %copy-done.21), channel_id=1, source_target_pairs={{0,64},{32,96},{64,0},{96,32},{1,65},{33,97},{65,1},{97,33},{2,66}... | collective-permute-start | bytes 983048 | tf_op jit(solution)/shard_map/ppermute | solution.py:880
  189.1 19.8 %collective-permute-start.4 = (bf16[128,1280]{1,0:T(8,128)(2,1)S(1)}, bf16[128,1280]{1,0:T(8,128)(2,1)S(1)}, u32[]{:S(2)}, u32[]{:S(2)}) collective-permute-start(bf16[128,1280]{1,0:T(8,128)(2,1)S(1)} %copy-done.20), channel_id=1, source_target_pairs={{0,96},{32,0},{64,32},{96,64},{1,97},{33,1},{65,33},{97,65},{2,98}... | collective-permute-start | bytes 983048 | tf_op jit(solution)/shard_map/ppermute | solution.py:880
  191.0 0.8 copy-start.15
  198.0 11.0 %collective-permute-start.5 = (bf16[128,768]{1,0:T(8,128)(2,1)}, bf16[128,768]{1,0:T(8,128)(2,1)S(1)}, u32[]{:S(2)}, u32[]{:S(2)}) collective-permute-start(bf16[128,768]{1,0:T(8,128)(2,1)} %get-tuple-element.75.refs_4_), channel_id=1, source_target_pairs={{0,32},{32,64},{64,96},{96,0},{1,33},{33,65},{65,97},{97,1},{2,34}... | collective-permute-start | bytes 589832 | tf_op jit(solution)/shard_map/ppermute | solution.py:880
  203.2 9.8 %copy-start.3 = (bf16[128,1280]{1,0:T(8,128)(2,1)}, bf16[128,1280]{1,0:T(8,128)(2,1)S(1)}, u32[]{:S(2)}) copy-start(bf16[128,1280]{1,0:T(8,128)(2,1)S(1)} %collective-permute-done.2.refs_1_.refs_5_) | copy-start | bytes 983044
  203.2 9.2 %collective-permute-start.6 = (bf16[128,768]{1,0:T(8,128)(2,1)}, bf16[128,768]{1,0:T(8,128)(2,1)S(1)}, u32[]{:S(2)}, u32[]{:S(2)}) collective-permute-start(bf16[128,768]{1,0:T(8,128)(2,1)} %get-tuple-element.75.refs_4_), channel_id=1, source_target_pairs={{0,64},{32,96},{64,0},{96,32},{1,65},{33,97},{65,1},{97,33},{2,66}... | collective-permute-start | bytes 589832 | tf_op jit(solution)/shard_map/ppermute | solution.py:880
  204.7 8.4 %copy-start.4 = (bf16[128,1280]{1,0:T(8,128)(2,1)}, bf16[128,1280]{1,0:T(8,128)(2,1)S(1)}, u32[]{:S(2)}) copy-start(bf16[128,1280]{1,0:T(8,128)(2,1)S(1)} %collective-permute-done.3.refs_2_.refs_6_) | copy-start | bytes 983044
  204.7 8.4 %collective-permute-start.7 = (bf16[128,768]{1,0:T(8,128)(2,1)}, bf16[128,768]{1,0:T(8,128)(2,1)S(1)}, u32[]{:S(2)}, u32[]{:S(2)}) collective-permute-start(bf16[128,768]{1,0:T(8,128)(2,1)} %get-tuple-element.75.refs_4_), channel_id=1, source_target_pairs={{0,96},{32,0},{64,32},{96,64},{1,97},{33,1},{65,33},{97,65},{2,98}... | collective-permute-start | bytes 589832 | tf_op jit(solution)/shard_map/ppermute | solution.py:880
  204.7 21.8 %all-to-all-start.6 = ((bf16[8,16,2048]{2,1,0:T(8,128)(2,1)}), bf16[8,16,2048]{2,1,0:T(8,128)(2,1)S(1)}, u32[]{:S(2)}, u32[]{:S(2)}) async-start(bf16[8,16,2048]{2,1,0:T(8,128)(2,1)} %bitcast.64), calls=%async_computation.6 | async-start | bytes 1048576 | tf_op jit(solution)/shard_map/all_to_all | solution.py:860
  208.8 4.2 %copy-start.5 = (bf16[128,1280]{1,0:T(8,128)(2,1)}, bf16[128,1280]{1,0:T(8,128)(2,1)S(1)}, u32[]{:S(2)}) copy-start(bf16[128,1280]{1,0:T(8,128)(2,1)S(1)} %collective-permute-done.4.refs_3_.refs_7_) | copy-start | bytes 983044
  209.0 4.1 %copy-start.16 = (bf16[128,768]{1,0:T(8,128)(2,1)}, bf16[128,768]{1,0:T(8,128)(2,1)S(1)}, u32[]{:S(2)}) copy-start(bf16[128,768]{1,0:T(8,128)(2,1)S(1)} %collective-permute-done.5.refs_5_) | copy-start | bytes 589828
  212.4 0.7 copy-start.17
  213.0 0.7 copy-start.18
  216.9 19.4 %collective-permute-start.8 = (bf16[2,3,128,256]{3,2,1,0:T(8,128)(2,1)}, bf16[2,3,128,256]{3,2,1,0:T(8,128)(2,1)}, u32[]{:S(2)}, u32[]{:S(2)}) collective-permute-start(bf16[2,3,128,256]{3,2,1,0:T(8,128)(2,1)} %get-tuple-element.77), channel_id=1, source_target_pairs={{0,8},{8,0},{1,9},{9,1},{2,10},{10,2},{3,11},{11,3},{4,12},{12,4},... | collective-permute-start | bytes 1179656 | tf_op jit(solution)/shard_map/ppermute | solution.py:869
  219.4 1.7 collective-permute-start.10
  221.1 8.8 %copy-start.19 = (bf16[2,1,128,256]{3,2,1,0:T(8,128)(2,1)}, bf16[2,1,128,256]{3,2,1,0:T(8,128)(2,1)S(1)}, u32[]{:S(2)}) copy-start(bf16[2,1,128,256]{3,2,1,0:T(8,128)(2,1)S(1)} %collective-permute-done.10) | copy-start | bytes 393220
  222.1 19.5 %collective-permute-start.11 = (bf16[1,128,256]{2,1,0:T(8,128)(2,1)S(1)}, bf16[1,128,256]{2,1,0:T(8,128)(2,1)}, u32[]{:S(2)}, u32[]{:S(2)}) collective-permute-start(bf16[1,128,256]{2,1,0:T(8,128)(2,1)S(1)} %fusion.3), channel_id=1, source_target_pairs={{0,16},{16,0},{1,17},{17,1},{2,18},{18,2},{3,19},{19,3},{4,20},{20... | collective-permute-start | bytes 196616 | tf_op jit(solution)/shard_map/ppermute | solution.py:869
  226.5 0.8 copy-start.8
  231.6 19.7 %copy-start.2 = (f32[2,3,128,1024]{3,2,1,0:T(8,128)S(1)}, f32[2,3,128,1024]{3,2,1,0:T(8,128)}, u32[]{:S(2)}) copy-start(f32[2,3,128,1024]{3,2,1,0:T(8,128)} %get-tuple-element.85) | copy-start | bytes 9437188
  232.3 14.1 %all-to-all-start.8 = ((f32[16,32,128]{2,1,0:T(8,128)}), f32[16,32,128]{2,1,0:T(8,128)S(1)}, u32[]{:S(2)}, u32[]{:S(2)}) async-start(f32[16,32,128]{2,1,0:T(8,128)} %pad_maximum_fusion), calls=%async_computation.8 | async-start | bytes 524288 | tf_op jit(solution)/shard_map/all_to_all | solution.py:860
  238.1 15.7 %collective-permute-start.9 = (bf16[3,128,256]{2,1,0:T(8,128)(2,1)}, bf16[3,128,256]{2,1,0:T(8,128)(2,1)}, u32[]{:S(2)}, u32[]{:S(2)}) collective-permute-start(bf16[3,128,256]{2,1,0:T(8,128)(2,1)} %fusion.1), channel_id=1, source_target_pairs={{0,16},{16,0},{1,17},{17,1},{2,18},{18,2},{3,19},{19,3},{4,20},{20... | collective-permute-start | bytes 589832 | tf_op jit(solution)/shard_map/ppermute | solution.py:869
  247.1 10.6 %all-to-all-start.9 = ((f32[8,32,128]{2,1,0:T(8,128)}), f32[8,32,128]{2,1,0:T(8,128)}, u32[]{:S(2)}, u32[]{:S(2)}) async-start(f32[8,32,128]{2,1,0:T(8,128)} %broadcast_in_dim.36), calls=%async_computation.9 | async-start | bytes 262144 | tf_op jit(solution)/shard_map/all_to_all | solution.py:856
  251.3 2.6 copy-start.14
  253.7 32.1 %collective-permute-start.16 = (bf16[3,128,1024]{2,1,0:T(8,128)(2,1)}, bf16[3,128,1024]{2,1,0:T(8,128)(2,1)}, u32[]{:S(2)}, u32[]{:S(2)}) collective-permute-start(bf16[3,128,1024]{2,1,0:T(8,128)(2,1)} %fusion), channel_id=1, source_target_pairs={{0,16},{16,0},{1,17},{17,1},{2,18},{18,2},{3,19},{19,3},{4,20},{20... | collective-permute-start | bytes 2359304 | tf_op jit(solution)/shard_map/ppermute | solution.py:869
  259.4 19.4 %all-to-all-start.7 = ((bf16[8,16,2048]{2,1,0:T(8,128)(2,1)}), bf16[8,16,2048]{2,1,0:T(8,128)(2,1)}, u32[]{:S(2)}, u32[]{:S(2)}) async-start(bf16[8,16,2048]{2,1,0:T(8,128)(2,1)} %broadcast_in_dim.33), calls=%async_computation.7 | async-start | bytes 1048576 | tf_op jit(solution)/shard_map/all_to_all | solution.py:856
  287.5 2.1 copy-start.10
Sparse Core Ops, SparseCore 0:
  107.5 35.6 all-gather.8
  144.9 40.9 all-gather.4
  187.5 44.0 all-gather.6
where the time goes:
time: 299 us; the launch traced here: 297 us
  Pallas kernels  75.5 us (25%)
  blocking collectives  75.4 us (25%)
  waiting for transfers between devices  54.9 us (18%)
  starting transfers between devices  45 us (15%)
  local copies, waits for them, and re-layouts  22.1 us (7%)
  between operations  14.1 us (5%)
  other arithmetic  10.5 us (4%)
    all_to_all x3, blocking collectives, to_all(): return lax.all_to_all(copies, axes, 0, 0, tiled=True)  56.5 us
    ppermute x9, waiting for transfers between devices, along_z(): lax.ppermute(pieces[i], 'z', [(a, (a + i) % n) for a in range(n)])  21.6 us
    all_to_all x1, blocking collectives, exchange(): return lax.all_to_all(blocks, axes, 0, 0, tiled=True)  18.9 us
    pallas_call x3, Pallas kernels, weight_part(): pl.pallas_call(functools.partial(weight_kernel, picks, tile, count, gathe...  16.2 us
    all_to_all x3, waiting for transfers between devices, to_all(): return lax.all_to_all(copies, axes, 0, 0, tiled=True)  15.2 us
    pallas_call x1, Pallas kernels, feed(): pl.pallas_call(feed_kernel, grid=(hidden // tile,), in_specs=[whole(pay.s...  13.9 us
    all_to_all x3, waiting for transfers between devices, exchange(): return lax.all_to_all(blocks, axes, 0, 0, tiled=True)  12.8 us
    all_to_all x3, starting transfers between devices, exchange(): return lax.all_to_all(blocks, axes, 0, 0, tiled=True)  12.8 us
  transfers between devices with their start and end apart: 26, of which 14 were waited for; matrix products, arithmetic and copies ran while one was open for 6% of the time, Pallas kernels for 15%

commit v1 on v0

--- a/solution.py
+++ b/solution.py
@@ -18,6 +18,7 @@
 DP = ("z", "yh", "core")
 TP = ("yl", "x")
 SMEM = pl.BlockSpec(memory_space=pltpu.SMEM)
+ANY = pl.BlockSpec(memory_space=pl.ANY)
 NT = (((1,), (1,)), ((), ()))
 TN = (((0,), (0,)), ((), ()))
 NN = (((1,), (0,)), ((), ()))
@@ -69,8 +70,12 @@
     return v * cos + pltpu.roll(v, 64, 1) * sin
 
 
-def params(limit, **kw):
-    return pltpu.CompilerParams(vmem_limit_bytes=60 * 2**20, **kw)
+def cost(us):
+    return pl.CostEstimate(flops=0, bytes_accessed=int(us * 3.69e6), transcendentals=0)
+
+
+def params():
+    return pltpu.CompilerParams(vmem_limit_bytes=60 * 2**20)
 
 
 def whole(shape):
@@ -101,9 +106,8 @@
 
 
 def unplanes(parts):
-    rows, width = parts[0].shape
-    v = dot(order(K * rows, False), jnp.concatenate(parts, 0))
-    return v.reshape(rows, K, width).astype(BF)
+    rows = parts[0].shape[0]
+    return dot(order(K * rows, False), jnp.concatenate(parts, 0)).astype(BF)
 
 
 def stream_coefs(ref, rows):
@@ -137,15 +141,26 @@
     mp_ref[0:32, :] = wide_ref[...].astype(BF)
 
 
+def columns_for(step, count, piece):
+    at = lax.rem(lax.axis_index("z") + step, count) * piece
+    return pl.ds(pl.multiple_of(at, piece), piece)
+
+
+def copies(ref):
+    for i in range(1, ref.shape[0]):
+        ref[i] = ref[0]
+
+
 def device_index():
     core = lax.axis_index("core")
     return (lax.axis_index("z") * 2 + lax.axis_index("yh")) * 2 + core, core
 
 
 def first_kernel(place_ref, st_ref, freq_ref, s_ref, m_ref, wq_ref, wk_ref, wv_ref,
-                 n_ref, c_ref, qkv_ref, trig_ref, wide_ref, mp_ref):
+                 c_ref, q_ref, kv_ref, trig_ref, *refs):
+    *x_refs, n_ref, wide_ref, mp_ref = refs
     rows, _, width = s_ref.shape
-    fill_parts(m_ref[0], wide_ref, mp_ref)
+    fill_parts(m_ref[:, 0, :], wide_ref, mp_ref)
     sums = fold_parts(dot(jnp.ones((16, width), BF), mp_ref[...], NT))[0:1]
     step = 32
     part = K * step
@@ -172,6 +187,9 @@
         return carry
 
     lax.fori_loop(0, rows // step, body, 0)
+    piece = width // len(x_refs)
+    for i, ref in enumerate(x_refs):
+        ref[...] = n_ref[:, columns_for(i, len(x_refs), piece)]
     me, _ = device_index()
     prompts = place_ref.shape[0] // 2
     start = jnp.minimum(place_ref[me], prompts) * rows
@@ -186,34 +204,40 @@
     heads = q.shape[1] // HEAD
     for h in range(heads):
         cut = slice(h * HEAD, (h + 1) * HEAD)
-        qkv_ref[:, cut] = turn(q[:, cut], cos, sin).astype(BF)
-        kcut = slice((heads + h) * HEAD, (heads + h + 1) * HEAD)
-        qkv_ref[:, kcut] = turn(k[:, cut], cos, sin).astype(BF)
-    qkv_ref[:, 2 * heads * HEAD :] = dot(normed, wv_ref[...]).astype(BF)
-
-
-def first(place, st, streams, mt, wq, wk, wv):
+        q_ref[:, cut] = turn(q[:, cut], cos, sin).astype(BF)
+        kv_ref[0, :, cut] = turn(k[:, cut], cos, sin).astype(BF)
+    kv_ref[0, :, heads * HEAD :] = dot(normed, wv_ref[...]).astype(BF)
+    copies(kv_ref)
+
+
+def first(place, st, streams, mt, wq, wk, wv, chips, count):
     rows, _, width = streams.shape
     cols = wq.shape[1]
     half = HEAD // 2
     freq = np.float32(THETA) ** (-np.arange(half, dtype=np.float32) / np.float32(half))
     freq = jnp.asarray(np.concatenate([freq, freq])[None].astype(np.float32))
     outs = (
-        ((rows, width), BF),
         ((K * rows, 128), F32),
-        ((rows, 3 * cols), BF),
+        ((rows, cols), BF),
+        ((chips, rows, 2 * cols), BF),
         ((2, rows, HEAD), F32),
+        *[((rows, width // count), BF)] * count,
     )
     return pl.pallas_call(
         first_kernel,
         grid=(1,),
         out_shape=like(*outs),
         in_specs=[SMEM, SMEM, whole(freq.shape), whole(streams.shape),
-                  pl.BlockSpec((1, *mt.shape[1:]), lambda i: (0, 0, 0)),
+                  whole(mt.shape),
                   whole(wq.shape), whole(wk.shape), whole(wv.shape)],
         out_specs=[whole(s) for s, _ in outs],
-        scratch_shapes=[pltpu.VMEM((32, width), F32), pltpu.VMEM((128, width), BF)],
-        compiler_params=params(26),
+        scratch_shapes=[
+            pltpu.VMEM((rows, width), BF),
+            pltpu.VMEM((32, width), F32),
+            pltpu.VMEM((128, width), BF),
+        ],
+        compiler_params=params(),
+        cost_estimate=cost(10),
         name="first",
     )(place, st, freq, streams, mt, wq, wk, wv)
 
@@ -232,7 +256,7 @@
         block = jnp.where((d % 2) == core, same_ref[d // 2], other_ref[d // 2])
         reach = jnp.where(is_cont | (s < own), 4096, jnp.where(s == own, 0, -4096))
         blocks.append((block, reach))
-    blocks.append((own_ref[...], jnp.where(is_cont, 0, -4096)))
+    blocks.append((own_ref[0], jnp.where(is_cont, 0, -4096)))
     return blocks
 
 
@@ -255,10 +279,10 @@
 
 
 def head_cuts(cols, h):
-    return [slice(i * cols + h * HEAD, i * cols + (h + 1) * HEAD) for i in range(3)]
-
-
-def attend_kernel(place_ref, own_ref, same_ref, other_ref, wo_ref, at_ref, log_ref, part_ref):
+    return [slice(i * cols + h * HEAD, i * cols + (h + 1) * HEAD) for i in (0, 1)]
+
+
+def attend_kernel(place_ref, q_ref, own_ref, same_ref, other_ref, wo_ref, at_ref, log_ref, part_ref, qcopy_ref):
     rows, cols = at_ref.shape
     heads = cols // HEAD
     scale = HEAD ** (-0.5)
@@ -266,10 +290,10 @@
     lag = key_after_query(rows, rows)
     logs = []
     for h in range(heads):
-        cut, kcut, vcut = head_cuts(cols, h)
-        q = own_ref[:, cut]
+        cut, vcut = head_cuts(cols, h)
+        q = q_ref[:, cut]
         scores = [
-            jnp.where(lag <= reach, dot(b[:, kcut], q, NT) * scale, -1e30) for b, reach in blocks
+            jnp.where(lag <= reach, dot(b[:, cut], q, NT) * scale, -1e30) for b, reach in blocks
         ]
         top = functools.reduce(jnp.maximum, [jnp.max(s, 0, keepdims=True) for s in scores])
         terms = [jnp.exp(s - top) for s in scores]
@@ -282,28 +306,33 @@
         at_ref[:, cut] = out.astype(BF)
         logs.append(top + jnp.log(total))
     log_ref[...] = jnp.concatenate(logs, 1)
+    qcopy_ref[...] = q_ref[...]
     part_ref[...] = dot(at_ref[...], wo_ref[...]).astype(BF)
 
 
-def attend(place, own, same, other, wo):
-    rows = own.shape[0]
-    cols = wo.shape[0]
-    args = (own, same, other, wo)
-    outs = (((rows, cols), BF), ((1, cols), F32), ((rows, wo.shape[1]), BF))
+def own_block(kv):
+    return pl.BlockSpec((1, *kv.shape[1:]), lambda i: (0, 0, 0))
+
+
+def attend(place, q, kv, same, other, wo):
+    rows, cols = q.shape
+    args = (q, kv, same, other, wo)
+    outs = (((rows, cols), BF), ((1, cols), F32), ((rows, wo.shape[1]), BF), ((rows, cols), BF))
     return pl.pallas_call(
         attend_kernel,
         grid=(1,),
         out_shape=like(*outs),
-        in_specs=[SMEM] + [whole(v.shape) for v in args],
+        in_specs=[SMEM, whole(q.shape), own_block(kv)] + [whole(v.shape) for v in args[2:]],
         out_specs=[whole(s) for s, _ in outs],
-        compiler_params=params(16),
+        compiler_params=params(),
+        cost_estimate=cost(4.5),
         name="attend",
     )(place, *args)
 
 
 def middle_kernel(t_ref, st_ref, parts_ref, s_ref, c_ref, m_ref, s1_ref, b1_ref, c2_ref, pay_ref,
                   wide_ref, mp_ref, split_ref):
-    fill_parts(m_ref[0], wide_ref, mp_ref)
+    fill_parts(m_ref[:, 1, :], wide_ref, mp_ref)
     b1 = jnp.sum(parts_ref[...].astype(F32), 0)
     b1_ref[...] = b1
     rows, width = b1.shape
@@ -331,11 +360,17 @@
         part = c[:, 0:1] * s1_ref[j]
         taken = part if taken is None else taken + part
         gives += [(4 * i + j, v.astype(F32)) for i, v in enumerate(three(c[:, 5:6]))]
-    pay_ref[:, 0:width] = norm_parts(taken)[0].astype(BF)
-    pay_ref[:, width:] = lanes(rows, gives).astype(BF)
-
-
-def token_call(kernel, name, t, tables, args, outs, scratch, limit):
+    pay_ref[0, :, 0:width] = norm_parts(taken)[0].astype(BF)
+    pay_ref[0, :, width:] = lanes(rows, gives).astype(BF)
+    copies(pay_ref)
+
+
+def token_call(kernel, name, t, tables, args, outs, scratch, waits=()):
+    count = 1 + len(tables) + len(args)
+
+    def body(*refs):
+        kernel(*refs[:count], *refs[count + len(waits) :])
+
     in_specs = [SMEM] * len(tables)
     for v, block in args:
         if block is None:
@@ -343,22 +378,23 @@
         else:
             in_specs.append(pl.BlockSpec(block, lambda i, t, n=v.ndim: (t[0],) + (0,) * (n - 1)))
     return pl.pallas_call(
-        kernel,
+        body,
         grid_spec=pltpu.PrefetchScalarGridSpec(
             num_scalar_prefetch=1,
             grid=(1,),
-            in_specs=in_specs,
+            in_specs=in_specs + [ANY] * len(waits),
             out_specs=[pl.BlockSpec(s, lambda i, t, n=len(s): (0,) * n) for s, _ in outs],
             scratch_shapes=scratch,
         ),
         out_shape=like(*outs),
-        compiler_params=params(limit),
+        compiler_params=params(),
+        cost_estimate=cost(4),
         name=name,
-    )(t, *tables, *[v for v, _ in args])
-
-
-def middle(t, st, parts, streams, c1, mt_two):
-    _, rows, width = parts.shape
+    )(t, *tables, *[v for v, _ in args], *waits)
+
+
+def middle(t, st, parts, streams, c1, mt, waits):
+    peers, rows, width = parts.shape
     return token_call(
         middle_kernel,
         "middle",
@@ -368,26 +404,21 @@
             (parts, None),
             (streams, (rows, K, width)),
             (c1, (K * rows, 128)),
-            (mt_two, None),
+            (mt, None),
         ),
         (
             ((K, rows, width), F32),
             ((rows, width), F32),
             ((K, rows, 128), F32),
-            ((rows, width + 128), BF),
+            ((peers, rows, width + 128), BF),
         ),
         [
             pltpu.VMEM((32, width), F32),
             pltpu.VMEM((128, width), BF),
             pltpu.VMEM((2 * K * rows, width), BF),
         ],
-        12,
-    )
-
-
-def columns_for(step, count, piece):
-    at = lax.rem(lax.axis_index("z") + step, count) * piece
-    return pl.ds(pl.multiple_of(at, piece), piece)
+        waits,
+    )
 
 
 def feed_kernel(pay_ref, cot_ref, wg_ref, wu_ref, wd_ref, *refs):
@@ -478,7 +509,8 @@
             pltpu.VMEM((rows, width), F32),
             pltpu.VMEM((rows, width), F32),
         ],
-        compiler_params=params(30),
+        compiler_params=params(),
+        cost_estimate=cost(14),
         name="feed",
     )(pay, cotangent, wg, wu, wd)
 
@@ -512,7 +544,7 @@
 
 
 def turn_kernel(t_ref, st_ref, parts_ref, s1_ref, c2_ref, cot_ref, s_ref, c1_ref, b1_ref, m_ref,
-                s2_ref, gb1_ref, base_ref, dm_ref, ds_ref):
+                own_ref, pair_ref, base_ref, gb1_ref, dm_ref, ds_ref):
     rows, width = b1_ref.shape
     both = jnp.sum(parts_ref[...].astype(F32), 0)
     b2, gn = both[:, 0:width], both[:, width:]
@@ -531,13 +563,15 @@
             grads[k][1 + j] = lsum(g2[j] * s1[k])
         part = c2[j][:, 0:1] * s1[j]
         taken = part if taken is None else taken + part
-    s2_ref[...] = unplanes(s2)
+    s2 = unplanes(s2)
+    own_ref[...] = s2
+    pair_ref[0] = s2
     normed, rstd = norm_parts(taken)
     gt = norm_back(gn, normed, rstd)
     for k in range(K):
         grads[k][0] = lsum(gt * s1[k])
     xhats = [(s1[k] - c2[k][:, 8:9]) * c2[k][:, 9:10] for k in range(K)]
-    gx = coef_back(grads, c2, st_ref, 1, m_ref[1], xhats, dm_ref, ds_ref, range(6))
+    gx = coef_back(grads, c2, st_ref, 1, m_ref[:, 1, :], xhats, dm_ref, ds_ref, range(6))
     g1 = []
     for k in range(K):
         v = c2[k][:, 0:1] * gt + norm_back(gx[k], xhats[k], c2[k][:, 9:10])
@@ -555,19 +589,18 @@
         grads[j][5] = lsum(g1[j] * b1)
         for k in range(K):
             grads[k][1 + j] = lsum(g1[j] * s0[k])
-    gb1_ref[...] = gb1.astype(BF)
+    gb1_ref[0] = gb1.astype(BF)
+    copies(gb1_ref)
     xhats = [(s0[k] - c1[k][:, 8:9]) * c1[k][:, 9:10] for k in range(K)]
-    gx = coef_back(grads, c1, st_ref, 0, m_ref[0], xhats, dm_ref, ds_ref, range(1, 6))
-    base = []
+    gx = coef_back(grads, c1, st_ref, 0, m_ref[:, 0, :], xhats, dm_ref, ds_ref, range(1, 6))
     for k in range(K):
         v = norm_back(gx[k], xhats[k], c1[k][:, 9:10])
         for j in range(K):
             v = v + c1[k][:, 1 + j : 2 + j] * g1[j]
-        base.append(v.astype(BF))
-    base_ref[...] = unplanes(base)
-
-
-def turn_back(t, st, parts, s1, c2, cotangent, streams, c1, b1, mt):
+        base_ref[k] = v
+
+
+def turn_back(t, st, parts, s1, c2, cotangent, streams, c1, b1, mt, waits):
     rows, width = b1.shape
     block = (rows, K, width)
     return token_call(
@@ -586,36 +619,37 @@
             (mt, None),
         ),
         (
-            (block, BF),
-            ((rows, width), BF),
-            (block, BF),
+            ((K * rows, width), BF),
+            ((2, K * rows, width), BF),
+            ((K, rows, width), F32),
+            ((parts.shape[0], rows, width), BF),
             ((2, 8, width), F32),
             ((2, 8, 128), F32),
         ),
         [],
-        20,
-    )
-
-
-def query_kernel(place_ref, gb_ref, wo_ref, own_ref, log_ref, same_ref, other_ref, trig_ref,
-                 at_ref, n_ref, do_ref, gq_ref, *ship_refs):
+        waits,
+    )
+
+
+def query_kernel(waits, place_ref, gb_ref, wo_ref, q_ref, own_ref, log_ref, same_ref, other_ref, trig_ref,
+                 *refs):
+    do_ref, gq_ref = refs[waits:]
     rows, cols = gq_ref.shape
     heads = cols // HEAD
     scale = HEAD ** (-0.5)
-    piece = gb_ref.shape[1] // len(ship_refs)
     grad = dot(gb_ref[...], wo_ref[...], NT).astype(BF)
-    do_ref[0:rows, :] = grad
+    do_ref[0, 0:rows, :] = grad
     blocks = own_blocks(place_ref, own_ref, same_ref, other_ref)
     lag = key_after_query(rows, rows)
     inners, logs = [], []
     for h in range(heads):
-        cut, kcut, vcut = head_cuts(cols, h)
-        q, do = own_ref[:, cut], grad[:, cut]
+        cut, vcut = head_cuts(cols, h)
+        q, do = q_ref[:, cut], grad[:, cut]
         log = log_ref[:, cut]
         logs.append(log)
         probs, gps, inner = [], [], None
         for b, reach in blocks:
-            s = jnp.where(lag <= reach, dot(b[:, kcut], q, NT) * scale, -1e30)
+            s = jnp.where(lag <= reach, dot(b[:, cut], q, NT) * scale, -1e30)
             p = jnp.exp(s - log)
             gp = dot(b[:, vcut], do, NT)
             part = jnp.sum(p * gp, 0, keepdims=True)
@@ -624,39 +658,40 @@
             gps.append(gp)
         gq = None
         for p, gp, (b, _) in zip(probs, gps, blocks):
-            part = dot((p * (gp - inner)).astype(BF), b[:, kcut], TN)
+            part = dot((p * (gp - inner)).astype(BF), b[:, cut], TN)
             gq = part if gq is None else gq + part
         gq_ref[:, cut] = turn(gq * scale, trig_ref[0], -trig_ref[1]).astype(BF)
         inners.append(inner)
-    do_ref[rows:, :] = jnp.concatenate(
+    do_ref[0, rows:, :] = jnp.concatenate(
         [vector_rows(i, log) for i, log in zip(inners, logs)], 1
     ).astype(BF)
-    for i, ref in enumerate(ship_refs):
-        at = columns_for(i, len(ship_refs), piece)
-        ref[:, 0:piece] = gb_ref[:, at]
-        ref[:, piece : 2 * piece] = n_ref[:, at]
-        ref[:, 2 * piece :] = at_ref[...]
-
-
-def query_back(place, gb1, wo, own, log, same, other, trig, attended, normed, count):
-    rows, cols = attended.shape
-    ship = ((rows, 2 * normed.shape[1] // count + cols), BF)
-    args = (gb1, wo, own, log, same, other, trig, attended, normed)
-    outs = (((rows + 16, cols), BF), ((rows, cols), BF), *[ship] * count)
+    copies(do_ref)
+
+
+def query_back(place, gb1, wo, q, kv, log, same, other, trig, waits):
+    rows, cols = q.shape
+    args = (gb1, wo, q, kv, log, same, other, trig)
+    outs = (((same.shape[0], rows + 16, cols), BF), ((rows, cols), BF))
+    specs = [whole(v.shape) for v in args]
+    specs[3] = own_block(kv)
     return pl.pallas_call(
-        query_kernel,
+        functools.partial(query_kernel, len(waits)),
         grid=(1,),
         out_shape=like(*outs),
-        in_specs=[SMEM] + [whole(v.shape) for v in args],
+        in_specs=[SMEM] + specs + [ANY] * len(waits),
         out_specs=[whole(s) for s, _ in outs],
-        compiler_params=params(24),
+        compiler_params=params(),
+        cost_estimate=cost(5.5),
         name="query_back",
-    )(place, *args)
-
-
-def key_kernel(place_ref, own_ref, qsame_ref, qother_ref, same_ref, other_ref, gq_ref, trig_ref,
-               wq_ref, wk_ref, wv_ref, small_ref, part_ref):
+    )(place, *args, *waits)
+
+
+def key_kernel(waits, place_ref, own_ref, qall_ref, same_ref, other_ref, gq_ref, trig_ref,
+               wq_ref, wk_ref, wv_ref, gb_ref, at_ref, *refs):
+    part_ref, *ship_refs = refs[waits:]
     rows, cols = gq_ref.shape
+    small_ref = ship_refs[0].at[:, cols : 4 * cols]
+    ship_refs[0][:, 0:cols] = at_ref[...]
     heads = cols // HEAD
     scale = HEAD ** (-0.5)
     me, core = device_index()
@@ -674,12 +709,12 @@
     lag = key_after_query(rows, rows)
     seen = jnp.concatenate([lag] * count, 1) <= reach
     for h in range(heads):
-        cut, kcut, vcut = head_cuts(cols, h)
-        k, v = own_ref[:, kcut], own_ref[:, vcut]
+        cut, vcut = head_cuts(cols, h)
+        k, v = own_ref[0, :, cut], own_ref[0, :, vcut]
         qs, dos, logs, inners = [], [], [], []
         for g, rel in groups:
             src = same_ref if rel == 0 else other_ref
-            qs.append((qsame_ref if rel == 0 else qother_ref)[g, :, cut])
+            qs.append(qall_ref[2 * g + (core + rel) % 2, :, cut])
             dos.append(src[g, 0:rows, cut])
             inners.append(vector_of(src[g, rows:, cut], 0))
             logs.append(vector_of(src[g, rows:, cut], 1))
@@ -691,34 +726,41 @@
         ds = (p * (gp - inners)).astype(BF)
         gv = dot(p.astype(BF), dos)
         gk = dot(ds, qs) * scale
-        small_ref[:, kcut] = turn(gk, trig_ref[0], -trig_ref[1]).astype(BF)
-        small_ref[:, vcut] = gv.astype(BF)
+        small_ref[:, vcut] = turn(gk, trig_ref[0], -trig_ref[1]).astype(BF)
+        small_ref[:, 2 * cols + h * HEAD : 2 * cols + (h + 1) * HEAD] = gv.astype(BF)
     small_ref[:, 0:cols] = gq_ref[...]
     part = dot(gq_ref[...], wq_ref[...], NT)
     part += dot(small_ref[:, cols : 2 * cols], wk_ref[...], NT)
     part += dot(small_ref[:, 2 * cols :], wv_ref[...], NT)
     part_ref[...] = part.astype(BF)
-
-
-def key_back(place, own, qsame, qother, same, other, gq, trig, wq, wk, wv):
+    count = len(ship_refs)
+    piece = gb_ref.shape[1] // count
+    for i, ref in enumerate(ship_refs):
+        if i:
+            ref[:, 0 : 4 * cols] = ship_refs[0][:, 0 : 4 * cols]
+        ref[:, 4 * cols :] = gb_ref[:, columns_for(i, count, piece)]
+
+
+def key_back(place, kv, qall, same, other, gq, trig, wq, wk, wv, gb1, attended, count, waits):
     rows, cols = gq.shape
-    args = (own, qsame, qother, same, other, gq, trig, wq, wk, wv)
-    queries = pl.BlockSpec((*qsame.shape[:2], cols), lambda i: (0, 0, 0))
+    width = wq.shape[0]
+    args = (kv, qall, same, other, gq, trig, wq, wk, wv, gb1, attended)
     specs = [whole(v.shape) for v in args]
-    specs[1] = specs[2] = queries
-    outs = (((rows, 3 * cols), BF), ((rows, wq.shape[0]), BF))
+    specs[0] = own_block(kv)
+    outs = (((rows, width), BF), *[((rows, 4 * cols + width // count), BF)] * count)
     return pl.pallas_call(
-        key_kernel,
+        functools.partial(key_kernel, len(waits)),
         grid=(1,),
         out_shape=like(*outs),
-        in_specs=[SMEM] + specs,
+        in_specs=[SMEM] + specs + [ANY] * len(waits),
         out_specs=[whole(s) for s, _ in outs],
-        compiler_params=params(32),
+        compiler_params=params(),
+        cost_estimate=cost(6.5),
         name="key_back",
-    )(place, *args)
-
-
-def last_kernel(t_ref, st_ref, parts_ref, s_ref, c_ref, dmin_ref, dsin_ref, gt_ref, dm_ref, ds_ref):
+    )(place, *args, *waits)
+
+
+def last_kernel(t_ref, st_ref, parts_ref, base_ref, s_ref, c_ref, m_ref, dm_ref, ds_ref, out_ref, keep_ref, give_ref):
     gn = jnp.sum(parts_ref[...].astype(F32), 0)
     rows, width = gn.shape
     s0 = planes(s_ref[...])
@@ -729,22 +771,46 @@
         taken = part if taken is None else taken + part
     normed, rstd = norm_parts(taken)
     gt = norm_back(gn, normed, rstd)
-    gt_ref[...] = gt.astype(BF)
-    dm_ref[...] = dmin_ref[...]
-    ds_ref[...] = dsin_ref[...]
-    total = None
+    total, statics, out = None, [], []
     lane = iota((1, 128), 1)
+    m = m_ref[0:1, 0, :]
+    ctr = m - lmean(m)
     for k in range(K):
         g = lsum(gt * s0[k])
         th = c1[k][:, 0:1] - st_ref[0, k, 0]
-        part = g * (1.0 - th * th) * ((s0[k] - c1[k][:, 8:9]) * c1[k][:, 9:10])
+        dz = g * (1.0 - th * th)
+        xhat = (s0[k] - c1[k][:, 8:9]) * c1[k][:, 9:10]
+        part = dz * xhat
         total = part if total is None else total + part
-        ds_ref[0, k : k + 1, :] += jnp.where(lane == 0, jnp.sum(g, 0, keepdims=True), 0.0)
-    dm_ref[0, 0:1, :] = jnp.sum(total, 0, keepdims=True)
-
-
-def last(t, st, parts, streams, c1, dm, ds):
-    _, rows, width = parts.shape
+        v = base_ref[k] + c1[k][:, 0:1] * gt
+        out.append((v + c1[k][:, 9:10] * dz * (ctr - xhat * lmean(m * xhat))).astype(BF))
+        statics.append(jnp.where(lane == 0, jnp.sum(g, 0, keepdims=True), 0.0))
+    out_ref[0] = unplanes(out)
+    copies(out_ref)
+    top = dm_ref[0] + jnp.concatenate(
+        [jnp.sum(total, 0, keepdims=True), jnp.zeros((7, width), F32)], 0
+    )
+    statics = ds_ref[0] + jnp.concatenate(statics + [jnp.zeros((8 - K, 128), F32)], 0)
+    bottom = dm_ref[1]
+    core = lax.axis_index("core")
+    blocks = keep_ref.shape[0] - 1
+    nz = blocks // 2
+    for yh in range(2):
+        for z in range(nz):
+            pair = []
+            for i in range(2):
+                at = ((z * 2 + yh) * 2 + i) * 128
+                pair.append(jnp.concatenate([top[:, at : at + 128], bottom[:, at : at + 128]], 0))
+            keep_ref[yh * nz + z] = jnp.where(core == 0, pair[0], pair[1])
+            give_ref[yh * nz + z] = jnp.where(core == 0, pair[1], pair[0])
+    both = jnp.concatenate([statics, ds_ref[1]], 0)
+    keep_ref[blocks] = both
+    give_ref[blocks] = both
+
+
+def last(t, st, parts, base, streams, c1, mt, dm, ds, waits):
+    peers, rows, width = parts.shape
+    blocks = ((width // 256 + 1, 16, 128), F32)
     return token_call(
         last_kernel,
         "last",
@@ -752,108 +818,88 @@
         (st,),
         (
             (parts, None),
+            (base, None),
             (streams, (rows, K, width)),
             (c1, (K * rows, 128)),
+            (mt, None),
             (dm, None),
             (ds, None),
         ),
-        (((rows, width), BF), (dm.shape, F32), (ds.shape, F32)),
+        (((peers, K * rows, width), BF), blocks, blocks),
         [],
-        12,
-    )
-
-
-def final_kernel(st_ref, gt_ref, base_ref, s_ref, c_ref, m_ref, out_ref):
-    rows, _, width = s_ref.shape
-    part = K * rows
-    spread = (iota((part, rows), 0) // K == iota((part, rows), 1)).astype(BF)
-    gt = dot(spread, gt_ref[...])
-    s0 = s_ref[...].reshape(part, width).astype(F32)
-    c = c_ref[...]
-    g = lsum(gt * s0)
-    th = (c - static_rows(st_ref, 0, part))[:, 0:1]
-    rstd = c[:, 9:10]
-    xhat = (s0 - c[:, 8:9]) * rstd
-    m = m_ref[0, 0:1, :]
-    back = (m - lmean(m)) - xhat * lmean(m * xhat)
-    v = base_ref[...].reshape(part, width).astype(F32) + c[:, 0:1] * gt
-    v = v + (rstd * g * (1.0 - th * th)) * back
-    out_ref[...] = v.astype(BF).reshape(rows, K, width)
-
-
-def final(st, gt, base, streams, c1, mt):
-    rows, _, width = streams.shape
-    step = 32
-    block = pl.BlockSpec((step, K, width), lambda i: (i, 0, 0))
-    return pl.pallas_call(
-        final_kernel,
-        grid=(rows // step,),
-        out_shape=jax.ShapeDtypeStruct(streams.shape, BF),
-        in_specs=[
-            SMEM,
-            pl.BlockSpec((step, width), lambda i: (i, 0)),
-            block,
-            block,
-            pl.BlockSpec((K * step, 128), lambda i: (i, 0)),
-            whole(mt.shape),
-        ],
-        out_specs=block,
-        compiler_params=params(20),
-        name="final",
-    )(st, gt, base, streams, c1, mt)
-
-
-def weight_kernel(picks, tile, count, gathered, *refs):
-    *lefts, keep_ref, give_ref, hold_ref = refs
+        waits,
+    )
+
+
+def weight_kernel(picks, tile, count, gathered, waits, whole_sums, *refs):
+    if whole_sums:
+        *lefts, sum_ref = refs
+        span = sum_ref.shape[3]
+    else:
+        *lefts, keep_ref, give_ref, hold_ref = refs
+        span = keep_ref.shape[3]
+    lefts = lefts[: len(lefts) - waits]
     rights = lefts[-1:] if gathered else lefts[-count:]
     lefts = lefts[: -len(rights)]
+    units = len(picks)
     core, z = lax.axis_index("core"), lax.axis_index("z")
     mats = [
-        jnp.concatenate([r[...] for r in lefts[i : i + count]], 0)
+        jnp.concatenate([r[...] for r in lefts[i : i + count]], 0).T
         for i in range(0, len(lefts), count)
     ]
-    part = mats[0].shape[1] // 2
-    for u, pick in enumerate(picks):
-        cut = slice(u * tile, (u + 1) * tile)
-        if gathered:
-            right = [rights[0][lax.rem(z - i + count, count), :, cut] for i in range(count)]
-        else:
-            right = [r[:, cut] for r in rights]
-        hold_ref[...] = dot(mats[pick], jnp.concatenate(right, 0), TN)
-        keep_ref[0, u] = hold_ref[pl.ds(pl.multiple_of(core * part, part), part), :]
-        give_ref[0, u] = hold_ref[pl.ds(pl.multiple_of((1 - core) * part, part), part), :].astype(BF)
-
-
-def weight_part(left, offsets, right, right_at, tiles, picks, tile, name):
-    count = len(left)
-    rows = left[0].shape[0]
+    part = 128
+    kept = pl.ds(pl.multiple_of(core * part, part), part)
+    given = pl.ds(pl.multiple_of((1 - core) * part, part), part)
+    for f in range(span // tile):
+        for u, pick in enumerate(picks):
+            cut = slice((f * units + u) * tile, (f * units + u + 1) * tile)
+            if gathered:
+                right = [rights[0][lax.rem(z - i + count, count), :, cut] for i in range(count)]
+            else:
+                right = [r[:, cut] for r in rights]
+            v = dot(mats[pick], jnp.concatenate(right, 0))
+            to = slice(f * tile, (f + 1) * tile)
+            if whole_sums:
+                sum_ref[0, u, :, to] = v[0:part].astype(BF)
+                sum_ref[1, u, :, to] = v[part:].astype(BF)
+            else:
+                hold_ref[f % 2] = v
+                keep_ref[0, u, :, to] = hold_ref[f % 2, kept, :]
+                give_ref[0, u, :, to] = hold_ref[f % 2, given, :].astype(BF)
+
+
+def weight_part(lefts, right, tiles, picks, tile, name, us, waits=(), whole_sums=False):
+    count = len(lefts[0][0])
+    rows = lefts[0][0][0].shape[0]
     units = len(picks)
     gathered = not isinstance(right, (list, tuple))
     shape = (2, units, 128, tiles * tile)
-    out = pl.BlockSpec((1, units, 128, tile), lambda f, y: (y, 0, 0, f))
+    out = pl.BlockSpec((1, *shape[1:]), lambda y: (y, 0, 0, 0))
+    outs, shapes = [out, out], like((shape, F32), (shape, BF))
+    scratch = [pltpu.VMEM((2, 256, tile), F32)]
+    if whole_sums:
+        outs = pl.BlockSpec(shape, lambda y: (y, 0, 0, 0))
+        shapes = jax.ShapeDtypeStruct((4, *shape[1:]), BF)
+        scratch = []
     specs = [
-        pl.BlockSpec((rows, 256), lambda f, y, o=o: (0, o + y)) for o in offsets for _ in left
+        pl.BlockSpec((rows, 256), lambda y, o=o: (0, o + y)) for pieces, o in lefts for _ in pieces
     ]
     if gathered:
-        specs.append(pl.BlockSpec((count, rows, units * tile), lambda f, y: (0, 0, right_at + f)))
+        specs.append(pl.BlockSpec((count, rows, units * tile * tiles), lambda y: (0, 0, 0)))
         right = [right]
     else:
-        specs += [pl.BlockSpec((rows, units * tile), lambda f, y: (0, right_at + f))] * count
+        specs += [pl.BlockSpec((rows, units * tile * tiles), lambda y: (0, 0))] * count
     return pl.pallas_call(
-        functools.partial(weight_kernel, picks, tile, count, gathered),
-        grid=(tiles, 2),
-        in_specs=specs,
-        out_specs=[out, out],
-        out_shape=like((shape, F32), (shape, BF)),
-        scratch_shapes=[pltpu.VMEM((256, tile), F32)],
-        compiler_params=params(16),
+        functools.partial(weight_kernel, picks, tile, count, gathered, len(waits), whole_sums),
+        grid=(2,),
+        in_specs=specs + [ANY] * len(waits),
+        out_specs=outs,
+        out_shape=shapes,
+        scratch_shapes=scratch,
+        compiler_params=params(),
+        cost_estimate=cost(us),
         name=name,
-    )(*[v for _ in offsets for v in left], *right)
-
-
-def to_all(shard, axes):
-    copies = jnp.broadcast_to(shard, (lax.axis_size(axes), *shard.shape))
-    return lax.all_to_all(copies, axes, 0, 0, tiled=True)
+    )(*[v for pieces, _ in lefts for v in pieces], *right, *waits)
 
 
 def exchange(blocks, axes):
@@ -867,11 +913,6 @@
 
 def swap(v, axis):
     return lax.ppermute(v, axis, [(0, 1), (1, 0)])
-
-
-def over_chips(shard):
-    same = to_all(shard, ("z", "yh"))
-    return same, swap(same, "core")
 
 
 def along_z(pieces):
@@ -881,14 +922,66 @@
     ]
 
 
+def pin(v, *waits):
+    def body(*refs):
+        pass
+
+    return pl.pallas_call(
+        body,
+        out_shape=jax.ShapeDtypeStruct(v.shape, v.dtype),
+        in_specs=[ANY] * (1 + len(waits)),
+        out_specs=ANY,
+        input_output_aliases={0: 0},
+        name="pin",
+    )(v, *waits)
+
+
+def over_tensor(pair):
+    half, _, rows, width = pair.shape
+    return pl.BlockSpec(
+        (half, 1, rows, width), lambda i, t: (0, jnp.abs(i - t[0] // half), 0, 0)
+    )
+
+
+def gathered_rows(blocks, t, wait):
+    rows, width = blocks.shape[-2:]
+    half = int(np.prod(blocks.shape[:-2])) // 2
+    out = (half * rows // K, K, width)
+    spec = pl.BlockSpec((half, rows, width), lambda i, t: (i, 0, 0))
+    if blocks.ndim == 4:
+        spec = over_tensor(blocks)
+
+    def body(t_ref, in_ref, _, out_ref):
+        out_ref[...] = in_ref[...].reshape(out)
+
+    return pl.pallas_call(
+        body,
+        grid_spec=pltpu.PrefetchScalarGridSpec(
+            num_scalar_prefetch=1,
+            grid=(2,),
+            in_specs=[spec, ANY],
+            out_specs=pl.BlockSpec(out, lambda i, t: (i, 0, 0)),
+        ),
+        out_shape=jax.ShapeDtypeStruct((2 * out[0], *out[1:]), blocks.dtype),
+        compiler_params=params(),
+        cost_estimate=cost(2.6),
+        name="rows",
+    )(t, blocks, wait)
+
+
+def to_each(v, axis):
+    n = lax.axis_size(axis)
+    return v + sum(lax.ppermute(v, axis, [(a, (a + i) % n) for a in range(n)]) for i in range(1, n))
+
+
 def pick(v, at):
     return lax.dynamic_index_in_dim(v, at, 0, keepdims=False)
 
 
-def over_yh(kept, got):
+def over_core(kept, got):
     yh = lax.axis_index("yh")
     give = pick(kept, 1 - yh) + pick(got, 1 - yh).astype(F32)
-    return pick(kept, yh) + pick(got, yh).astype(F32) + swap(give.astype(BF), "yh").astype(F32)
+    return pick(kept, yh) + pick(got, yh).astype(F32), give.astype(BF)
 
 
 def per_device(streams, placement, w_query, w_key, w_value, w_output, w_gate, w_up, w_down,
@@ -897,57 +990,80 @@
     groups = placement.shape[0]
     t = lax.axis_index(TP).astype(jnp.int32)[None]
     nz = lax.axis_size("z")
-    mt = jnp.transpose(mix_dynamic, (0, 2, 1))
-
-    normed_one, c1, own, trig = first(placement, mix_static, streams, mt, w_query, w_key, w_value)
-    same, other = over_chips(own)
-    attended, log, part_one = attend(placement, own, same, other, w_output)
-    s1, b1, c2, pay = middle(t, mix_static, scatter_parts(part_one, TP), streams, c1, mt[1:2])
-    pay = to_all(pay, TP).reshape(rows, width + 128)
+    mt = jnp.transpose(mix_dynamic, (2, 0, 1))
+
+    c1, q, kv, trig, *x_one = first(
+        placement, mix_static, streams, mt, w_query, w_key, w_value, groups // 2, nz
+    )
+    same = exchange(kv, ("z", "yh"))
+    other = swap(same, "core")
+    attended, log, part_one, q = attend(placement, q, kv, same, other, w_output)
+    qall = lax.all_gather(q, DP, axis=0)
+    x_one = along_z(x_one)
+    s1, b1, c2, pay = middle(
+        t, mix_static, scatter_parts(part_one, TP), streams, c1, mt, x_one[1:]
+    )
+    pay = exchange(pay, TP).reshape(rows, width + 128)
     *xy, acts, part_two = feed(pay, cotangent, w_gate, w_up, w_down, nz)
     acts = lax.all_gather(acts, "z", axis=0)
-    xy = along_z(xy)
-    parts = scatter_parts(part_two, TP)
-    s2, gb1, base, dm, ds = turn_back(t, mix_static, parts, s1, c2, cotangent, streams, c1, b1, mt)
-    gb1 = to_all(gb1, TP).reshape(rows, width)
-    base = lax.all_gather(base, TP, axis=0, tiled=True)
-    streams_out = lax.all_gather(s2, TP, axis=0, tiled=True)
-    do, gq, *ship = query_back(
-        placement, gb1, w_output, own, log, same, other, trig, attended, normed_one, nz
+    turned, pair, base, gb1, dm, ds = turn_back(
+        t, mix_static, scatter_parts(part_two, TP), s1, c2, cotangent, streams, c1, b1, mt, (qall,)
+    )
+    turned = swap(turned, "yl")
+    pair = lax.dynamic_update_slice(pair, turned[None], (1, 0, 0))
+    gb1 = exchange(gb1, TP).reshape(rows, width)
+    do, gq = query_back(placement, gb1, w_output, q, kv, log, same, other, trig, (pair,))
+    pair = lax.all_gather(pin(pair, gb1), "x", axis=0)
+    tiles = w_gate.shape[1] // FEED_TILE
+    xy = along_z([pin(v, gq) for v in xy])
+    do_same = exchange(do, ("z", "yh"))
+    do_same = pin(do_same, *xy[1:])
+    do_other = swap(do_same, "core")
+    part_three, *ship = key_back(
+        placement, kv, qall, do_same, do_other, gq, trig, w_query, w_key, w_value, gb1, attended, nz,
+        (),
+    )
+    ff_keep, ff_give = weight_part(
+        ((xy, 0), (xy, 2)), acts, tiles, (0, 0, 1), FEED_TILE, "feed_weights", 8, (part_three,)
     )
     ship = along_z(ship)
-    do_same, do_other = over_chips(do)
-    small, part_three = key_back(
-        placement, own, same, other, do_same, do_other, gq, trig, w_query, w_key, w_value
-    )
-    small = along_z([small] * nz)
-    parts = scatter_parts(part_three, TP)
-    gt, dm, ds = last(t, mix_static, parts, streams, c1, dm, ds)
-    gt = to_all(gt, TP).reshape(rows, width)
-    grad_streams = final(mix_static, gt, base, streams, c1, mt)
-
-    tiles = w_gate.shape[1] // FEED_TILE
-    keep, give = weight_part(xy, (0, 2), acts, 0, tiles, (0, 0, 1), FEED_TILE, "feed_weights")
-    ff = over_yh(keep, swap(give, "core"))
-    keep, give = weight_part(ship, (0,), ship, 4, 1, (0,), 256, "output_weights")
-    out = over_yh(keep, swap(give, "core"))
-    keep, give = weight_part(ship, (2,), small, 0, 1, (0, 0, 0), 256, "qkv_weights")
-    qkv = over_yh(keep, swap(give, "core"))
-
-    spread = jnp.transpose(dm.reshape(16, groups, width // groups), (1, 0, 2))
-    statics = jnp.broadcast_to(ds.reshape(1, 16, 128), (groups, 16, 128))
-    packed = jnp.concatenate([spread, statics], 1)
-    packed = jnp.sum(exchange(packed, DP), 0)
-    packed = jnp.sum(to_all(packed, TP), 0)
-    grad_dynamic = jnp.transpose(packed[:16].reshape(2, 8, -1)[:, :6], (0, 2, 1))
-    grad_static = packed[16:].reshape(2, 8, 128)[:, :4, :6]
+    gt, mix_keep, mix_give = last(
+        t, mix_static, scatter_parts(part_three, TP), base, streams, c1, mt, dm, ds, (ff_keep,)
+    )
+    streams_out = gathered_rows(pair, t, mix_keep)
+    gt = exchange(gt, TP)
+    grad_streams = gathered_rows(gt, t, streams_out)
+    ff_keep, ff_give = over_core(ff_keep, swap(ff_give, "core"))
+    ff = ff_keep + swap(ff_give, "yh").astype(F32)
+    v = mix_keep + swap(mix_give, "core")
+    yh, z = lax.axis_index("yh"), lax.axis_index("z")
+
+    def half(at):
+        return jnp.concatenate([lax.dynamic_slice_in_dim(v, at * nz, nz, 0), v[2 * nz :]], 0)
+
+    v = half(yh) + swap(half(1 - yh), "yh")
+    mix_mid = v
+
+    def mine(at):
+        return jnp.stack([pick(v, lax.rem(at, nz)), v[nz]])
+
+    v = sum(along_z([mine(z + i) for i in range(nz)]))
+    v = to_each(to_each(v, "yl"), "x")
+    grad_dynamic = jnp.transpose(v[0].reshape(2, 8, -1)[:, :6], (0, 2, 1))
+    grad_static = v[1].reshape(2, 8, 128)[:, :4, :6]
+    keep, give = weight_part(
+        ((ship, 4), (x_one, 0)), ship, 1, (0, 1, 1, 1), 256, "tail_weights", 4, (mix_mid,)
+    )
+    keep, give = over_core(keep, swap(give, "core"))
+    tail = keep + swap(give, "yh").astype(F32)
+
     return (
         streams_out,
         grad_streams,
-        qkv[0],
-        qkv[1],
-        qkv[2],
-        jnp.transpose(out[0]),
+        tail[1],
+        tail[2],
+        tail[3],
+        jnp.transpose(tail[0]),
         ff[0],
         ff[1],
         jnp.transpose(ff[2]),

time: 299 us -> 280 us (0.936)
  blocking collectives: 75.4 us -> 57.7 us
  waiting for transfers between devices: 54.9 us -> 67.4 us
  local copies, waits for them, and re-layouts: 22.1 us -> 12.1 us
  Pallas kernels: 75.5 us -> 70.6 us
  starting transfers between devices: 45 us -> 49.1 us
    all_to_all x3 -> x0, blocking collectives: 56.5 us -> none  [to_all(): return lax.all_to_all(copies, axes, 0, 0, tiled=True)]
    all_to_all x1 -> x3, blocking collectives: 18.9 us -> 57.7 us  [exchange(): return lax.all_to_all(blocks, axes, 0, 0, tiled=True)]
    ppermute x8 -> x9, waiting for transfers between devices: 4.62 us -> 23.4 us  [swap(): return lax.ppermute(v, axis, [(0, 1), (1, 0)])]
    all_to_all x3 -> x0, waiting for transfers between devices: 15.2 us -> none  [to_all(): return lax.all_to_all(copies, axes, 0, 0, tiled=True)]
    ppermute x9 -> x12, waiting for transfers between devices: 21.6 us -> 34.2 us  [along_z(): lax.ppermute(pieces[i], 'z', [(a, (a + i) % n) for a in range(n)])]
    all_to_all x3 -> x0, starting transfers between devices: 11.9 us -> none  [to_all(): return lax.all_to_all(copies, axes, 0, 0, tiled=True)]
    all_to_all x3 -> x5, starting transfers between devices: 12.8 us -> 22.7 us  [exchange(): return lax.all_to_all(blocks, axes, 0, 0, tiled=True)]
    broadcast_in_dim x7 -> x0, local copies, waits for them, and re-layouts: 7.74 us -> none  [the longest x6 7.03 us: to_all(): copies = jnp.broadcast_to(shard, (lax.axis_size(axes), *shard.shape))]
  transfers between devices with their start and end apart: 26 -> 33, of which waited for: 14 -> 19; matrix products, arithmetic and copies ran while one was open for 6% -> 3% of each run, Pallas kernels for 15% -> 20%
where the time goes in v1:
time: 280 us; the launch traced here: 279 us
  Pallas kernels  70.6 us (25%)
  waiting for transfers between devices  67.4 us (24%)
  blocking collectives  57.7 us (21%)
  starting transfers between devices  49.1 us (18%)
  between operations  14 us (5%)
  local copies, waits for them, and re-layouts  12.1 us (4%)
  other arithmetic  7.85 us (3%)
    all_to_all x3, blocking collectives, exchange(): return lax.all_to_all(blocks, axes, 0, 0, tiled=True)  57.7 us
    ppermute x12, waiting for transfers between devices, along_z(): lax.ppermute(pieces[i], 'z', [(a, (a + i) % n) for a in range(n)])  34.2 us
    ppermute x9, waiting for transfers between devices, swap(): return lax.ppermute(v, axis, [(0, 1), (1, 0)])  23.4 us
    all_to_all x5, starting transfers between devices, exchange(): return lax.all_to_all(blocks, axes, 0, 0, tiled=True)  22.7 us
    ppermute x12, starting transfers between devices, along_z(): lax.ppermute(pieces[i], 'z', [(a, (a + i) % n) for a in range(n)])  15.3 us
    pallas_call x1, Pallas kernels, feed(): pl.pallas_call(feed_kernel, grid=(hidden // tile,), in_specs=[whole(pay.s...  14 us
    pallas_call x3, Pallas kernels, token_call(): pl.pallas_call(body, grid_spec=pltpu.PrefetchScalarGridSpec(num_scalar_pr...  13 us
    pallas_call x1, Pallas kernels, first(): pl.pallas_call(first_kernel, grid=(1,), out_shape=like(*outs), in_specs=[...  11 us
  transfers between devices with their start and end apart: 33, of which 19 were waited for; matrix products, arithmetic and copies ran while one was open for 3% of the time, Pallas kernels for 20%

profile of v1, /device:TPU:0, one launch (start us, length us, event | category | flops | bytes accessed | tf_op | source)
XLA Modules:
  0.0 278.8 jit_solution(16659759545284370358)
XLA Ops:
  7.2 11.0 %first.1 = (f32[512,128]{1,0:T(8,128)}, bf16[128,256]{1,0:T(8,128)(2,1)}, bf16[8,128,512]{2,1,0:T(8,128)(2,1)}, f32[2,128,128]{2,1,0:T(8,128)}, bf16[128,512]{1,...) custom-call(s32[16]{0:T(128)} %place_ref.7, f32[2,4,6]{2,1,0:T(4,128)} %refs_1_.5, ...), custom_call_target="tpu_custom_call" | custom-call | bytes 36900000 | tf_op jit(solution)/shard_map/first/pallas_call | solution.py:226
  18.2 25.2 %all_to_all.40.same_ref = bf16[8,128,512]{2,1,0:T(8,128)(2,1)S(1)} all-to-all(bf16[8,128,512]{2,1,0:T(8,128)(2,1)} %get-tuple-element.54.own_ref), channel_id=1, replica_groups=mesh['z'=4,'yh'=2,'core'=2,'yl'=2,'x'=4] {'z','yh'}, dimensions={0} | all-to-all | bytes 2097152 | tf_op jit(solution)/shard_map/all_to_all | solution.py:906
  43.5 2.7 collective-permute-done.other_ref
  46.2 1.0 copy-done.4
  47.2 4.5 %attend.1 = (bf16[128,256]{1,0:T(8,128)(2,1)}, f32[1,256]{1,0:T(1,128)}, bf16[128,2048]{1,0:T(8,128)(2,1)}, bf16[128,256]{1,0:T(8,128)(2,1)}) custom-call(s32[16]{0:T(128)} %place_ref.7, bf16[128,256]{1,0:T(8,128)(2,1)} %get-tuple-element.53.q_ref, bf16[8,128,512]{2,1,0:T(8,128)(2,1)} %get-tuple-element.54.own_ref, bf16[8,128,512]{2,1,0:T(8,128)(2,1)} %copy-done.1, ...), custom_call_target="tpu_custom_call" | custom-call | bytes 16605000 | tf_op jit(solution)/shard_map/attend/pallas_call | solution.py:321
  51.6 4.5 %all-to-all-start.1 = ((bf16[8,16,2048]{2,1,0:T(8,128)(2,1)}), bf16[8,16,2048]{2,1,0:T(8,128)(2,1)S(1)}, u32[]{:S(2)}, u32[]{:S(2)}) async-start(bf16[8,16,2048]{2,1,0:T(8,128)(2,1)} %bitcast.60), calls=%async_computation.1 | async-start | bytes 1048576 | tf_op jit(solution)/shard_map/all_to_all | solution.py:906
  56.4 2.1 collective-permute-start.2
  58.5 1.5 collective-permute-start.3
  60.0 5.9 %collective-permute-done.1.refs_6_.refs_5_ = bf16[128,512]{1,0:T(8,128)(2,1)S(1)} collective-permute-done((bf16[128,512]{1,0:T(8,128)(2,1)S(1)}, bf16[128,512]{1,0:T(8,128)(2,1)S(1)}, u32[]{:S(2)}, u32[]{:S(2)}) %collective-permute-start.1) | collective-permute-done | bytes 131104 | tf_op jit(solution)/shard_map/ppermute | solution.py:921
  67.5 3.3 %middle.1 = (f32[4,16,2048]{2,1,0:T(8,128)}, f32[16,2048]{1,0:T(8,128)}, f32[4,16,128]{2,1,0:T(8,128)}, bf16[8,16,2176]{2,1,0:T(8,128)(2,1)}) custom-call(s32[1]{0:T(128)} %bitcast.refs_0_.t_ref, f32[2,4,6]{2,1,0:T(4,128)} %refs_1_.5, bf16[8,16,2048]{2,1,0:T(8,128)(2,1)} %copy-done.9, bf16[128,4,2048]{2,1,0:T(4,128)(2,1)} %refs_4_.1, ...), custom_call_target="tpu_custom_call" | custom-call | bytes 14760000 | tf_op jit(solution)/shard_map/middle/pallas_call | solution.py:380
  70.8 15.3 %all_to_all.41 = bf16[8,16,2176]{2,1,0:T(8,128)(2,1)} all-to-all(bf16[8,16,2176]{2,1,0:T(8,128)(2,1)} %get-tuple-element.60), channel_id=1, replica_groups=mesh['z'=4,'yh'=2,'core'=2,'yl'=2,'x'=4] {'yl','x'}, dimensions={0} | all-to-all | bytes 1114112 | tf_op jit(solution)/shard_map/all_to_all | solution.py:906
  86.1 14.0 %feed.1 = (bf16[128,1024]{1,0:T(8,128)(2,1)}, bf16[128,1024]{1,0:T(8,128)(2,1)}, bf16[128,1024]{1,0:T(8,128)(2,1)}, bf16[128,1024]{1,0:T(8,128)(2,1)}, bf16[128,...) custom-call(bf16[128,2176]{1,0:T(8,128)(2,1)} %bitcast.52, bf16[128,4,2048]{2,1,0:T(4,128)(2,1)} %refs_5_.1, ...), custom_call_target="tpu_custom_call" | custom-call | bytes 51660000 | tf_op jit(solution)/shard_map/feed/pallas_call | solution.py:487
  100.1 17.1 %all_to_all.42.refs_2_ = bf16[8,16,4096]{2,1,0:T(8,128)(2,1)} all-to-all(bf16[8,16,4096]{2,1,0:T(8,128)(2,1)} %bitcast.59), channel_id=1, replica_groups=mesh['z'=4,'yh'=2,'core'=2,'yl'=2,'x'=4] {'yl','x'}, dimensions={0} | all-to-all | bytes 2097152 | tf_op jit(solution)/shard_map/all_to_all | solution.py:906
  117.2 5.8 %turn.1 = (bf16[64,2048]{1,0:T(8,128)(2,1)}, bf16[2,64,2048]{2,1,0:T(8,128)(2,1)}, f32[4,16,2048]{2,1,0:T(8,128)}, bf16[8,16,2048]{2,1,0:T(8,128)(2,1)}, f32[2,8,2048]{2,1,0:T(8,128)}, /*index=5*/f32[2,8,128]{2,1,0:T(8,128)}) custom-call(s32[1]{0:T(128)} %bitcast.refs_0_.t_ref, f32[2,4,6]{2,1,0:T(4,128)} %refs_1_.5, ...), custom_call_target="tpu_custom_call" | custom-call | bytes 14760000 | tf_op jit(solution)/shard_map/turn/pallas_call | solution.py:380
  123.5 3.5 %all-to-all-start.4 = ((bf16[8,16,2048]{2,1,0:T(8,128)(2,1)}), bf16[8,16,2048]{2,1,0:T(8,128)(2,1)S(1)}, u32[]{:S(2)}, u32[]{:S(2)}) async-start(bf16[8,16,2048]{2,1,0:T(8,128)(2,1)} %get-tuple-element.68), calls=%async_computation.4 | async-start | bytes 1048576 | tf_op jit(solution)/shard_map/all_to_all | solution.py:906
  127.0 4.7 %collective-permute-done.4 = bf16[64,2048]{1,0:T(8,128)(2,1)S(1)} collective-permute-done((bf16[64,2048]{1,0:T(8,128)(2,1)}, bf16[64,2048]{1,0:T(8,128)(2,1)S(1)}, u32[]{:S(2)}, u32[]{:S(2)}) %collective-permute-start.4) | collective-permute-done | bytes 262176 | tf_op jit(solution)/shard_map/ppermute | solution.py:915
  132.4 3.2 %all-to-all-done.4 = bf16[8,16,2048]{2,1,0:T(8,128)(2,1)S(1)} async-done(((bf16[8,16,2048]{2,1,0:T(8,128)(2,1)}), bf16[8,16,2048]{2,1,0:T(8,128)(2,1)S(1)}, u32[]{:S(2)}, u32[]{:S(2)}) %all-to-all-start.4) | async-done | bytes 524320 | tf_op jit(solution)/shard_map/all_to_all | solution.py:906
  135.6 0.8 copy-done.2
  136.4 5.2 %query_back.1 = (bf16[8,144,256]{2,1,0:T(8,128)(2,1)}, bf16[128,256]{1,0:T(8,128)(2,1)}) custom-call(s32[16]{0:T(128)} %place_ref.7, bf16[128,2048]{1,0:T(8,128)(2,1)} %bitcast.46, bf16[256,2048]{1,0:T(8,128)(2,1)} %wo_ref.3, bf16[128,256]{1,0:T(8,128)(2,1)} %get-tuple-element.65.q_ref, bf16[8,128,512]{2,1,0:T(8,128)(2,1)} %get-tuple-element.54.own_ref, ...), custom_call_target="tpu_custom_call" | custom-call | bytes 20295000 | tf_op jit(solution)/shard_map/query_back/pallas_call | solution.py:677
  142.3 6.8 %all-to-all-start.5 = ((bf16[8,144,256]{2,1,0:T(8,128)(2,1)}), bf16[8,144,256]{2,1,0:T(8,128)(2,1)S(1)}, u32[]{:S(2)}, u32[]{:S(2)}) async-start(bf16[8,144,256]{2,1,0:T(8,128)(2,1)} %get-tuple-element.71), calls=%async_computation.5 | async-start | bytes 1179648 | tf_op jit(solution)/shard_map/all_to_all | solution.py:906
  149.1 3.2 %collective-permute-start.7 = (bf16[128,1024]{1,0:T(8,128)(2,1)}, bf16[128,1024]{1,0:T(8,128)(2,1)S(1)}, u32[]{:S(2)}, u32[]{:S(2)}) collective-permute-start(bf16[128,1024]{1,0:T(8,128)(2,1)} %pin.9), channel_id=1, source_target_pairs={{0,96},{32,0},{64,32},{96,64},{1,97},{33,1},{65,33},{97,65},{2,98}... | collective-permute-start | bytes 786440 | tf_op jit(solution)/shard_map/ppermute | solution.py:921
  152.4 0.9 collective-permute-start.6
  153.2 0.9 collective-permute-start.5
  154.1 9.7 %collective-permute-done.7.refs_3_.refs_7_ = bf16[128,1024]{1,0:T(8,128)(2,1)S(1)} collective-permute-done((bf16[128,1024]{1,0:T(8,128)(2,1)}, bf16[128,1024]{1,0:T(8,128)(2,1)S(1)}, u32[]{:S(2)}, u32[]{:S(2)}) %collective-permute-start.7) | collective-permute-done | bytes 262176 | tf_op jit(solution)/shard_map/ppermute | solution.py:921
  163.8 1.9 collective-permute-done.6.refs_2_.refs_6_
  165.7 3.4 %collective-permute-done.5.refs_1_.refs_5_ = bf16[128,1024]{1,0:T(8,128)(2,1)S(1)} collective-permute-done((bf16[128,1024]{1,0:T(8,128)(2,1)}, bf16[128,1024]{1,0:T(8,128)(2,1)S(1)}, u32[]{:S(2)}, u32[]{:S(2)}) %collective-permute-start.5) | collective-permute-done | bytes 262176 | tf_op jit(solution)/shard_map/ppermute | solution.py:921
  169.8 0.8 copy-done.3
  170.6 2.2 collective-permute-done.8.other_ref
  172.9 0.8 copy-done.14
  173.7 6.9 %key_back.1 = (bf16[128,2048]{1,0:T(8,128)(2,1)}, bf16[128,1536]{1,0:T(8,128)(2,1)}, bf16[128,1536]{1,0:T(8,128)(2,1)}, bf16[128,1536]{1,0:T(8,128)(2,1)}, bf16[128,1536]{1,0:T(8,128)(2,1)}) custom-call(s32[16]{0:T(128)} %place_ref.7, bf16[8,128,512]{2,1,0:T(8,128)(2,1)} %get-tuple-element.54.own_ref, bf16[16,128,256]{2,1,0:T(8,128)(2,1)} %bitcast.50, ...), custom_call_target="tpu_custom_call" | custom-call | bytes 23985000 | tf_op jit(solution)/shard_map/key_back/pallas_call | solution.py:751
  180.6 3.5 %all-to-all-start.6 = ((bf16[8,16,2048]{2,1,0:T(8,128)(2,1)}), bf16[8,16,2048]{2,1,0:T(8,128)(2,1)S(1)}, u32[]{:S(2)}, u32[]{:S(2)}) async-start(bf16[8,16,2048]{2,1,0:T(8,128)(2,1)} %bitcast.54), calls=%async_computation.6 | async-start | bytes 1048576 | tf_op jit(solution)/shard_map/all_to_all | solution.py:906
  184.1 6.9 %feed_weights.1 = (f32[2,3,128,1024]{3,2,1,0:T(8,128)}, bf16[2,3,128,1024]{3,2,1,0:T(8,128)(2,1)}) custom-call(bf16[128,1024]{1,0:T(8,128)(2,1)} %pin.11.refs_0_.refs_4_, bf16[128,1024]{1,0:T(8,128)(2,1)} %copy-done.7, bf16[128,1024]{1,0:T(8,128)(2,1)} %copy-done.6, bf16[128,1024]{1,0:T(8,128)(2,1)} %copy-done.5, bf16[128,1024]{1,0:T(8,128)(2,1)} %pin.11.refs_0_.refs_4_, ...), custom_call_target="tpu_custom_call" | custom-call | bytes 29520000 | tf_op jit(solution)/shard_map/feed_weights/pallas_call | solution.py:892
  191.2 3.5 %all-to-all-done.6.refs_2_ = bf16[8,16,2048]{2,1,0:T(8,128)(2,1)S(1)} async-done(((bf16[8,16,2048]{2,1,0:T(8,128)(2,1)}), bf16[8,16,2048]{2,1,0:T(8,128)(2,1)S(1)}, u32[]{:S(2)}, u32[]{:S(2)}) %all-to-all-start.6) | async-done | bytes 524320 | tf_op jit(solution)/shard_map/all_to_all | solution.py:906
  194.6 0.8 copy-done.8
  195.4 3.9 %last.1 = (bf16[8,64,2048]{2,1,0:T(8,128)(2,1)}, f32[9,16,128]{2,1,0:T(8,128)}, f32[9,16,128]{2,1,0:T(8,128)}) custom-call(s32[1]{0:T(128)} %bitcast.refs_0_.t_ref, f32[2,4,6]{2,1,0:T(4,128)} %refs_1_.5, bf16[8,16,2048]{2,1,0:T(8,128)(2,1)} %copy-done.8, f32[4,16,2048]{2,1,0:T(8,128)} %get-tuple-element.78.refs_3_, bf16[128,4,2048]{2,1,0:T(4,128)(2,1)} %refs_4_.1, ...), custom_call_target="tpu_custom_call" | custom-call | bytes 14760000 | tf_op jit(solution)/shard_map/last/pallas_call | solution.py:380
  199.4 0.9 collective-permute-start.10
  200.3 1.4 collective-permute-start.11
  202.3 0.9 add.102
  203.3 2.5 collective-permute-start.13
  205.7 4.4 %all-to-all-start.7 = ((bf16[8,64,2048]{2,1,0:T(8,128)(2,1)}), bf16[8,64,2048]{2,1,0:T(8,128)(2,1)}, u32[]{:S(2)}, u32[]{:S(2)}) async-start(bf16[8,64,2048]{2,1,0:T(8,128)(2,1)} %get-tuple-element.85), calls=%async_computation.7 | async-start | bytes 4194304 | tf_op jit(solution)/shard_map/all_to_all | solution.py:906
  210.7 2.2 collective-permute-done.10.refs_2_.refs_10_
  212.9 5.9 %collective-permute-done.11.refs_3_.refs_11_ = bf16[128,1536]{1,0:T(8,128)(2,1)S(1)} collective-permute-done((bf16[128,1536]{1,0:T(8,128)(2,1)S(1)}, bf16[128,1536]{1,0:T(8,128)(2,1)S(1)}, u32[]{:S(2)}, u32[]{:S(2)}) %collective-permute-start.11) | collective-permute-done | bytes 393248 | tf_op jit(solution)/shard_map/ppermute | solution.py:921
  218.8 2.1 collective-permute-done.9.refs_1_.refs_9_
  221.6 3.8 %tail_weights.1 = (f32[2,4,128,256]{3,2,1,0:T(8,128)}, bf16[2,4,128,256]{3,2,1,0:T(8,128)(2,1)}) custom-call(bf16[128,1536]{1,0:T(8,128)(2,1)} %get-tuple-element.86.refs_0_.refs_8_, bf16[128,1536]{1,0:T(8,128)(2,1)} %copy-done.12, bf16[128,1536]{1,0:T(8,128)(2,1)} %copy-done.10, bf16[128,1536]{1,0:T(8,128)(2,1)} %copy-done.11, ...), custom_call_target="tpu_custom_call" | custom-call | bytes 14760000 | tf_op jit(solution)/shard_map/tail_weights/pallas_call | solution.py:892
  225.7 2.2 collective-permute-start.19
  227.8 1.3 collective-permute-start.20
  229.2 1.6 collective-permute-done.18
  232.2 2.8 %rows.2._ = bf16[128,4,2048]{2,1,0:T(4,128)(2,1)} custom-call(s32[1]{0:T(128)} %bitcast.refs_0_.t_ref, bf16[4,2,64,2048]{3,2,1,0:T(8,128)(2,1)} %bitcast.53, f32[9,16,128]{2,1,0:T(8,128)} %get-tuple-element.84._), custom_call_target="tpu_custom_call" | custom-call | bytes 9594000 | tf_op jit(solution)/shard_map/rows/pallas_call | solution.py:957
  235.0 2.3 collective-permute-done.21
  237.3 0.9 collective-permute-start.22
  238.2 1.4 collective-permute-start.23
  239.6 1.4 collective-permute-start.24
  241.0 1.3 fusion.1
  242.2 1.0 collective-permute-start.15
  243.2 2.3 fusion
  245.5 2.7 collective-permute-start.17
  249.4 3.7 %collective-permute-done.15 = bf16[4,128,256]{2,1,0:T(8,128)(2,1)S(1)} collective-permute-done((bf16[4,128,256]{2,1,0:T(8,128)(2,1)S(1)}, bf16[4,128,256]{2,1,0:T(8,128)(2,1)S(1)}, u32[]{:S(2)}, u32[]{:S(2)}) %collective-permute-start.15) | collective-permute-done | bytes 262176 | tf_op jit(solution)/shard_map/ppermute | solution.py:915
  253.1 1.0 bitcast_add_fusion.1
  254.8 0.8 copy.34
  255.6 2.6 rows.3
  258.2 10.2 %collective-permute-done.17 = bf16[3,128,1024]{2,1,0:T(8,128)(2,1)} collective-permute-done((bf16[3,128,1024]{2,1,0:T(8,128)(2,1)}, bf16[3,128,1024]{2,1,0:T(8,128)(2,1)}, u32[]{:S(2)}, u32[]{:S(2)}) %collective-permute-start.17) | collective-permute-done | bytes 786464 | tf_op jit(solution)/shard_map/ppermute | solution.py:915
  268.4 1.7 bitcast_add_fusion
  270.1 1.1 slice_bitcast_fusion
  271.2 1.0 copy.35
  (98 shorter events, 10.4 us)
Async XLA Ops:
  7.2 110.0 %all-gather.7.cloned.1.call-start = ((), (), s32[]{:S(2)}) async-start(), calls=%async_computation.8 | async-start | bytes 1114112 | tf_op jit(solution)/shard_map/all_gather | solution.py:1001
  43.5 2.7 copy-start.1
  43.5 2.7 collective-permute-start
  46.2 1.0 copy-start.4
  47.2 9.1 %copy-start.24 = (bf16[128,512]{1,0:T(8,128)(2,1)S(1)}, bf16[128,512]{1,0:T(8,128)(2,1)}, u32[]{:S(2)}) copy-start(bf16[128,512]{1,0:T(8,128)(2,1)} %get-tuple-element.57) | copy-start | bytes 393220
  47.2 9.3 %copy-start.23 = (bf16[128,512]{1,0:T(8,128)(2,1)S(1)}, bf16[128,512]{1,0:T(8,128)(2,1)}, u32[]{:S(2)}) copy-start(bf16[128,512]{1,0:T(8,128)(2,1)} %get-tuple-element.58) | copy-start | bytes 393220
  47.2 11.4 %copy-start.22 = (bf16[128,512]{1,0:T(8,128)(2,1)S(1)}, bf16[128,512]{1,0:T(8,128)(2,1)}, u32[]{:S(2)}) copy-start(bf16[128,512]{1,0:T(8,128)(2,1)} %get-tuple-element.59) | copy-start | bytes 393220
  51.6 15.0 %all-to-all-start.1 = ((bf16[8,16,2048]{2,1,0:T(8,128)(2,1)}), bf16[8,16,2048]{2,1,0:T(8,128)(2,1)S(1)}, u32[]{:S(2)}, u32[]{:S(2)}) async-start(bf16[8,16,2048]{2,1,0:T(8,128)(2,1)} %bitcast.60), calls=%async_computation.1 | async-start | bytes 1048576 | tf_op jit(solution)/shard_map/all_to_all | solution.py:906
  56.2 127.9 %all-gather.11.cloned.1.call-start = ((), (), s32[]{:S(2)}) async-start(), calls=%async_computation.10 | async-start | bytes 3932160 | tf_op jit(solution)/shard_map/all_gather | solution.py:1008
  56.2 9.7 %collective-permute-start.1 = (bf16[128,512]{1,0:T(8,128)(2,1)S(1)}, bf16[128,512]{1,0:T(8,128)(2,1)S(1)}, u32[]{:S(2)}, u32[]{:S(2)}) collective-permute-start(bf16[128,512]{1,0:T(8,128)(2,1)S(1)} %copy-done.24), channel_id=1, source_target_pairs={{0,32},{32,64},{64,96},{96,0},{1,33},{33,65},{65,97},{97,1},{2,34}... | collective-permute-start | bytes 393224 | tf_op jit(solution)/shard_map/ppermute | solution.py:921
  56.4 9.5 %collective-permute-start.2 = (bf16[128,512]{1,0:T(8,128)(2,1)S(1)}, bf16[128,512]{1,0:T(8,128)(2,1)S(1)}, u32[]{:S(2)}, u32[]{:S(2)}) collective-permute-start(bf16[128,512]{1,0:T(8,128)(2,1)S(1)} %copy-done.23), channel_id=1, source_target_pairs={{0,64},{32,96},{64,0},{96,32},{1,65},{33,97},{65,1},{97,33},{2,66}... | collective-permute-start | bytes 393224 | tf_op jit(solution)/shard_map/ppermute | solution.py:921
  58.5 8.1 %collective-permute-start.3 = (bf16[128,512]{1,0:T(8,128)(2,1)S(1)}, bf16[128,512]{1,0:T(8,128)(2,1)S(1)}, u32[]{:S(2)}, u32[]{:S(2)}) collective-permute-start(bf16[128,512]{1,0:T(8,128)(2,1)S(1)} %copy-done.22), channel_id=1, source_target_pairs={{0,96},{32,0},{64,32},{96,64},{1,97},{33,1},{65,33},{97,65},{2,98}... | collective-permute-start | bytes 393224 | tf_op jit(solution)/shard_map/ppermute | solution.py:921
  65.9 0.7 copy-start.15
  65.9 0.7 copy-start.16
  66.6 0.7 copy-start.17
  66.6 0.8 copy-start.9
  123.0 8.7 %collective-permute-start.4 = (bf16[64,2048]{1,0:T(8,128)(2,1)}, bf16[64,2048]{1,0:T(8,128)(2,1)S(1)}, u32[]{:S(2)}, u32[]{:S(2)}) collective-permute-start(bf16[64,2048]{1,0:T(8,128)(2,1)} %get-tuple-element.67), channel_id=1, source_target_pairs={{0,4},{4,0},{1,5},{5,1},{2,6},{6,2},{3,7},{7,3},{8,12},{12,8},{9,1... | collective-permute-start | bytes 786440 | tf_op jit(solution)/shard_map/ppermute | solution.py:915
  123.5 12.1 %all-to-all-start.4 = ((bf16[8,16,2048]{2,1,0:T(8,128)(2,1)}), bf16[8,16,2048]{2,1,0:T(8,128)(2,1)S(1)}, u32[]{:S(2)}, u32[]{:S(2)}) async-start(bf16[8,16,2048]{2,1,0:T(8,128)(2,1)} %get-tuple-element.68), calls=%async_computation.4 | async-start | bytes 1048576 | tf_op jit(solution)/shard_map/all_to_all | solution.py:906
  135.6 0.8 copy-start.2
  141.6 90.6 %all-gather.9.cloned.1.call-start = ((), (), s32[]{:S(2)}) async-start(), calls=%async_computation.9 | async-start | bytes 2621440 | tf_op jit(solution)/shard_map/all_gather | solution.py:1016
  142.3 26.8 %all-to-all-start.5 = ((bf16[8,144,256]{2,1,0:T(8,128)(2,1)}), bf16[8,144,256]{2,1,0:T(8,128)(2,1)S(1)}, u32[]{:S(2)}, u32[]{:S(2)}) async-start(bf16[8,144,256]{2,1,0:T(8,128)(2,1)} %get-tuple-element.71), calls=%async_computation.5 | async-start | bytes 1179648 | tf_op jit(solution)/shard_map/all_to_all | solution.py:906
  149.1 14.7 %collective-permute-start.7 = (bf16[128,1024]{1,0:T(8,128)(2,1)}, bf16[128,1024]{1,0:T(8,128)(2,1)S(1)}, u32[]{:S(2)}, u32[]{:S(2)}) collective-permute-start(bf16[128,1024]{1,0:T(8,128)(2,1)} %pin.9), channel_id=1, source_target_pairs={{0,96},{32,0},{64,32},{96,64},{1,97},{33,1},{65,33},{97,65},{2,98}... | collective-permute-start | bytes 786440 | tf_op jit(solution)/shard_map/ppermute | solution.py:921
  152.4 13.4 %collective-permute-start.6 = (bf16[128,1024]{1,0:T(8,128)(2,1)}, bf16[128,1024]{1,0:T(8,128)(2,1)S(1)}, u32[]{:S(2)}, u32[]{:S(2)}) collective-permute-start(bf16[128,1024]{1,0:T(8,128)(2,1)} %pin.8), channel_id=1, source_target_pairs={{0,64},{32,96},{64,0},{96,32},{1,65},{33,97},{65,1},{97,33},{2,66}... | collective-permute-start | bytes 786440 | tf_op jit(solution)/shard_map/ppermute | solution.py:921
  153.2 15.9 %collective-permute-start.5 = (bf16[128,1024]{1,0:T(8,128)(2,1)}, bf16[128,1024]{1,0:T(8,128)(2,1)S(1)}, u32[]{:S(2)}, u32[]{:S(2)}) collective-permute-start(bf16[128,1024]{1,0:T(8,128)(2,1)} %pin.7), channel_id=1, source_target_pairs={{0,32},{32,64},{64,96},{96,0},{1,33},{33,65},{65,97},{97,1},{2,34}... | collective-permute-start | bytes 786440 | tf_op jit(solution)/shard_map/ppermute | solution.py:921
  163.8 5.3 %copy-start.5 = (bf16[128,1024]{1,0:T(8,128)(2,1)}, bf16[128,1024]{1,0:T(8,128)(2,1)S(1)}, u32[]{:S(2)}) copy-start(bf16[128,1024]{1,0:T(8,128)(2,1)S(1)} %collective-permute-done.7.refs_3_.refs_7_) | copy-start | bytes 786436
  165.7 3.4 %copy-start.6 = (bf16[128,1024]{1,0:T(8,128)(2,1)}, bf16[128,1024]{1,0:T(8,128)(2,1)S(1)}, u32[]{:S(2)}) copy-start(bf16[128,1024]{1,0:T(8,128)(2,1)S(1)} %collective-permute-done.6.refs_2_.refs_6_) | copy-start | bytes 786436
  169.1 0.7 copy-start.7
  169.8 0.8 copy-start.3
  170.6 2.2 collective-permute-start.8
  172.9 0.8 copy-start.14
  180.6 14.1 %all-to-all-start.6 = ((bf16[8,16,2048]{2,1,0:T(8,128)(2,1)}), bf16[8,16,2048]{2,1,0:T(8,128)(2,1)S(1)}, u32[]{:S(2)}, u32[]{:S(2)}) async-start(bf16[8,16,2048]{2,1,0:T(8,128)(2,1)} %bitcast.54), calls=%async_computation.6 | async-start | bytes 1048576 | tf_op jit(solution)/shard_map/all_to_all | solution.py:906
  191.0 52.1 %collective-permute-start.16 = (bf16[2,3,128,1024]{3,2,1,0:T(8,128)(2,1)}, bf16[2,3,128,1024]{3,2,1,0:T(8,128)(2,1)}, u32[]{:S(2)}, u32[]{:S(2)}) collective-permute-start(bf16[2,3,128,1024]{3,2,1,0:T(8,128)(2,1)} %get-tuple-element.94), channel_id=1, source_target_pairs={{0,8},{8,0},{1,9},{9,1},{2,10},{10,2},{3,11},{11,3},{4,12},{12,4},... | collective-permute-start | bytes 4718600 | tf_op jit(solution)/shard_map/ppermute | solution.py:915
  194.6 0.8 copy-start.8
  195.4 3.9 %copy-start.21 = (bf16[128,1536]{1,0:T(8,128)(2,1)S(1)}, bf16[128,1536]{1,0:T(8,128)(2,1)}, u32[]{:S(2)}) copy-start(bf16[128,1536]{1,0:T(8,128)(2,1)} %get-tuple-element.88) | copy-start | bytes 1179652
  195.4 4.9 %copy-start.20 = (bf16[128,1536]{1,0:T(8,128)(2,1)S(1)}, bf16[128,1536]{1,0:T(8,128)(2,1)}, u32[]{:S(2)}) copy-start(bf16[128,1536]{1,0:T(8,128)(2,1)} %get-tuple-element.89) | copy-start | bytes 1179652
  195.4 6.3 %copy-start.19 = (bf16[128,1536]{1,0:T(8,128)(2,1)S(1)}, bf16[128,1536]{1,0:T(8,128)(2,1)}, u32[]{:S(2)}) copy-start(bf16[128,1536]{1,0:T(8,128)(2,1)} %get-tuple-element.87) | copy-start | bytes 1179652
  199.3 3.0 %collective-permute-start.12 = (f32[9,16,128]{2,1,0:T(8,128)}, f32[9,16,128]{2,1,0:T(8,128)S(1)}, u32[]{:S(2)}, u32[]{:S(2)}) collective-permute-start(f32[9,16,128]{2,1,0:T(8,128)} %get-tuple-element.91), channel_id=1, source_target_pairs={{0,8},{8,0},{1,9},{9,1},{2,10},{10,2},{3,11},{11,3},{4,12},{12,4},... | collective-permute-start | bytes 221192 | tf_op jit(solution)/shard_map/ppermute | solution.py:915
  199.4 13.5 %collective-permute-start.10 = (bf16[128,1536]{1,0:T(8,128)(2,1)S(1)}, bf16[128,1536]{1,0:T(8,128)(2,1)S(1)}, u32[]{:S(2)}, u32[]{:S(2)}) collective-permute-start(bf16[128,1536]{1,0:T(8,128)(2,1)S(1)} %copy-done.21), channel_id=1, source_target_pairs={{0,64},{32,96},{64,0},{96,32},{1,65},{33,97},{65,1},{97,33},{2,66}... | collective-permute-start | bytes 1179656 | tf_op jit(solution)/shard_map/ppermute | solution.py:921
  200.3 18.5 %collective-permute-start.11 = (bf16[128,1536]{1,0:T(8,128)(2,1)S(1)}, bf16[128,1536]{1,0:T(8,128)(2,1)S(1)}, u32[]{:S(2)}, u32[]{:S(2)}) collective-permute-start(bf16[128,1536]{1,0:T(8,128)(2,1)S(1)} %copy-done.20), channel_id=1, source_target_pairs={{0,96},{32,0},{64,32},{96,64},{1,97},{33,1},{65,33},{97,65},{2,98}... | collective-permute-start | bytes 1179656 | tf_op jit(solution)/shard_map/ppermute | solution.py:921
  201.7 19.1 %collective-permute-start.9 = (bf16[128,1536]{1,0:T(8,128)(2,1)S(1)}, bf16[128,1536]{1,0:T(8,128)(2,1)S(1)}, u32[]{:S(2)}, u32[]{:S(2)}) collective-permute-start(bf16[128,1536]{1,0:T(8,128)(2,1)S(1)} %copy-done.19), channel_id=1, source_target_pairs={{0,32},{32,64},{64,96},{96,0},{1,33},{33,65},{65,97},{97,1},{2,34}... | collective-permute-start | bytes 1179656 | tf_op jit(solution)/shard_map/ppermute | solution.py:921
  203.3 6.8 %collective-permute-start.13 = (f32[5,16,128]{2,1,0:T(8,128)S(1)}, f32[5,16,128]{2,1,0:T(8,128)S(1)}, u32[]{:S(2)}, u32[]{:S(2)}) collective-permute-start(f32[5,16,128]{2,1,0:T(8,128)S(1)} %pad_maximum_fusion), channel_id=1, source_target_pairs={{0,16},{16,0},{1,17},{17,1},{2,18},{18,2},{3,19},{19,3},{4,20},{20... | collective-permute-start | bytes 122888 | tf_op jit(solution)/shard_map/ppermute | solution.py:915
  205.7 49.9 %all-to-all-start.7 = ((bf16[8,64,2048]{2,1,0:T(8,128)(2,1)}), bf16[8,64,2048]{2,1,0:T(8,128)(2,1)}, u32[]{:S(2)}, u32[]{:S(2)}) async-start(bf16[8,64,2048]{2,1,0:T(8,128)(2,1)} %get-tuple-element.85), calls=%async_computation.7 | async-start | bytes 4194304 | tf_op jit(solution)/shard_map/all_to_all | solution.py:906
  210.7 14.8 %copy-start.18 = (f32[5,16,128]{2,1,0:T(8,128)S(1)}, f32[5,16,128]{2,1,0:T(8,128)}, u32[]{:S(2)}) copy-start(f32[5,16,128]{2,1,0:T(8,128)} %fusion.2.refs_12_) | copy-start | bytes 122884
  212.9 7.9 %copy-start.10 = (bf16[128,1536]{1,0:T(8,128)(2,1)}, bf16[128,1536]{1,0:T(8,128)(2,1)S(1)}, u32[]{:S(2)}) copy-start(bf16[128,1536]{1,0:T(8,128)(2,1)S(1)} %collective-permute-done.10.refs_2_.refs_10_) | copy-start | bytes 1179652
  218.8 2.1 copy-start.11
  220.8 0.7 copy-start.12
  225.4 15.6 %collective-permute-start.14 = (bf16[2,4,128,256]{3,2,1,0:T(8,128)(2,1)}, bf16[2,4,128,256]{3,2,1,0:T(8,128)(2,1)}, u32[]{:S(2)}, u32[]{:S(2)}) collective-permute-start(bf16[2,4,128,256]{3,2,1,0:T(8,128)(2,1)} %get-tuple-element.93), channel_id=1, source_target_pairs={{0,8},{8,0},{1,9},{9,1},{2,10},{10,2},{3,11},{11,3},{4,12},{12,4},... | collective-permute-start | bytes 1572872 | tf_op jit(solution)/shard_map/ppermute | solution.py:915
  225.6 5.2 %collective-permute-start.18 = (f32[2,16,128]{2,1,0:T(8,128)S(1)}, f32[2,16,128]{2,1,0:T(8,128)S(1)}, u32[]{:S(2)}, u32[]{:S(2)}) collective-permute-start(f32[2,16,128]{2,1,0:T(8,128)S(1)} %get-tuple-element.133), channel_id=1, source_target_pairs={{0,32},{32,64},{64,96},{96,0},{1,33},{33,65},{65,97},{97,1},{2,34}... | collective-permute-start | bytes 49160 | tf_op jit(solution)/shard_map/ppermute | solution.py:921
  225.7 5.6 %collective-permute-start.19 = (f32[2,16,128]{2,1,0:T(8,128)S(1)}, f32[2,16,128]{2,1,0:T(8,128)S(1)}, u32[]{:S(2)}, u32[]{:S(2)}) collective-permute-start(f32[2,16,128]{2,1,0:T(8,128)S(1)} %get-tuple-element.134), channel_id=1, source_target_pairs={{0,64},{32,96},{64,0},{96,32},{1,65},{33,97},{65,1},{97,33},{2,66}... | collective-permute-start | bytes 49160 | tf_op jit(solution)/shard_map/ppermute | solution.py:921
  227.8 3.8 %collective-permute-start.20 = (f32[2,16,128]{2,1,0:T(8,128)S(1)}, f32[2,16,128]{2,1,0:T(8,128)S(1)}, u32[]{:S(2)}, u32[]{:S(2)}) collective-permute-start(f32[2,16,128]{2,1,0:T(8,128)S(1)} %get-tuple-element.135), channel_id=1, source_target_pairs={{0,96},{32,0},{64,32},{96,64},{1,97},{33,1},{65,33},{97,65},{2,98}... | collective-permute-start | bytes 49160 | tf_op jit(solution)/shard_map/ppermute | solution.py:921
  231.7 5.7 %collective-permute-start.21 = (f32[2,16,128]{2,1,0:T(8,128)S(1)}, f32[2,16,128]{2,1,0:T(8,128)S(1)}, u32[]{:S(2)}, u32[]{:S(2)}) collective-permute-start(f32[2,16,128]{2,1,0:T(8,128)S(1)} %fusion.5), channel_id=1, source_target_pairs={{0,4},{4,0},{1,5},{5,1},{2,6},{6,2},{3,7},{7,3},{8,12},{12,8},{9,1... | collective-permute-start | bytes 49160 | tf_op jit(solution)/shard_map/ppermute | solution.py:974
  232.2 11.0 %copy-start = (f32[2,3,128,1024]{3,2,1,0:T(8,128)S(1)}, f32[2,3,128,1024]{3,2,1,0:T(8,128)}, u32[]{:S(2)}) copy-start(f32[2,3,128,1024]{3,2,1,0:T(8,128)} %get-tuple-element.83.refs_9_) | copy-start | bytes 9437188
  237.3 10.8 %collective-permute-start.22 = (f32[2,16,128]{2,1,0:T(8,128)S(1)}, f32[2,16,128]{2,1,0:T(8,128)S(1)}, u32[]{:S(2)}, u32[]{:S(2)}) collective-permute-start(f32[2,16,128]{2,1,0:T(8,128)S(1)} %add.126), channel_id=1, source_target_pairs={{0,1},{1,2},{2,3},{3,0},{4,5},{5,6},{6,7},{7,4},{8,9},{9,10},{10,1... | collective-permute-start | bytes 49160 | tf_op jit(solution)/shard_map/ppermute | solution.py:974
  238.2 10.0 %collective-permute-start.23 = (f32[2,16,128]{2,1,0:T(8,128)S(1)}, f32[2,16,128]{2,1,0:T(8,128)S(1)}, u32[]{:S(2)}, u32[]{:S(2)}) collective-permute-start(f32[2,16,128]{2,1,0:T(8,128)S(1)} %add.126), channel_id=1, source_target_pairs={{0,2},{1,3},{2,0},{3,1},{4,6},{5,7},{6,4},{7,5},{8,10},{9,11},{10,... | collective-permute-start | bytes 49160 | tf_op jit(solution)/shard_map/ppermute | solution.py:974
  239.6 8.6 %collective-permute-start.24 = (f32[2,16,128]{2,1,0:T(8,128)S(1)}, f32[2,16,128]{2,1,0:T(8,128)S(1)}, u32[]{:S(2)}, u32[]{:S(2)}) collective-permute-start(f32[2,16,128]{2,1,0:T(8,128)S(1)} %add.126), channel_id=1, source_target_pairs={{0,3},{1,0},{2,1},{3,2},{4,7},{5,4},{6,5},{7,6},{8,11},{9,8},{10,9... | collective-permute-start | bytes 49160 | tf_op jit(solution)/shard_map/ppermute | solution.py:974
  241.0 12.1 %copy-start.13 = (f32[2,4,128,256]{3,2,1,0:T(8,128)S(1)}, f32[2,4,128,256]{3,2,1,0:T(8,128)}, u32[]{:S(2)}) copy-start(f32[2,4,128,256]{3,2,1,0:T(8,128)} %get-tuple-element.92) | copy-start | bytes 3145732
  242.2 10.8 %collective-permute-start.15 = (bf16[4,128,256]{2,1,0:T(8,128)(2,1)S(1)}, bf16[4,128,256]{2,1,0:T(8,128)(2,1)S(1)}, u32[]{:S(2)}, u32[]{:S(2)}) collective-permute-start(bf16[4,128,256]{2,1,0:T(8,128)(2,1)S(1)} %fusion.1), channel_id=1, source_target_pairs={{0,16},{16,0},{1,17},{17,1},{2,18},{18,2},{3,19},{19,3},{4,20},{20... | collective-permute-start | bytes 786440 | tf_op jit(solution)/shard_map/ppermute | solution.py:915
  245.5 22.9 %collective-permute-start.17 = (bf16[3,128,1024]{2,1,0:T(8,128)(2,1)}, bf16[3,128,1024]{2,1,0:T(8,128)(2,1)}, u32[]{:S(2)}, u32[]{:S(2)}) collective-permute-start(bf16[3,128,1024]{2,1,0:T(8,128)(2,1)} %fusion), channel_id=1, source_target_pairs={{0,16},{16,0},{1,17},{17,1},{2,18},{18,2},{3,19},{19,3},{4,20},{20... | collective-permute-start | bytes 2359304 | tf_op jit(solution)/shard_map/ppermute | solution.py:915
Sparse Core Ops, SparseCore 0:
  51.8 43.1 all-gather.6
  100.2 37.7 all-gather.10
  144.7 30.4 all-gather.8

commit v2 on v1

--- a/solution.py
+++ b/solution.py
@@ -186,7 +186,7 @@
         n_ref[pl.ds(r, step), :] = norm_parts(taken)[0].astype(BF)
         return carry
 
-    lax.fori_loop(0, rows // step, body, 0)
+    lax.fori_loop(0, rows // step, body, 0, unroll=True)
     piece = width // len(x_refs)
     for i, ref in enumerate(x_refs):
         ref[...] = n_ref[:, columns_for(i, len(x_refs), piece)]
@@ -425,7 +425,8 @@
     *xy_refs, acts_ref, out_ref, gb_ref, b_ref, l_ref = refs
     step, steps = pl.program_id(0), pl.num_programs(0)
     rows, width = gb_ref.shape
-    piece = width // len(xy_refs)
+    count = len(xy_refs) // 2
+    piece = width // count
 
     @pl.when(step == 0)
     def _():
@@ -446,11 +447,11 @@
             gb_ref[pl.ds(r, chunk), :] = total.astype(BF)
             return carry
 
-        lax.fori_loop(0, rows // chunk, body, 0)
-        for i, ref in enumerate(xy_refs):
-            at = columns_for(i, len(xy_refs), piece)
-            ref[:, 0:piece] = pay_ref[:, at]
-            ref[:, piece:] = gb_ref[:, at]
+        lax.fori_loop(0, rows // chunk, body, 0, unroll=True)
+        for i in range(count):
+            at = columns_for(i, count, piece)
+            xy_refs[i][...] = pay_ref[:, at]
+            xy_refs[count + i][...] = gb_ref[:, at]
         b_ref[...] = jnp.zeros_like(b_ref)
         l_ref[...] = jnp.zeros_like(l_ref)
 
@@ -483,7 +484,7 @@
     rows, _, width = cotangent.shape
     hidden = wg.shape[1]
     tile = FEED_TILE
-    xy = (rows, 2 * width // count)
+    xy = (rows, width // count)
     return pl.pallas_call(
         feed_kernel,
         grid=(hidden // tile,),
@@ -495,12 +496,12 @@
             pl.BlockSpec((tile, width), lambda f: (f, 0)),
         ],
         out_specs=[
-            *[whole(xy)] * count,
+            *[whole(xy)] * (2 * count),
             pl.BlockSpec((rows, 3 * tile), lambda f: (0, f)),
             whole((rows, 2 * width)),
         ],
         out_shape=like(
-            *[(xy, BF)] * count,
+            *[(xy, BF)] * (2 * count),
             ((rows, 3 * hidden), BF),
             ((rows, 2 * width), BF),
         ),
@@ -943,7 +944,7 @@
     )
 
 
-def gathered_rows(blocks, t, wait):
+def gathered_rows(blocks, t, *waits):
     rows, width = blocks.shape[-2:]
     half = int(np.prod(blocks.shape[:-2])) // 2
     out = (half * rows // K, K, width)
@@ -951,22 +952,22 @@
     if blocks.ndim == 4:
         spec = over_tensor(blocks)
 
-    def body(t_ref, in_ref, _, out_ref):
-        out_ref[...] = in_ref[...].reshape(out)
+    def body(t_ref, in_ref, *refs):
+        refs[-1][...] = in_ref[...].reshape(out)
 
     return pl.pallas_call(
         body,
         grid_spec=pltpu.PrefetchScalarGridSpec(
             num_scalar_prefetch=1,
             grid=(2,),
-            in_specs=[spec, ANY],
+            in_specs=[spec, *[ANY] * len(waits)],
             out_specs=pl.BlockSpec(out, lambda i, t: (i, 0, 0)),
         ),
         out_shape=jax.ShapeDtypeStruct((2 * out[0], *out[1:]), blocks.dtype),
         compiler_params=params(),
         cost_estimate=cost(2.6),
         name="rows",
-    )(t, blocks, wait)
+    )(t, blocks, *waits)
 
 
 def to_each(v, axis):
@@ -1006,36 +1007,36 @@
     pay = exchange(pay, TP).reshape(rows, width + 128)
     *xy, acts, part_two = feed(pay, cotangent, w_gate, w_up, w_down, nz)
     acts = lax.all_gather(acts, "z", axis=0)
+    x_two = along_z(xy[:nz])
     turned, pair, base, gb1, dm, ds = turn_back(
-        t, mix_static, scatter_parts(part_two, TP), s1, c2, cotangent, streams, c1, b1, mt, (qall,)
-    )
-    turned = swap(turned, "yl")
-    pair = lax.dynamic_update_slice(pair, turned[None], (1, 0, 0))
+        t, mix_static, scatter_parts(part_two, TP), s1, c2, cotangent, streams, c1, b1, mt, (qall, *x_two[1:])
+    )
+    pair = lax.dynamic_update_slice(pair, swap(turned, "yl")[None], (1, 0, 0))
     gb1 = exchange(gb1, TP).reshape(rows, width)
-    do, gq = query_back(placement, gb1, w_output, q, kv, log, same, other, trig, (pair,))
+    y_two = along_z(xy[nz:])
+    do, gq = query_back(placement, gb1, w_output, q, kv, log, same, other, trig, (pair, *y_two[1:],))
+    own_pair = pair
     pair = lax.all_gather(pin(pair, gb1), "x", axis=0)
     tiles = w_gate.shape[1] // FEED_TILE
-    xy = along_z([pin(v, gq) for v in xy])
     do_same = exchange(do, ("z", "yh"))
-    do_same = pin(do_same, *xy[1:])
     do_other = swap(do_same, "core")
     part_three, *ship = key_back(
         placement, kv, qall, do_same, do_other, gq, trig, w_query, w_key, w_value, gb1, attended, nz,
         (),
     )
     ff_keep, ff_give = weight_part(
-        ((xy, 0), (xy, 2)), acts, tiles, (0, 0, 1), FEED_TILE, "feed_weights", 8, (part_three,)
+        ((x_two, 0), (y_two, 0)), acts, tiles, (0, 0, 1), FEED_TILE, "feed_weights", 8, (part_three,)
     )
     ship = along_z(ship)
     gt, mix_keep, mix_give = last(
         t, mix_static, scatter_parts(part_three, TP), base, streams, c1, mt, dm, ds, (ff_keep,)
     )
-    streams_out = gathered_rows(pair, t, mix_keep)
-    gt = exchange(gt, TP)
-    grad_streams = gathered_rows(gt, t, streams_out)
     ff_keep, ff_give = over_core(ff_keep, swap(ff_give, "core"))
-    ff = ff_keep + swap(ff_give, "yh").astype(F32)
+    ff_got = swap(ff_give, "yh")
+    ff = ff_keep + ff_got.astype(F32)
+
     v = mix_keep + swap(mix_give, "core")
+    mix_low = v
     yh, z = lax.axis_index("yh"), lax.axis_index("z")
 
     def half(at):
@@ -1048,6 +1049,7 @@
         return jnp.stack([pick(v, lax.rem(at, nz)), v[nz]])
 
     v = sum(along_z([mine(z + i) for i in range(nz)]))
+    mix_high = v
     v = to_each(to_each(v, "yl"), "x")
     grad_dynamic = jnp.transpose(v[0].reshape(2, 8, -1)[:, :6], (0, 2, 1))
     grad_static = v[1].reshape(2, 8, 128)[:, :4, :6]
@@ -1056,7 +1058,9 @@
     )
     keep, give = over_core(keep, swap(give, "core"))
     tail = keep + swap(give, "yh").astype(F32)
-
+    streams_out = gathered_rows(pair, t, mix_keep)
+    gt = exchange(gt, TP)
+    grad_streams = gathered_rows(gt, t, streams_out)
     return (
         streams_out,
         grad_streams,

time: 280 us -> 270 us (0.964)
  waiting for transfers between devices: 67.4 us -> 60.3 us
  starting transfers between devices: 49.1 us -> 53 us
  Pallas kernels: 70.6 us -> 66.9 us
    ppermute x12 -> x15, starting transfers between devices: 15.3 us -> 21.5 us  [along_z(): lax.ppermute(pieces[i], 'z', [(a, (a + i) % n) for a in range(n)])]
    ppermute x9, waiting for transfers between devices: 23.4 us -> 17.9 us  [swap(): return lax.ppermute(v, axis, [(0, 1), (1, 0)])]
    ppermute x12 -> x15, waiting for transfers between devices: 34.2 us -> 37.4 us  [along_z(): lax.ppermute(pieces[i], 'z', [(a, (a + i) % n) for a in range(n)])]
    all_to_all x5, starting transfers between devices: 22.7 us -> 19.6 us  [exchange(): return lax.all_to_all(blocks, axes, 0, 0, tiled=True)]
    pallas_call x1, Pallas kernels: 11 us -> 7.95 us  [first(): pl.pallas_call(first_kernel, grid=(1,), out_shape=like(*outs), in_specs=[...]
    all_to_all x5, waiting for transfers between devices: 6.69 us -> 3.81 us  [exchange(): return lax.all_to_all(blocks, axes, 0, 0, tiled=True)]
    unnamed x53 -> x75, local copies, waits for them, and re-layouts: 8.88 us -> 8.71 us
  transfers between devices with their start and end apart: 33 -> 36, of which waited for: 19 -> 20; matrix products, arithmetic and copies ran while one was open for 3% -> 4% of each run, Pallas kernels for 20% -> 20%
where the time goes in v2:
time: 270 us; the launch traced here: 269 us
  Pallas kernels  66.9 us (25%)
  waiting for transfers between devices  60.3 us (22%)
  blocking collectives  55.3 us (20%)
  starting transfers between devices  53 us (20%)
  between operations  14.1 us (5%)
  local copies, waits for them, and re-layouts  11.9 us (4%)
  other arithmetic  7.85 us (3%)
    all_to_all x3, blocking collectives, exchange(): return lax.all_to_all(blocks, axes, 0, 0, tiled=True)  55.3 us
    ppermute x15, waiting for transfers between devices, along_z(): lax.ppermute(pieces[i], 'z', [(a, (a + i) % n) for a in range(n)])  37.4 us
    ppermute x15, starting transfers between devices, along_z(): lax.ppermute(pieces[i], 'z', [(a, (a + i) % n) for a in range(n)])  21.5 us
    all_to_all x5, starting transfers between devices, exchange(): return lax.all_to_all(blocks, axes, 0, 0, tiled=True)  19.6 us
    ppermute x9, waiting for transfers between devices, swap(): return lax.ppermute(v, axis, [(0, 1), (1, 0)])  17.9 us
    pallas_call x1, Pallas kernels, feed(): pl.pallas_call(feed_kernel, grid=(hidden // tile,), in_specs=[whole(pay.s...  13.2 us
    pallas_call x3, Pallas kernels, token_call(): pl.pallas_call(body, grid_spec=pltpu.PrefetchScalarGridSpec(num_scalar_pr...  13 us
    pallas_call x2, Pallas kernels, weight_part(): pl.pallas_call(functools.partial(weight_kernel, picks, tile, count, gathe...  10.8 us
  transfers between devices with their start and end apart: 36, of which 20 were waited for; matrix products, arithmetic and copies ran while one was open for 4% of the time, Pallas kernels for 20%

profile of v2, /device:TPU:0, one launch (start us, length us, event | category | flops | bytes accessed | tf_op | source)
XLA Modules:
  0.0 269.3 jit_solution(9830566131343304354)
XLA Ops:
  7.2 8.0 %first.1 = (f32[512,128]{1,0:T(8,128)}, bf16[128,256]{1,0:T(8,128)(2,1)}, bf16[8,128,512]{2,1,0:T(8,128)(2,1)}, f32[2,128,128]{2,1,0:T(8,128)}, bf16[128,512]{1,...) custom-call(s32[16]{0:T(128)} %place_ref.7, f32[2,4,6]{2,1,0:T(4,128)} %refs_1_.5, ...), custom_call_target="tpu_custom_call" | custom-call | bytes 36900000 | tf_op jit(solution)/shard_map/first/pallas_call | solution.py:226
  15.2 25.2 %all_to_all.40.same_ref = bf16[8,128,512]{2,1,0:T(8,128)(2,1)S(1)} all-to-all(bf16[8,128,512]{2,1,0:T(8,128)(2,1)} %get-tuple-element.58.own_ref), channel_id=1, replica_groups=mesh['z'=4,'yh'=2,'core'=2,'yl'=2,'x'=4] {'z','yh'}, dimensions={0} | all-to-all | bytes 2097152 | tf_op jit(solution)/shard_map/all_to_all | solution.py:907
  40.4 2.7 collective-permute-done.other_ref
  43.1 1.0 copy-done.3
  44.1 4.5 %attend.1 = (bf16[128,256]{1,0:T(8,128)(2,1)}, f32[1,256]{1,0:T(1,128)}, bf16[128,2048]{1,0:T(8,128)(2,1)}, bf16[128,256]{1,0:T(8,128)(2,1)}) custom-call(s32[16]{0:T(128)} %place_ref.7, bf16[128,256]{1,0:T(8,128)(2,1)} %get-tuple-element.57.q_ref, bf16[8,128,512]{2,1,0:T(8,128)(2,1)} %get-tuple-element.58.own_ref, bf16[8,128,512]{2,1,0:T(8,128)(2,1)} %copy-done.1, ...), custom_call_target="tpu_custom_call" | custom-call | bytes 16605000 | tf_op jit(solution)/shard_map/attend/pallas_call | solution.py:321
  48.6 4.5 %all-to-all-start.1 = ((bf16[8,16,2048]{2,1,0:T(8,128)(2,1)}), bf16[8,16,2048]{2,1,0:T(8,128)(2,1)S(1)}, u32[]{:S(2)}, u32[]{:S(2)}) async-start(bf16[8,16,2048]{2,1,0:T(8,128)(2,1)} %bitcast.60), calls=%async_computation.1 | async-start | bytes 1048576 | tf_op jit(solution)/shard_map/all_to_all | solution.py:907
  53.4 2.1 collective-permute-start.2
  55.4 1.5 collective-permute-start.3
  57.0 5.9 %collective-permute-done.1.refs_6_.refs_5_ = bf16[128,512]{1,0:T(8,128)(2,1)S(1)} collective-permute-done((bf16[128,512]{1,0:T(8,128)(2,1)S(1)}, bf16[128,512]{1,0:T(8,128)(2,1)S(1)}, u32[]{:S(2)}, u32[]{:S(2)}) %collective-permute-start.1) | collective-permute-done | bytes 131104 | tf_op jit(solution)/shard_map/ppermute | solution.py:922
  64.4 3.3 %middle.1 = (f32[4,16,2048]{2,1,0:T(8,128)}, f32[16,2048]{1,0:T(8,128)}, f32[4,16,128]{2,1,0:T(8,128)}, bf16[8,16,2176]{2,1,0:T(8,128)(2,1)}) custom-call(s32[1]{0:T(128)} %bitcast.refs_0_.t_ref, f32[2,4,6]{2,1,0:T(4,128)} %refs_1_.5, bf16[8,16,2048]{2,1,0:T(8,128)(2,1)} %copy-done.7, bf16[128,4,2048]{2,1,0:T(4,128)(2,1)} %refs_4_.1, ...), custom_call_target="tpu_custom_call" | custom-call | bytes 14760000 | tf_op jit(solution)/shard_map/middle/pallas_call | solution.py:380
  67.7 15.3 %all_to_all.41 = bf16[8,16,2176]{2,1,0:T(8,128)(2,1)} all-to-all(bf16[8,16,2176]{2,1,0:T(8,128)(2,1)} %get-tuple-element.64), channel_id=1, replica_groups=mesh['z'=4,'yh'=2,'core'=2,'yl'=2,'x'=4] {'yl','x'}, dimensions={0} | all-to-all | bytes 1114112 | tf_op jit(solution)/shard_map/all_to_all | solution.py:907
  83.0 13.2 %feed.1 = (bf16[128,512]{1,0:T(8,128)(2,1)}, bf16[128,512]{1,0:T(8,128)(2,1)}, bf16[128,512]{1,0:T(8,128)(2,1)}, bf16[128,512]{1,0:T(8,128)(2,1)}, bf16[128,512]...) custom-call(bf16[128,2176]{1,0:T(8,128)(2,1)} %bitcast.52, ...), custom_call_target="tpu_custom_call" | custom-call | bytes 51660000 | tf_op jit(solution)/shard_map/feed/pallas_call | solution.py:488
  96.3 3.7 %all-to-all-start.3 = ((bf16[8,16,4096]{2,1,0:T(8,128)(2,1)}), bf16[8,16,4096]{2,1,0:T(8,128)(2,1)S(1)}, u32[]{:S(2)}, u32[]{:S(2)}) async-start(bf16[8,16,4096]{2,1,0:T(8,128)(2,1)} %bitcast.59), calls=%async_computation.3 | async-start | bytes 2097152 | tf_op jit(solution)/shard_map/all_to_all | solution.py:907
  100.6 4.6 %collective-permute-start.5 = (bf16[128,512]{1,0:T(8,128)(2,1)S(1)}, bf16[128,512]{1,0:T(8,128)(2,1)S(1)}, u32[]{:S(2)}, u32[]{:S(2)}) collective-permute-start(bf16[128,512]{1,0:T(8,128)(2,1)S(1)} %copy-done.34), channel_id=1, source_target_pairs={{0,64},{32,96},{64,0},{96,32},{1,65},{33,97},{65,1},{97,33},{2,66}... | collective-permute-start | bytes 393224 | tf_op jit(solution)/shard_map/ppermute | solution.py:922
  105.3 2.9 %collective-permute-done.4.refs_11_.refs_1_ = bf16[128,512]{1,0:T(8,128)(2,1)S(1)} collective-permute-done((bf16[128,512]{1,0:T(8,128)(2,1)S(1)}, bf16[128,512]{1,0:T(8,128)(2,1)S(1)}, u32[]{:S(2)}, u32[]{:S(2)}) %collective-permute-start.4) | collective-permute-done | bytes 131104 | tf_op jit(solution)/shard_map/ppermute | solution.py:922
  108.1 4.1 %collective-permute-done.5.refs_12_.refs_2_ = bf16[128,512]{1,0:T(8,128)(2,1)S(1)} collective-permute-done((bf16[128,512]{1,0:T(8,128)(2,1)S(1)}, bf16[128,512]{1,0:T(8,128)(2,1)S(1)}, u32[]{:S(2)}, u32[]{:S(2)}) %collective-permute-start.5) | collective-permute-done | bytes 131104 | tf_op jit(solution)/shard_map/ppermute | solution.py:922
  112.2 1.8 collective-permute-done.6.refs_13_.refs_3_
  115.0 5.8 %turn.1 = (bf16[64,2048]{1,0:T(8,128)(2,1)}, bf16[2,64,2048]{2,1,0:T(8,128)(2,1)}, f32[4,16,2048]{2,1,0:T(8,128)}, bf16[8,16,2048]{2,1,0:T(8,128)(2,1)}, f32[2,8,2048]{2,1,0:T(8,128)}, /*index=5*/f32[2,8,128]{2,1,0:T(8,128)}) custom-call(s32[1]{0:T(128)} %bitcast.refs_0_.t_ref, f32[2,4,6]{2,1,0:T(4,128)} %refs_1_.5, bf16[8,16,4096]{2,1,0:T(8,128)(2,1)} %copy-done.4, ...), custom_call_target="tpu_custom_call" | custom-call | bytes 14760000 | tf_op jit(solution)/shard_map/turn/pallas_call | solution.py:380
  120.8 2.1 collective-permute-start.7
  122.9 2.8 %collective-permute-start.10 = (bf16[128,512]{1,0:T(8,128)(2,1)S(1)}, bf16[128,512]{1,0:T(8,128)(2,1)S(1)}, u32[]{:S(2)}, u32[]{:S(2)}) collective-permute-start(bf16[128,512]{1,0:T(8,128)(2,1)S(1)} %copy-done.29), channel_id=1, source_target_pairs={{0,96},{32,0},{64,32},{96,64},{1,97},{33,1},{65,33},{97,65},{2,98}... | collective-permute-start | bytes 393224 | tf_op jit(solution)/shard_map/ppermute | solution.py:922
  125.7 1.5 collective-permute-start.9
  127.2 3.5 %all-to-all-start.4 = ((bf16[8,16,2048]{2,1,0:T(8,128)(2,1)}), bf16[8,16,2048]{2,1,0:T(8,128)(2,1)S(1)}, u32[]{:S(2)}, u32[]{:S(2)}) async-start(bf16[8,16,2048]{2,1,0:T(8,128)(2,1)} %get-tuple-element.75), calls=%async_computation.4 | async-start | bytes 1048576 | tf_op jit(solution)/shard_map/all_to_all | solution.py:907
  131.4 2.2 collective-permute-done.10.refs_3_.refs_7_
  133.6 3.9 %collective-permute-done.8.refs_1_.refs_5_ = bf16[128,512]{1,0:T(8,128)(2,1)S(1)} collective-permute-done((bf16[128,512]{1,0:T(8,128)(2,1)S(1)}, bf16[128,512]{1,0:T(8,128)(2,1)S(1)}, u32[]{:S(2)}, u32[]{:S(2)}) %collective-permute-start.8) | collective-permute-done | bytes 131104 | tf_op jit(solution)/shard_map/ppermute | solution.py:922
  137.5 1.9 collective-permute-done.9.refs_2_.refs_6_
  140.8 5.2 %query_back.1 = (bf16[8,144,256]{2,1,0:T(8,128)(2,1)}, bf16[128,256]{1,0:T(8,128)(2,1)}) custom-call(s32[16]{0:T(128)} %place_ref.7, bf16[128,2048]{1,0:T(8,128)(2,1)} %bitcast.46, bf16[256,2048]{1,0:T(8,128)(2,1)} %wo_ref.3, bf16[128,256]{1,0:T(8,128)(2,1)} %get-tuple-element.69.q_ref, bf16[8,128,512]{2,1,0:T(8,128)(2,1)} %get-tuple-element.58.own_ref, ...), custom_call_target="tpu_custom_call" | custom-call | bytes 20295000 | tf_op jit(solution)/shard_map/query_back/pallas_call | solution.py:678
  147.1 14.8 %all_to_all.42.same_ref = bf16[8,144,256]{2,1,0:T(8,128)(2,1)S(1)} all-to-all(bf16[8,144,256]{2,1,0:T(8,128)(2,1)S(1)} %copy-done.13), channel_id=1, replica_groups=mesh['z'=4,'yh'=2,'core'=2,'yl'=2,'x'=4] {'z','yh'}, dimensions={0} | all-to-all | bytes 1179648 | tf_op jit(solution)/shard_map/all_to_all | solution.py:907
  161.8 2.0 collective-permute-done.11.other_ref
  163.8 0.8 copy-done.12
  164.6 6.9 %key_back.1 = (bf16[128,2048]{1,0:T(8,128)(2,1)}, bf16[128,1536]{1,0:T(8,128)(2,1)}, bf16[128,1536]{1,0:T(8,128)(2,1)}, bf16[128,1536]{1,0:T(8,128)(2,1)}, bf16[128,1536]{1,0:T(8,128)(2,1)}) custom-call(s32[16]{0:T(128)} %place_ref.7, bf16[8,128,512]{2,1,0:T(8,128)(2,1)} %get-tuple-element.58.own_ref, bf16[16,128,256]{2,1,0:T(8,128)(2,1)} %bitcast.50, ...), custom_call_target="tpu_custom_call" | custom-call | bytes 23985000 | tf_op jit(solution)/shard_map/key_back/pallas_call | solution.py:752
  171.5 3.5 %all-to-all-start.6 = ((bf16[8,16,2048]{2,1,0:T(8,128)(2,1)}), bf16[8,16,2048]{2,1,0:T(8,128)(2,1)S(1)}, u32[]{:S(2)}, u32[]{:S(2)}) async-start(bf16[8,16,2048]{2,1,0:T(8,128)(2,1)} %bitcast.53), calls=%async_computation.6 | async-start | bytes 1048576 | tf_op jit(solution)/shard_map/all_to_all | solution.py:907
  175.0 7.0 %feed_weights.1 = (f32[2,3,128,1024]{3,2,1,0:T(8,128)}, bf16[2,3,128,1024]{3,2,1,0:T(8,128)(2,1)}) custom-call(bf16[128,512]{1,0:T(8,128)(2,1)} %get-tuple-element.88.refs_0_, bf16[128,512]{1,0:T(8,128)(2,1)} %copy-done.14, bf16[128,512]{1,0:T(8,128)(2,1)} %copy-done.15, bf16[128,512]{1,0:T(8,128)(2,1)} %copy-done.16, ...), custom_call_target="tpu_custom_call" | custom-call | bytes 29520000 | tf_op jit(solution)/shard_map/feed_weights/pallas_call | solution.py:893
  182.4 3.2 %all-to-all-done.6.refs_2_ = bf16[8,16,2048]{2,1,0:T(8,128)(2,1)S(1)} async-done(((bf16[8,16,2048]{2,1,0:T(8,128)(2,1)}), bf16[8,16,2048]{2,1,0:T(8,128)(2,1)S(1)}, u32[]{:S(2)}, u32[]{:S(2)}) %all-to-all-start.6) | async-done | bytes 524320 | tf_op jit(solution)/shard_map/all_to_all | solution.py:907
  185.7 0.8 copy-done.6
  186.5 3.9 %last.1 = (bf16[8,64,2048]{2,1,0:T(8,128)(2,1)}, f32[9,16,128]{2,1,0:T(8,128)}, f32[9,16,128]{2,1,0:T(8,128)}) custom-call(s32[1]{0:T(128)} %bitcast.refs_0_.t_ref, f32[2,4,6]{2,1,0:T(4,128)} %refs_1_.5, bf16[8,16,2048]{2,1,0:T(8,128)(2,1)} %copy-done.6, f32[4,16,2048]{2,1,0:T(8,128)} %get-tuple-element.85.refs_3_, bf16[128,4,2048]{2,1,0:T(4,128)(2,1)} %refs_4_.1, ...), custom_call_target="tpu_custom_call" | custom-call | bytes 14760000 | tf_op jit(solution)/shard_map/last/pallas_call | solution.py:380
  191.0 2.0 collective-permute-start.13
  193.0 1.3 collective-permute-start.14
  194.3 0.9 add.102
  195.2 1.5 collective-permute-start.16
  196.8 4.3 %all-to-all-start.7 = ((bf16[8,64,2048]{2,1,0:T(8,128)(2,1)}), bf16[8,64,2048]{2,1,0:T(8,128)(2,1)}, u32[]{:S(2)}, u32[]{:S(2)}) async-start(bf16[8,64,2048]{2,1,0:T(8,128)(2,1)} %get-tuple-element.93), calls=%async_computation.7 | async-start | bytes 4194304 | tf_op jit(solution)/shard_map/all_to_all | solution.py:907
  201.7 9.8 %collective-permute-done.12.refs_1_.refs_9_ = bf16[128,1536]{1,0:T(8,128)(2,1)S(1)} collective-permute-done((bf16[128,1536]{1,0:T(8,128)(2,1)S(1)}, bf16[128,1536]{1,0:T(8,128)(2,1)S(1)}, u32[]{:S(2)}, u32[]{:S(2)}) %collective-permute-start.12) | collective-permute-done | bytes 393248 | tf_op jit(solution)/shard_map/ppermute | solution.py:922
  212.9 3.8 %tail_weights.1 = (f32[2,4,128,256]{3,2,1,0:T(8,128)}, bf16[2,4,128,256]{3,2,1,0:T(8,128)(2,1)}) custom-call(bf16[128,1536]{1,0:T(8,128)(2,1)} %get-tuple-element.94.refs_0_.refs_8_, bf16[128,1536]{1,0:T(8,128)(2,1)} %copy-done.8, bf16[128,1536]{1,0:T(8,128)(2,1)} %copy-done.9, bf16[128,1536]{1,0:T(8,128)(2,1)} %copy-done.10, ...), custom_call_target="tpu_custom_call" | custom-call | bytes 14760000 | tf_op jit(solution)/shard_map/tail_weights/pallas_call | solution.py:893
  216.9 0.7 collective-permute-start.21
  217.6 3.5 %collective-permute-start.22 = (f32[2,16,128]{2,1,0:T(8,128)S(1)}, f32[2,16,128]{2,1,0:T(8,128)S(1)}, u32[]{:S(2)}, u32[]{:S(2)}) collective-permute-start(f32[2,16,128]{2,1,0:T(8,128)S(1)} %get-tuple-element.142), channel_id=1, source_target_pairs={{0,64},{32,96},{64,0},{96,32},{1,65},{33,97},{65,1},{97,33},{2,66}... | collective-permute-start | bytes 49160 | tf_op jit(solution)/shard_map/ppermute | solution.py:922
  221.1 0.7 collective-permute-done.21
  221.9 1.1 collective-permute-done.22
  223.0 1.9 collective-permute-done.23
  225.4 2.8 %rows.2.refs_0_ = bf16[128,4,2048]{2,1,0:T(4,128)(2,1)} custom-call(s32[1]{0:T(128)} %bitcast.refs_0_.t_ref, bf16[4,2,64,2048]{3,2,1,0:T(8,128)(2,1)} %bitcast.54, f32[9,16,128]{2,1,0:T(8,128)} %get-tuple-element.92.refs_0_), custom_call_target="tpu_custom_call" | custom-call | bytes 9594000 | tf_op jit(solution)/shard_map/rows/pallas_call | solution.py:958
  228.6 0.7 collective-permute-start.25
  229.4 1.9 collective-permute-start.26
  231.2 0.9 collective-permute-start.27
  232.1 1.3 fusion.1
  233.4 1.7 collective-permute-start.18
  235.1 2.3 fusion
  237.4 1.9 collective-permute-start.20
  240.6 2.6 collective-permute-done.18
  243.1 1.0 bitcast_add_fusion.1
  244.2 0.8 slice_bitcast_fusion.3
  244.9 0.8 copy.29
  245.7 2.6 rows.3
  248.3 10.7 %collective-permute-done.20 = bf16[3,128,1024]{2,1,0:T(8,128)(2,1)} collective-permute-done((bf16[3,128,1024]{2,1,0:T(8,128)(2,1)}, bf16[3,128,1024]{2,1,0:T(8,128)(2,1)}, u32[]{:S(2)}, u32[]{:S(2)}) %collective-permute-start.20) | collective-permute-done | bytes 786464 | tf_op jit(solution)/shard_map/ppermute | solution.py:916
  259.0 1.7 bitcast_add_fusion
  260.7 1.1 slice_bitcast_fusion
  261.8 1.0 copy.30
  (121 shorter events, 12.1 us)
Async XLA Ops:
  7.2 106.8 %all-gather.7.cloned.1.call-start = ((), (), s32[]{:S(2)}) async-start(), calls=%async_computation.8 | async-start | bytes 1114112 | tf_op jit(solution)/shard_map/all_gather | solution.py:1002
  40.4 2.7 copy-start.1
  40.4 2.7 collective-permute-start
  43.1 1.0 copy-start.3
  44.1 9.1 %copy-start.32 = (bf16[128,512]{1,0:T(8,128)(2,1)S(1)}, bf16[128,512]{1,0:T(8,128)(2,1)}, u32[]{:S(2)}) copy-start(bf16[128,512]{1,0:T(8,128)(2,1)} %get-tuple-element.61) | copy-start | bytes 393220
  44.1 9.3 %copy-start.31 = (bf16[128,512]{1,0:T(8,128)(2,1)S(1)}, bf16[128,512]{1,0:T(8,128)(2,1)}, u32[]{:S(2)}) copy-start(bf16[128,512]{1,0:T(8,128)(2,1)} %get-tuple-element.62) | copy-start | bytes 393220
  44.1 11.4 %copy-start.30 = (bf16[128,512]{1,0:T(8,128)(2,1)S(1)}, bf16[128,512]{1,0:T(8,128)(2,1)}, u32[]{:S(2)}) copy-start(bf16[128,512]{1,0:T(8,128)(2,1)} %get-tuple-element.63) | copy-start | bytes 393220
  48.6 15.0 %all-to-all-start.1 = ((bf16[8,16,2048]{2,1,0:T(8,128)(2,1)}), bf16[8,16,2048]{2,1,0:T(8,128)(2,1)S(1)}, u32[]{:S(2)}, u32[]{:S(2)}) async-start(bf16[8,16,2048]{2,1,0:T(8,128)(2,1)} %bitcast.60), calls=%async_computation.1 | async-start | bytes 1048576 | tf_op jit(solution)/shard_map/all_to_all | solution.py:907
  53.1 121.9 %all-gather.11.cloned.1.call-start = ((), (), s32[]{:S(2)}) async-start(), calls=%async_computation.10 | async-start | bytes 3932160 | tf_op jit(solution)/shard_map/all_gather | solution.py:1009
  53.2 9.7 %collective-permute-start.1 = (bf16[128,512]{1,0:T(8,128)(2,1)S(1)}, bf16[128,512]{1,0:T(8,128)(2,1)S(1)}, u32[]{:S(2)}, u32[]{:S(2)}) collective-permute-start(bf16[128,512]{1,0:T(8,128)(2,1)S(1)} %copy-done.32), channel_id=1, source_target_pairs={{0,32},{32,64},{64,96},{96,0},{1,33},{33,65},{65,97},{97,1},{2,34}... | collective-permute-start | bytes 393224 | tf_op jit(solution)/shard_map/ppermute | solution.py:922
  53.4 9.5 %collective-permute-start.2 = (bf16[128,512]{1,0:T(8,128)(2,1)S(1)}, bf16[128,512]{1,0:T(8,128)(2,1)S(1)}, u32[]{:S(2)}, u32[]{:S(2)}) collective-permute-start(bf16[128,512]{1,0:T(8,128)(2,1)S(1)} %copy-done.31), channel_id=1, source_target_pairs={{0,64},{32,96},{64,0},{96,32},{1,65},{33,97},{65,1},{97,33},{2,66}... | collective-permute-start | bytes 393224 | tf_op jit(solution)/shard_map/ppermute | solution.py:922
  55.4 8.1 %collective-permute-start.3 = (bf16[128,512]{1,0:T(8,128)(2,1)S(1)}, bf16[128,512]{1,0:T(8,128)(2,1)S(1)}, u32[]{:S(2)}, u32[]{:S(2)}) collective-permute-start(bf16[128,512]{1,0:T(8,128)(2,1)S(1)} %copy-done.30), channel_id=1, source_target_pairs={{0,96},{32,0},{64,32},{96,64},{1,97},{33,1},{65,33},{97,65},{2,98}... | collective-permute-start | bytes 393224 | tf_op jit(solution)/shard_map/ppermute | solution.py:922
  63.6 0.8 copy-start.7
  96.2 3.8 %copy-start.35 = (bf16[128,512]{1,0:T(8,128)(2,1)S(1)}, bf16[128,512]{1,0:T(8,128)(2,1)}, u32[]{:S(2)}) copy-start(bf16[128,512]{1,0:T(8,128)(2,1)} %get-tuple-element.70) | copy-start | bytes 393220
  96.2 4.4 %copy-start.34 = (bf16[128,512]{1,0:T(8,128)(2,1)S(1)}, bf16[128,512]{1,0:T(8,128)(2,1)}, u32[]{:S(2)}) copy-start(bf16[128,512]{1,0:T(8,128)(2,1)} %get-tuple-element.71) | copy-start | bytes 393220
  96.2 9.0 %copy-start.33 = (bf16[128,512]{1,0:T(8,128)(2,1)S(1)}, bf16[128,512]{1,0:T(8,128)(2,1)}, u32[]{:S(2)}) copy-start(bf16[128,512]{1,0:T(8,128)(2,1)} %get-tuple-element.72) | copy-start | bytes 393220
  96.3 17.7 %all-to-all-start.3 = ((bf16[8,16,4096]{2,1,0:T(8,128)(2,1)}), bf16[8,16,4096]{2,1,0:T(8,128)(2,1)S(1)}, u32[]{:S(2)}, u32[]{:S(2)}) async-start(bf16[8,16,4096]{2,1,0:T(8,128)(2,1)} %bitcast.59), calls=%async_computation.3 | async-start | bytes 2097152 | tf_op jit(solution)/shard_map/all_to_all | solution.py:907
  100.0 8.1 %collective-permute-start.4 = (bf16[128,512]{1,0:T(8,128)(2,1)S(1)}, bf16[128,512]{1,0:T(8,128)(2,1)S(1)}, u32[]{:S(2)}, u32[]{:S(2)}) collective-permute-start(bf16[128,512]{1,0:T(8,128)(2,1)S(1)} %copy-done.35), channel_id=1, source_target_pairs={{0,32},{32,64},{64,96},{96,0},{1,33},{33,65},{65,97},{97,1},{2,34}... | collective-permute-start | bytes 393224 | tf_op jit(solution)/shard_map/ppermute | solution.py:922
  100.6 11.6 %collective-permute-start.5 = (bf16[128,512]{1,0:T(8,128)(2,1)S(1)}, bf16[128,512]{1,0:T(8,128)(2,1)S(1)}, u32[]{:S(2)}, u32[]{:S(2)}) collective-permute-start(bf16[128,512]{1,0:T(8,128)(2,1)S(1)} %copy-done.34), channel_id=1, source_target_pairs={{0,64},{32,96},{64,0},{96,32},{1,65},{33,97},{65,1},{97,33},{2,66}... | collective-permute-start | bytes 393224 | tf_op jit(solution)/shard_map/ppermute | solution.py:922
  105.3 8.7 %collective-permute-start.6 = (bf16[128,512]{1,0:T(8,128)(2,1)S(1)}, bf16[128,512]{1,0:T(8,128)(2,1)S(1)}, u32[]{:S(2)}, u32[]{:S(2)}) collective-permute-start(bf16[128,512]{1,0:T(8,128)(2,1)S(1)} %copy-done.33), channel_id=1, source_target_pairs={{0,96},{32,0},{64,32},{96,64},{1,97},{33,1},{65,33},{97,65},{2,98}... | collective-permute-start | bytes 393224 | tf_op jit(solution)/shard_map/ppermute | solution.py:922
  108.1 5.9 %copy-start.14 = (bf16[128,512]{1,0:T(8,128)(2,1)}, bf16[128,512]{1,0:T(8,128)(2,1)S(1)}, u32[]{:S(2)}) copy-start(bf16[128,512]{1,0:T(8,128)(2,1)S(1)} %collective-permute-done.4.refs_11_.refs_1_) | copy-start | bytes 393220
  112.2 1.8 copy-start.15
  114.0 1.0 copy-start.4
  115.0 7.9 %copy-start.29 = (bf16[128,512]{1,0:T(8,128)(2,1)S(1)}, bf16[128,512]{1,0:T(8,128)(2,1)}, u32[]{:S(2)}) copy-start(bf16[128,512]{1,0:T(8,128)(2,1)} %get-tuple-element.80) | copy-start | bytes 393220
  115.0 10.7 %copy-start.28 = (bf16[128,512]{1,0:T(8,128)(2,1)S(1)}, bf16[128,512]{1,0:T(8,128)(2,1)}, u32[]{:S(2)}) copy-start(bf16[128,512]{1,0:T(8,128)(2,1)} %get-tuple-element.78) | copy-start | bytes 393220
  115.0 10.7 %copy-start.27 = (bf16[128,512]{1,0:T(8,128)(2,1)S(1)}, bf16[128,512]{1,0:T(8,128)(2,1)}, u32[]{:S(2)}) copy-start(bf16[128,512]{1,0:T(8,128)(2,1)} %get-tuple-element.79) | copy-start | bytes 393220
  120.8 9.9 %collective-permute-start.7 = (bf16[64,2048]{1,0:T(8,128)(2,1)}, bf16[64,2048]{1,0:T(8,128)(2,1)S(1)}, u32[]{:S(2)}, u32[]{:S(2)}) collective-permute-start(bf16[64,2048]{1,0:T(8,128)(2,1)} %get-tuple-element.74), channel_id=1, source_target_pairs={{0,4},{4,0},{1,5},{5,1},{2,6},{6,2},{3,7},{7,3},{8,12},{12,8},{9,1... | collective-permute-start | bytes 786440 | tf_op jit(solution)/shard_map/ppermute | solution.py:916
  122.9 10.7 %collective-permute-start.10 = (bf16[128,512]{1,0:T(8,128)(2,1)S(1)}, bf16[128,512]{1,0:T(8,128)(2,1)S(1)}, u32[]{:S(2)}, u32[]{:S(2)}) collective-permute-start(bf16[128,512]{1,0:T(8,128)(2,1)S(1)} %copy-done.29), channel_id=1, source_target_pairs={{0,96},{32,0},{64,32},{96,64},{1,97},{33,1},{65,33},{97,65},{2,98}... | collective-permute-start | bytes 393224 | tf_op jit(solution)/shard_map/ppermute | solution.py:922
  125.7 11.8 %collective-permute-start.8 = (bf16[128,512]{1,0:T(8,128)(2,1)S(1)}, bf16[128,512]{1,0:T(8,128)(2,1)S(1)}, u32[]{:S(2)}, u32[]{:S(2)}) collective-permute-start(bf16[128,512]{1,0:T(8,128)(2,1)S(1)} %copy-done.28), channel_id=1, source_target_pairs={{0,32},{32,64},{64,96},{96,0},{1,33},{33,65},{65,97},{97,1},{2,34}... | collective-permute-start | bytes 393224 | tf_op jit(solution)/shard_map/ppermute | solution.py:922
  125.7 13.7 %collective-permute-start.9 = (bf16[128,512]{1,0:T(8,128)(2,1)S(1)}, bf16[128,512]{1,0:T(8,128)(2,1)S(1)}, u32[]{:S(2)}, u32[]{:S(2)}) collective-permute-start(bf16[128,512]{1,0:T(8,128)(2,1)S(1)} %copy-done.27), channel_id=1, source_target_pairs={{0,64},{32,96},{64,0},{96,32},{1,65},{33,97},{65,1},{97,33},{2,66}... | collective-permute-start | bytes 393224 | tf_op jit(solution)/shard_map/ppermute | solution.py:922
  127.2 12.8 %all-to-all-start.4 = ((bf16[8,16,2048]{2,1,0:T(8,128)(2,1)}), bf16[8,16,2048]{2,1,0:T(8,128)(2,1)S(1)}, u32[]{:S(2)}, u32[]{:S(2)}) async-start(bf16[8,16,2048]{2,1,0:T(8,128)(2,1)} %get-tuple-element.75), calls=%async_computation.4 | async-start | bytes 1048576 | tf_op jit(solution)/shard_map/all_to_all | solution.py:907
  133.6 6.4 %copy-start.20 = (bf16[128,512]{1,0:T(8,128)(2,1)}, bf16[128,512]{1,0:T(8,128)(2,1)S(1)}, u32[]{:S(2)}) copy-start(bf16[128,512]{1,0:T(8,128)(2,1)S(1)} %collective-permute-done.10.refs_3_.refs_7_) | copy-start | bytes 393220
  137.5 2.5 copy-start.21
  140.0 0.8 copy-start.2
  146.0 1.1 copy-start.13
  146.0 79.4 %all-gather.9.cloned.1.call-start = ((), (), s32[]{:S(2)}) async-start(), calls=%async_computation.9 | async-start | bytes 2621440 | tf_op jit(solution)/shard_map/all_gather | solution.py:1019
  161.8 2.0 copy-start.5
  161.8 2.0 collective-permute-start.11
  163.8 0.8 copy-start.12
  171.5 14.2 %all-to-all-start.6 = ((bf16[8,16,2048]{2,1,0:T(8,128)(2,1)}), bf16[8,16,2048]{2,1,0:T(8,128)(2,1)S(1)}, u32[]{:S(2)}, u32[]{:S(2)}) async-start(bf16[8,16,2048]{2,1,0:T(8,128)(2,1)} %bitcast.53), calls=%async_computation.6 | async-start | bytes 1048576 | tf_op jit(solution)/shard_map/all_to_all | solution.py:907
  182.0 53.1 %collective-permute-start.19 = (bf16[2,3,128,1024]{3,2,1,0:T(8,128)(2,1)}, bf16[2,3,128,1024]{3,2,1,0:T(8,128)(2,1)}, u32[]{:S(2)}, u32[]{:S(2)}) collective-permute-start(bf16[2,3,128,1024]{3,2,1,0:T(8,128)(2,1)} %get-tuple-element.102), channel_id=1, source_target_pairs={{0,8},{8,0},{1,9},{9,1},{2,10},{10,2},{3,11},{11,3},{4,12},{12,4},... | collective-permute-start | bytes 4718600 | tf_op jit(solution)/shard_map/ppermute | solution.py:916
  186.5 3.9 %copy-start.26 = (bf16[128,1536]{1,0:T(8,128)(2,1)S(1)}, bf16[128,1536]{1,0:T(8,128)(2,1)}, u32[]{:S(2)}) copy-start(bf16[128,1536]{1,0:T(8,128)(2,1)} %get-tuple-element.95) | copy-start | bytes 1179652
  186.5 4.5 %copy-start.25 = (bf16[128,1536]{1,0:T(8,128)(2,1)S(1)}, bf16[128,1536]{1,0:T(8,128)(2,1)}, u32[]{:S(2)}) copy-start(bf16[128,1536]{1,0:T(8,128)(2,1)} %get-tuple-element.96) | copy-start | bytes 1179652
  186.5 6.6 %copy-start.24 = (bf16[128,1536]{1,0:T(8,128)(2,1)S(1)}, bf16[128,1536]{1,0:T(8,128)(2,1)}, u32[]{:S(2)}) copy-start(bf16[128,1536]{1,0:T(8,128)(2,1)} %get-tuple-element.97) | copy-start | bytes 1179652
  190.4 3.9 %collective-permute-start.15 = (f32[9,16,128]{2,1,0:T(8,128)}, f32[9,16,128]{2,1,0:T(8,128)S(1)}, u32[]{:S(2)}, u32[]{:S(2)}) collective-permute-start(f32[9,16,128]{2,1,0:T(8,128)} %get-tuple-element.99), channel_id=1, source_target_pairs={{0,8},{8,0},{1,9},{9,1},{2,10},{10,2},{3,11},{11,3},{4,12},{12,4},... | collective-permute-start | bytes 221192 | tf_op jit(solution)/shard_map/ppermute | solution.py:916
  190.4 21.2 %collective-permute-start.12 = (bf16[128,1536]{1,0:T(8,128)(2,1)S(1)}, bf16[128,1536]{1,0:T(8,128)(2,1)S(1)}, u32[]{:S(2)}, u32[]{:S(2)}) collective-permute-start(bf16[128,1536]{1,0:T(8,128)(2,1)S(1)} %copy-done.26), channel_id=1, source_target_pairs={{0,32},{32,64},{64,96},{96,0},{1,33},{33,65},{65,97},{97,1},{2,34}... | collective-permute-start | bytes 1179656 | tf_op jit(solution)/shard_map/ppermute | solution.py:922
  191.0 20.5 %collective-permute-start.13 = (bf16[128,1536]{1,0:T(8,128)(2,1)S(1)}, bf16[128,1536]{1,0:T(8,128)(2,1)S(1)}, u32[]{:S(2)}, u32[]{:S(2)}) collective-permute-start(bf16[128,1536]{1,0:T(8,128)(2,1)S(1)} %copy-done.25), channel_id=1, source_target_pairs={{0,64},{32,96},{64,0},{96,32},{1,65},{33,97},{65,1},{97,33},{2,66}... | collective-permute-start | bytes 1179656 | tf_op jit(solution)/shard_map/ppermute | solution.py:922
  193.0 19.1 %collective-permute-start.14 = (bf16[128,1536]{1,0:T(8,128)(2,1)S(1)}, bf16[128,1536]{1,0:T(8,128)(2,1)S(1)}, u32[]{:S(2)}, u32[]{:S(2)}) collective-permute-start(bf16[128,1536]{1,0:T(8,128)(2,1)S(1)} %copy-done.24), channel_id=1, source_target_pairs={{0,96},{32,0},{64,32},{96,64},{1,97},{33,1},{65,33},{97,65},{2,98}... | collective-permute-start | bytes 1179656 | tf_op jit(solution)/shard_map/ppermute | solution.py:922
  195.2 5.9 %collective-permute-start.16 = (f32[5,16,128]{2,1,0:T(8,128)S(1)}, f32[5,16,128]{2,1,0:T(8,128)S(1)}, u32[]{:S(2)}, u32[]{:S(2)}) collective-permute-start(f32[5,16,128]{2,1,0:T(8,128)S(1)} %pad_maximum_fusion), channel_id=1, source_target_pairs={{0,16},{16,0},{1,17},{17,1},{2,18},{18,2},{3,19},{19,3},{4,20},{20... | collective-permute-start | bytes 122888 | tf_op jit(solution)/shard_map/ppermute | solution.py:916
  196.8 48.9 %all-to-all-start.7 = ((bf16[8,64,2048]{2,1,0:T(8,128)(2,1)}), bf16[8,64,2048]{2,1,0:T(8,128)(2,1)}, u32[]{:S(2)}, u32[]{:S(2)}) async-start(bf16[8,64,2048]{2,1,0:T(8,128)(2,1)} %get-tuple-element.93), calls=%async_computation.7 | async-start | bytes 4194304 | tf_op jit(solution)/shard_map/all_to_all | solution.py:907
  201.7 15.1 %copy-start.23 = (f32[5,16,128]{2,1,0:T(8,128)S(1)}, f32[5,16,128]{2,1,0:T(8,128)}, u32[]{:S(2)}) copy-start(f32[5,16,128]{2,1,0:T(8,128)} %fusion.2.refs_12_) | copy-start | bytes 122884
  211.5 0.9 copy-start.9
  216.7 15.4 %collective-permute-start.17 = (bf16[2,4,128,256]{3,2,1,0:T(8,128)(2,1)}, bf16[2,4,128,256]{3,2,1,0:T(8,128)(2,1)}, u32[]{:S(2)}, u32[]{:S(2)}) collective-permute-start(bf16[2,4,128,256]{3,2,1,0:T(8,128)(2,1)} %get-tuple-element.101), channel_id=1, source_target_pairs={{0,8},{8,0},{1,9},{9,1},{2,10},{10,2},{3,11},{11,3},{4,12},{12,4},... | collective-permute-start | bytes 1572872 | tf_op jit(solution)/shard_map/ppermute | solution.py:916
  216.9 5.0 %collective-permute-start.21 = (f32[2,16,128]{2,1,0:T(8,128)S(1)}, f32[2,16,128]{2,1,0:T(8,128)S(1)}, u32[]{:S(2)}, u32[]{:S(2)}) collective-permute-start(f32[2,16,128]{2,1,0:T(8,128)S(1)} %get-tuple-element.141), channel_id=1, source_target_pairs={{0,32},{32,64},{64,96},{96,0},{1,33},{33,65},{65,97},{97,1},{2,34}... | collective-permute-start | bytes 49160 | tf_op jit(solution)/shard_map/ppermute | solution.py:922
  217.6 5.4 %collective-permute-start.22 = (f32[2,16,128]{2,1,0:T(8,128)S(1)}, f32[2,16,128]{2,1,0:T(8,128)S(1)}, u32[]{:S(2)}, u32[]{:S(2)}) collective-permute-start(f32[2,16,128]{2,1,0:T(8,128)S(1)} %get-tuple-element.142), channel_id=1, source_target_pairs={{0,64},{32,96},{64,0},{96,32},{1,65},{33,97},{65,1},{97,33},{2,66}... | collective-permute-start | bytes 49160 | tf_op jit(solution)/shard_map/ppermute | solution.py:922
  221.1 3.7 %collective-permute-start.23 = (f32[2,16,128]{2,1,0:T(8,128)S(1)}, f32[2,16,128]{2,1,0:T(8,128)S(1)}, u32[]{:S(2)}, u32[]{:S(2)}) collective-permute-start(f32[2,16,128]{2,1,0:T(8,128)S(1)} %get-tuple-element.143), channel_id=1, source_target_pairs={{0,96},{32,0},{64,32},{96,64},{1,97},{33,1},{65,33},{97,65},{2,98}... | collective-permute-start | bytes 49160 | tf_op jit(solution)/shard_map/ppermute | solution.py:922
  224.9 3.7 %collective-permute-start.24 = (f32[2,16,128]{2,1,0:T(8,128)S(1)}, f32[2,16,128]{2,1,0:T(8,128)S(1)}, u32[]{:S(2)}, u32[]{:S(2)}) collective-permute-start(f32[2,16,128]{2,1,0:T(8,128)S(1)} %fusion.5), channel_id=1, source_target_pairs={{0,4},{4,0},{1,5},{5,1},{2,6},{6,2},{3,7},{7,3},{8,12},{12,8},{9,1... | collective-permute-start | bytes 49160 | tf_op jit(solution)/shard_map/ppermute | solution.py:975
  225.4 9.7 %copy-start = (f32[2,3,128,1024]{3,2,1,0:T(8,128)S(1)}, f32[2,3,128,1024]{3,2,1,0:T(8,128)}, u32[]{:S(2)}) copy-start(f32[2,3,128,1024]{3,2,1,0:T(8,128)} %get-tuple-element.91.refs_9_) | copy-start | bytes 9437188
  228.6 10.7 %collective-permute-start.25 = (f32[2,16,128]{2,1,0:T(8,128)S(1)}, f32[2,16,128]{2,1,0:T(8,128)S(1)}, u32[]{:S(2)}, u32[]{:S(2)}) collective-permute-start(f32[2,16,128]{2,1,0:T(8,128)S(1)} %add.126), channel_id=1, source_target_pairs={{0,1},{1,2},{2,3},{3,0},{4,5},{5,6},{6,7},{7,4},{8,9},{9,10},{10,1... | collective-permute-start | bytes 49160 | tf_op jit(solution)/shard_map/ppermute | solution.py:975
  229.4 10.0 %collective-permute-start.26 = (f32[2,16,128]{2,1,0:T(8,128)S(1)}, f32[2,16,128]{2,1,0:T(8,128)S(1)}, u32[]{:S(2)}, u32[]{:S(2)}) collective-permute-start(f32[2,16,128]{2,1,0:T(8,128)S(1)} %add.126), channel_id=1, source_target_pairs={{0,2},{1,3},{2,0},{3,1},{4,6},{5,7},{6,4},{7,5},{8,10},{9,11},{10,... | collective-permute-start | bytes 49160 | tf_op jit(solution)/shard_map/ppermute | solution.py:975
  231.2 8.1 %collective-permute-start.27 = (f32[2,16,128]{2,1,0:T(8,128)S(1)}, f32[2,16,128]{2,1,0:T(8,128)S(1)}, u32[]{:S(2)}, u32[]{:S(2)}) collective-permute-start(f32[2,16,128]{2,1,0:T(8,128)S(1)} %add.126), channel_id=1, source_target_pairs={{0,3},{1,0},{2,1},{3,2},{4,7},{5,4},{6,5},{7,6},{8,11},{9,8},{10,9... | collective-permute-start | bytes 49160 | tf_op jit(solution)/shard_map/ppermute | solution.py:975
  232.1 11.0 %copy-start.11 = (f32[2,4,128,256]{3,2,1,0:T(8,128)S(1)}, f32[2,4,128,256]{3,2,1,0:T(8,128)}, u32[]{:S(2)}) copy-start(f32[2,4,128,256]{3,2,1,0:T(8,128)} %get-tuple-element.100) | copy-start | bytes 3145732
  233.4 9.7 %collective-permute-start.18 = (bf16[4,128,256]{2,1,0:T(8,128)(2,1)S(1)}, bf16[4,128,256]{2,1,0:T(8,128)(2,1)S(1)}, u32[]{:S(2)}, u32[]{:S(2)}) collective-permute-start(bf16[4,128,256]{2,1,0:T(8,128)(2,1)S(1)} %fusion.1), channel_id=1, source_target_pairs={{0,16},{16,0},{1,17},{17,1},{2,18},{18,2},{3,19},{19,3},{4,20},{20... | collective-permute-start | bytes 786440 | tf_op jit(solution)/shard_map/ppermute | solution.py:916
  237.4 21.6 %collective-permute-start.20 = (bf16[3,128,1024]{2,1,0:T(8,128)(2,1)}, bf16[3,128,1024]{2,1,0:T(8,128)(2,1)}, u32[]{:S(2)}, u32[]{:S(2)}) collective-permute-start(bf16[3,128,1024]{2,1,0:T(8,128)(2,1)} %fusion), channel_id=1, source_target_pairs={{0,16},{16,0},{1,17},{17,1},{2,18},{18,2},{3,19},{19,3},{4,20},{20... | collective-permute-start | bytes 2359304 | tf_op jit(solution)/shard_map/ppermute | solution.py:916
  (8 other events, 5.7 us)
Sparse Core Ops, SparseCore 0:
  48.7 43.1 all-gather.6
  96.4 44.9 all-gather.10
  149.1 27.1 all-gather.8

commit v3 on v2

--- a/solution.py
+++ b/solution.py
@@ -1015,7 +1015,6 @@
     gb1 = exchange(gb1, TP).reshape(rows, width)
     y_two = along_z(xy[nz:])
     do, gq = query_back(placement, gb1, w_output, q, kv, log, same, other, trig, (pair, *y_two[1:],))
-    own_pair = pair
     pair = lax.all_gather(pin(pair, gb1), "x", axis=0)
     tiles = w_gate.shape[1] // FEED_TILE
     do_same = exchange(do, ("z", "yh"))
@@ -1027,10 +1026,10 @@
     ff_keep, ff_give = weight_part(
         ((x_two, 0), (y_two, 0)), acts, tiles, (0, 0, 1), FEED_TILE, "feed_weights", 8, (part_three,)
     )
-    ship = along_z(ship)
     gt, mix_keep, mix_give = last(
         t, mix_static, scatter_parts(part_three, TP), base, streams, c1, mt, dm, ds, (ff_keep,)
     )
+    ship = along_z([pin(v, mix_keep) for v in ship])
     ff_keep, ff_give = over_core(ff_keep, swap(ff_give, "core"))
     ff_got = swap(ff_give, "yh")
     ff = ff_keep + ff_got.astype(F32)
@@ -1043,18 +1042,16 @@
         return jnp.concatenate([lax.dynamic_slice_in_dim(v, at * nz, nz, 0), v[2 * nz :]], 0)
 
     v = half(yh) + swap(half(1 - yh), "yh")
-    mix_mid = v
 
     def mine(at):
         return jnp.stack([pick(v, lax.rem(at, nz)), v[nz]])
 
     v = sum(along_z([mine(z + i) for i in range(nz)]))
-    mix_high = v
     v = to_each(to_each(v, "yl"), "x")
     grad_dynamic = jnp.transpose(v[0].reshape(2, 8, -1)[:, :6], (0, 2, 1))
     grad_static = v[1].reshape(2, 8, 128)[:, :4, :6]
     keep, give = weight_part(
-        ((ship, 4), (x_one, 0)), ship, 1, (0, 1, 1, 1), 256, "tail_weights", 4, (mix_mid,)
+        ((ship, 4), (x_one, 0)), ship, 1, (0, 1, 1, 1), 256, "tail_weights", 4, (mix_low,)
     )
     keep, give = over_core(keep, swap(give, "core"))
     tail = keep + swap(give, "yh").astype(F32)

time: 270 us -> 269 us (level)
    unnamed x75 -> x71, local copies, waits for them, and re-layouts: 8.71 us -> 8.66 us
  transfers between devices with their start and end apart: 36 -> 36, of which waited for: 20 -> 21; matrix products, arithmetic and copies ran while one was open for 4% -> 3% of each run, Pallas kernels for 20% -> 20%
where the time goes in v3:
time: 269 us; the launch traced here: 268 us
  Pallas kernels  66.8 us (25%)
  waiting for transfers between devices  61.3 us (23%)
  blocking collectives  55.3 us (21%)
  starting transfers between devices  51.9 us (19%)
  between operations  14.1 us (5%)
  local copies, waits for them, and re-layouts  11.9 us (4%)
  other arithmetic  6.38 us (2%)
    all_to_all x3, blocking collectives, exchange(): return lax.all_to_all(blocks, axes, 0, 0, tiled=True)  55.3 us
    ppermute x15, waiting for transfers between devices, along_z(): lax.ppermute(pieces[i], 'z', [(a, (a + i) % n) for a in range(n)])  38.9 us
    ppermute x15, starting transfers between devices, along_z(): lax.ppermute(pieces[i], 'z', [(a, (a + i) % n) for a in range(n)])  20.3 us
    all_to_all x5, starting transfers between devices, exchange(): return lax.all_to_all(blocks, axes, 0, 0, tiled=True)  19.6 us
    ppermute x9, waiting for transfers between devices, swap(): return lax.ppermute(v, axis, [(0, 1), (1, 0)])  17.3 us
    pallas_call x1, Pallas kernels, feed(): pl.pallas_call(feed_kernel, grid=(hidden // tile,), in_specs=[whole(pay.s...  13.2 us
    pallas_call x3, Pallas kernels, token_call(): pl.pallas_call(body, grid_spec=pltpu.PrefetchScalarGridSpec(num_scalar_pr...  12.9 us
    pallas_call x2, Pallas kernels, weight_part(): pl.pallas_call(functools.partial(weight_kernel, picks, tile, count, gathe...  10.7 us
  transfers between devices with their start and end apart: 36, of which 21 were waited for; matrix products, arithmetic and copies ran while one was open for 3% of the time, Pallas kernels for 20%

profile of v3, /device:TPU:0, one launch (start us, length us, event | category | flops | bytes accessed | tf_op | source)
XLA Modules:
  0.0 267.5 jit_solution(9058240507763064774)
XLA Ops:
  7.2 8.0 %first.1 = (f32[512,128]{1,0:T(8,128)}, bf16[128,256]{1,0:T(8,128)(2,1)}, bf16[8,128,512]{2,1,0:T(8,128)(2,1)}, f32[2,128,128]{2,1,0:T(8,128)}, bf16[128,512]{1,...) custom-call(s32[16]{0:T(128)} %place_ref.7, f32[2,4,6]{2,1,0:T(4,128)} %refs_1_.5, ...), custom_call_target="tpu_custom_call" | custom-call | bytes 36900000 | tf_op jit(solution)/shard_map/first/pallas_call | solution.py:226
  15.2 25.2 %all_to_all.40.same_ref = bf16[8,128,512]{2,1,0:T(8,128)(2,1)S(1)} all-to-all(bf16[8,128,512]{2,1,0:T(8,128)(2,1)} %get-tuple-element.58.own_ref), channel_id=1, replica_groups=mesh['z'=4,'yh'=2,'core'=2,'yl'=2,'x'=4] {'z','yh'}, dimensions={0} | all-to-all | bytes 2097152 | tf_op jit(solution)/shard_map/all_to_all | solution.py:907
  40.4 2.7 collective-permute-done.other_ref
  43.1 1.0 copy-done.3
  44.1 4.5 %attend.1 = (bf16[128,256]{1,0:T(8,128)(2,1)}, f32[1,256]{1,0:T(1,128)}, bf16[128,2048]{1,0:T(8,128)(2,1)}, bf16[128,256]{1,0:T(8,128)(2,1)}) custom-call(s32[16]{0:T(128)} %place_ref.7, bf16[128,256]{1,0:T(8,128)(2,1)} %get-tuple-element.57.q_ref, bf16[8,128,512]{2,1,0:T(8,128)(2,1)} %get-tuple-element.58.own_ref, bf16[8,128,512]{2,1,0:T(8,128)(2,1)} %copy-done.1, ...), custom_call_target="tpu_custom_call" | custom-call | bytes 16605000 | tf_op jit(solution)/shard_map/attend/pallas_call | solution.py:321
  48.6 4.5 %all-to-all-start.1 = ((bf16[8,16,2048]{2,1,0:T(8,128)(2,1)}), bf16[8,16,2048]{2,1,0:T(8,128)(2,1)S(1)}, u32[]{:S(2)}, u32[]{:S(2)}) async-start(bf16[8,16,2048]{2,1,0:T(8,128)(2,1)} %bitcast.60), calls=%async_computation.1 | async-start | bytes 1048576 | tf_op jit(solution)/shard_map/all_to_all | solution.py:907
  53.4 2.1 collective-permute-start.2
  55.4 1.5 collective-permute-start.3
  57.0 5.9 %collective-permute-done.1.refs_6_.refs_5_ = bf16[128,512]{1,0:T(8,128)(2,1)S(1)} collective-permute-done((bf16[128,512]{1,0:T(8,128)(2,1)S(1)}, bf16[128,512]{1,0:T(8,128)(2,1)S(1)}, u32[]{:S(2)}, u32[]{:S(2)}) %collective-permute-start.1) | collective-permute-done | bytes 131104 | tf_op jit(solution)/shard_map/ppermute | solution.py:922
  64.4 3.3 %middle.1 = (f32[4,16,2048]{2,1,0:T(8,128)}, f32[16,2048]{1,0:T(8,128)}, f32[4,16,128]{2,1,0:T(8,128)}, bf16[8,16,2176]{2,1,0:T(8,128)(2,1)}) custom-call(s32[1]{0:T(128)} %bitcast.refs_0_.t_ref, f32[2,4,6]{2,1,0:T(4,128)} %refs_1_.5, bf16[8,16,2048]{2,1,0:T(8,128)(2,1)} %copy-done.8, bf16[128,4,2048]{2,1,0:T(4,128)(2,1)} %refs_4_.1, ...), custom_call_target="tpu_custom_call" | custom-call | bytes 14760000 | tf_op jit(solution)/shard_map/middle/pallas_call | solution.py:380
  67.7 15.3 %all_to_all.41 = bf16[8,16,2176]{2,1,0:T(8,128)(2,1)} all-to-all(bf16[8,16,2176]{2,1,0:T(8,128)(2,1)} %get-tuple-element.64), channel_id=1, replica_groups=mesh['z'=4,'yh'=2,'core'=2,'yl'=2,'x'=4] {'yl','x'}, dimensions={0} | all-to-all | bytes 1114112 | tf_op jit(solution)/shard_map/all_to_all | solution.py:907
  83.0 13.2 %feed.1 = (bf16[128,512]{1,0:T(8,128)(2,1)}, bf16[128,512]{1,0:T(8,128)(2,1)}, bf16[128,512]{1,0:T(8,128)(2,1)}, bf16[128,512]{1,0:T(8,128)(2,1)}, bf16[128,512]...) custom-call(bf16[128,2176]{1,0:T(8,128)(2,1)} %bitcast.52, ...), custom_call_target="tpu_custom_call" | custom-call | bytes 51660000 | tf_op jit(solution)/shard_map/feed/pallas_call | solution.py:488
  96.3 3.7 %all-to-all-start.3 = ((bf16[8,16,4096]{2,1,0:T(8,128)(2,1)}), bf16[8,16,4096]{2,1,0:T(8,128)(2,1)S(1)}, u32[]{:S(2)}, u32[]{:S(2)}) async-start(bf16[8,16,4096]{2,1,0:T(8,128)(2,1)} %bitcast.59), calls=%async_computation.3 | async-start | bytes 2097152 | tf_op jit(solution)/shard_map/all_to_all | solution.py:907
  100.6 4.6 %collective-permute-start.5 = (bf16[128,512]{1,0:T(8,128)(2,1)S(1)}, bf16[128,512]{1,0:T(8,128)(2,1)S(1)}, u32[]{:S(2)}, u32[]{:S(2)}) collective-permute-start(bf16[128,512]{1,0:T(8,128)(2,1)S(1)} %copy-done.32), channel_id=1, source_target_pairs={{0,64},{32,96},{64,0},{96,32},{1,65},{33,97},{65,1},{97,33},{2,66}... | collective-permute-start | bytes 393224 | tf_op jit(solution)/shard_map/ppermute | solution.py:922
  105.3 2.9 %collective-permute-done.4.refs_11_.refs_1_ = bf16[128,512]{1,0:T(8,128)(2,1)S(1)} collective-permute-done((bf16[128,512]{1,0:T(8,128)(2,1)S(1)}, bf16[128,512]{1,0:T(8,128)(2,1)S(1)}, u32[]{:S(2)}, u32[]{:S(2)}) %collective-permute-start.4) | collective-permute-done | bytes 131104 | tf_op jit(solution)/shard_map/ppermute | solution.py:922
  108.1 4.2 %collective-permute-done.5.refs_12_.refs_2_ = bf16[128,512]{1,0:T(8,128)(2,1)S(1)} collective-permute-done((bf16[128,512]{1,0:T(8,128)(2,1)S(1)}, bf16[128,512]{1,0:T(8,128)(2,1)S(1)}, u32[]{:S(2)}, u32[]{:S(2)}) %collective-permute-start.5) | collective-permute-done | bytes 131104 | tf_op jit(solution)/shard_map/ppermute | solution.py:922
  112.3 1.7 collective-permute-done.6.refs_13_.refs_3_
  115.0 5.8 %turn.1 = (bf16[64,2048]{1,0:T(8,128)(2,1)}, bf16[2,64,2048]{2,1,0:T(8,128)(2,1)}, f32[4,16,2048]{2,1,0:T(8,128)}, bf16[8,16,2048]{2,1,0:T(8,128)(2,1)}, f32[2,8,2048]{2,1,0:T(8,128)}, /*index=5*/f32[2,8,128]{2,1,0:T(8,128)}) custom-call(s32[1]{0:T(128)} %bitcast.refs_0_.t_ref, f32[2,4,6]{2,1,0:T(4,128)} %refs_1_.5, bf16[8,16,4096]{2,1,0:T(8,128)(2,1)} %copy-done.4, ...), custom_call_target="tpu_custom_call" | custom-call | bytes 14760000 | tf_op jit(solution)/shard_map/turn/pallas_call | solution.py:380
  120.8 2.1 collective-permute-start.7
  122.9 2.8 %collective-permute-start.10 = (bf16[128,512]{1,0:T(8,128)(2,1)S(1)}, bf16[128,512]{1,0:T(8,128)(2,1)S(1)}, u32[]{:S(2)}, u32[]{:S(2)}) collective-permute-start(bf16[128,512]{1,0:T(8,128)(2,1)S(1)} %copy-done.27), channel_id=1, source_target_pairs={{0,96},{32,0},{64,32},{96,64},{1,97},{33,1},{65,33},{97,65},{2,98}... | collective-permute-start | bytes 393224 | tf_op jit(solution)/shard_map/ppermute | solution.py:922
  125.7 1.5 collective-permute-start.9
  127.2 3.5 %all-to-all-start.4 = ((bf16[8,16,2048]{2,1,0:T(8,128)(2,1)}), bf16[8,16,2048]{2,1,0:T(8,128)(2,1)S(1)}, u32[]{:S(2)}, u32[]{:S(2)}) async-start(bf16[8,16,2048]{2,1,0:T(8,128)(2,1)} %get-tuple-element.75), calls=%async_computation.4 | async-start | bytes 1048576 | tf_op jit(solution)/shard_map/all_to_all | solution.py:907
  131.5 2.1 collective-permute-done.10.refs_3_.refs_7_
  133.6 3.9 %collective-permute-done.8.refs_1_.refs_5_ = bf16[128,512]{1,0:T(8,128)(2,1)S(1)} collective-permute-done((bf16[128,512]{1,0:T(8,128)(2,1)S(1)}, bf16[128,512]{1,0:T(8,128)(2,1)S(1)}, u32[]{:S(2)}, u32[]{:S(2)}) %collective-permute-start.8) | collective-permute-done | bytes 131104 | tf_op jit(solution)/shard_map/ppermute | solution.py:922
  137.5 1.9 collective-permute-done.9.refs_2_.refs_6_
  140.1 0.8 copy-done.2
  140.8 5.2 %query_back.1 = (bf16[8,144,256]{2,1,0:T(8,128)(2,1)}, bf16[128,256]{1,0:T(8,128)(2,1)}) custom-call(s32[16]{0:T(128)} %place_ref.7, bf16[128,2048]{1,0:T(8,128)(2,1)} %bitcast.46, bf16[256,2048]{1,0:T(8,128)(2,1)} %wo_ref.3, bf16[128,256]{1,0:T(8,128)(2,1)} %get-tuple-element.69.q_ref, bf16[8,128,512]{2,1,0:T(8,128)(2,1)} %get-tuple-element.58.own_ref, ...), custom_call_target="tpu_custom_call" | custom-call | bytes 20295000 | tf_op jit(solution)/shard_map/query_back/pallas_call | solution.py:678
  147.1 14.8 %all_to_all.42.same_ref = bf16[8,144,256]{2,1,0:T(8,128)(2,1)S(1)} all-to-all(bf16[8,144,256]{2,1,0:T(8,128)(2,1)S(1)} %copy-done.15), channel_id=1, replica_groups=mesh['z'=4,'yh'=2,'core'=2,'yl'=2,'x'=4] {'z','yh'}, dimensions={0} | all-to-all | bytes 1179648 | tf_op jit(solution)/shard_map/all_to_all | solution.py:907
  161.8 2.0 collective-permute-done.11.other_ref
  163.8 0.8 copy-done.14
  164.7 6.9 %key_back.1 = (bf16[128,2048]{1,0:T(8,128)(2,1)}, bf16[128,1536]{1,0:T(8,128)(2,1)}, bf16[128,1536]{1,0:T(8,128)(2,1)}, bf16[128,1536]{1,0:T(8,128)(2,1)}, bf16[128,1536]{1,0:T(8,128)(2,1)}) custom-call(s32[16]{0:T(128)} %place_ref.7, bf16[8,128,512]{2,1,0:T(8,128)(2,1)} %get-tuple-element.58.own_ref, bf16[16,128,256]{2,1,0:T(8,128)(2,1)} %bitcast.50, ...), custom_call_target="tpu_custom_call" | custom-call | bytes 23985000 | tf_op jit(solution)/shard_map/key_back/pallas_call | solution.py:752
  171.5 3.5 %all-to-all-start.6 = ((bf16[8,16,2048]{2,1,0:T(8,128)(2,1)}), bf16[8,16,2048]{2,1,0:T(8,128)(2,1)S(1)}, u32[]{:S(2)}, u32[]{:S(2)}) async-start(bf16[8,16,2048]{2,1,0:T(8,128)(2,1)} %bitcast.53), calls=%async_computation.6 | async-start | bytes 1048576 | tf_op jit(solution)/shard_map/all_to_all | solution.py:907
  175.1 6.9 %feed_weights.1 = (f32[2,3,128,1024]{3,2,1,0:T(8,128)}, bf16[2,3,128,1024]{3,2,1,0:T(8,128)(2,1)}) custom-call(bf16[128,512]{1,0:T(8,128)(2,1)} %get-tuple-element.88.refs_0_, bf16[128,512]{1,0:T(8,128)(2,1)} %copy-done.16, bf16[128,512]{1,0:T(8,128)(2,1)} %copy-done.17, bf16[128,512]{1,0:T(8,128)(2,1)} %copy-done.18, ...), custom_call_target="tpu_custom_call" | custom-call | bytes 29520000 | tf_op jit(solution)/shard_map/feed_weights/pallas_call | solution.py:893
  182.4 3.3 %all-to-all-done.6.refs_2_ = bf16[8,16,2048]{2,1,0:T(8,128)(2,1)S(1)} async-done(((bf16[8,16,2048]{2,1,0:T(8,128)(2,1)}), bf16[8,16,2048]{2,1,0:T(8,128)(2,1)S(1)}, u32[]{:S(2)}, u32[]{:S(2)}) %all-to-all-start.6) | async-done | bytes 524320 | tf_op jit(solution)/shard_map/all_to_all | solution.py:907
  185.7 0.8 copy-done.7
  186.5 3.8 %last.1 = (bf16[8,64,2048]{2,1,0:T(8,128)(2,1)}, f32[9,16,128]{2,1,0:T(8,128)}, f32[9,16,128]{2,1,0:T(8,128)}) custom-call(s32[1]{0:T(128)} %bitcast.refs_0_.t_ref, f32[2,4,6]{2,1,0:T(4,128)} %refs_1_.5, bf16[8,16,2048]{2,1,0:T(8,128)(2,1)} %copy-done.7, f32[4,16,2048]{2,1,0:T(8,128)} %get-tuple-element.85.refs_3_, bf16[128,4,2048]{2,1,0:T(4,128)(2,1)} %refs_4_.1, ...), custom_call_target="tpu_custom_call" | custom-call | bytes 14760000 | tf_op jit(solution)/shard_map/last/pallas_call | solution.py:380
  190.3 1.2 collective-permute-start.14
  191.5 1.5 collective-permute-start.13
  193.1 1.5 collective-permute-start.20
  194.6 4.4 %all-to-all-start.7 = ((bf16[8,64,2048]{2,1,0:T(8,128)(2,1)}), bf16[8,64,2048]{2,1,0:T(8,128)(2,1)}, u32[]{:S(2)}, u32[]{:S(2)}) async-start(bf16[8,64,2048]{2,1,0:T(8,128)(2,1)} %get-tuple-element.93), calls=%async_computation.7 | async-start | bytes 4194304 | tf_op jit(solution)/shard_map/all_to_all | solution.py:907
  199.0 3.5 %collective-permute-done.14.refs_3_.refs_11_ = bf16[128,1536]{1,0:T(8,128)(2,1)S(1)} collective-permute-done((bf16[128,1536]{1,0:T(8,128)(2,1)}, bf16[128,1536]{1,0:T(8,128)(2,1)S(1)}, u32[]{:S(2)}, u32[]{:S(2)}) %collective-permute-start.14) | collective-permute-done | bytes 393248 | tf_op jit(solution)/shard_map/ppermute | solution.py:922
  202.5 2.7 %collective-permute-done.13.refs_2_.refs_10_ = bf16[128,1536]{1,0:T(8,128)(2,1)S(1)} collective-permute-done((bf16[128,1536]{1,0:T(8,128)(2,1)}, bf16[128,1536]{1,0:T(8,128)(2,1)S(1)}, u32[]{:S(2)}, u32[]{:S(2)}) %collective-permute-start.13) | collective-permute-done | bytes 393248 | tf_op jit(solution)/shard_map/ppermute | solution.py:922
  205.2 7.6 %collective-permute-done.12.refs_1_.refs_9_ = bf16[128,1536]{1,0:T(8,128)(2,1)S(1)} collective-permute-done((bf16[128,1536]{1,0:T(8,128)(2,1)}, bf16[128,1536]{1,0:T(8,128)(2,1)S(1)}, u32[]{:S(2)}, u32[]{:S(2)}) %collective-permute-start.12) | collective-permute-done | bytes 393248 | tf_op jit(solution)/shard_map/ppermute | solution.py:922
  213.6 3.8 %tail_weights.1 = (f32[2,4,128,256]{3,2,1,0:T(8,128)}, bf16[2,4,128,256]{3,2,1,0:T(8,128)(2,1)}) custom-call(bf16[128,1536]{1,0:T(8,128)(2,1)} %pin.6.refs_0_.refs_8_, bf16[128,1536]{1,0:T(8,128)(2,1)} %copy-done.11, bf16[128,1536]{1,0:T(8,128)(2,1)} %copy-done.10, bf16[128,1536]{1,0:T(8,128)(2,1)} %copy-done.9, bf16[128,512]{1,0:T(8,128)(2,1)} %get-tuple-element.98.refs_4_, ...), custom_call_target="tpu_custom_call" | custom-call | bytes 14760000 | tf_op jit(solution)/shard_map/tail_weights/pallas_call | solution.py:893
  217.7 2.0 collective-permute-start.22
  219.6 2.2 collective-permute-start.23
  221.8 0.8 collective-permute-done.21
  224.2 2.8 %rows.2.refs_0_ = bf16[128,4,2048]{2,1,0:T(4,128)(2,1)} custom-call(s32[1]{0:T(128)} %bitcast.refs_0_.t_ref, bf16[4,2,64,2048]{3,2,1,0:T(8,128)(2,1)} %bitcast.54, f32[9,16,128]{2,1,0:T(8,128)} %get-tuple-element.92.refs_0_.refs_1_), custom_call_target="tpu_custom_call" | custom-call | bytes 9594000 | tf_op jit(solution)/shard_map/rows/pallas_call | solution.py:958
  227.4 0.8 collective-permute-start.25
  228.2 1.9 collective-permute-start.26
  230.0 0.9 collective-permute-start.27
  230.9 1.3 fusion.1
  232.2 1.7 collective-permute-start.17
  233.9 2.3 fusion
  236.2 1.9 collective-permute-start.19
  239.4 2.1 collective-permute-done.17
  241.5 1.0 bitcast_add_fusion.1
  242.5 0.8 slice_bitcast_fusion.3
  243.3 0.8 copy.33
  244.0 2.6 rows.3
  246.7 10.5 %collective-permute-done.19 = bf16[3,128,1024]{2,1,0:T(8,128)(2,1)} collective-permute-done((bf16[3,128,1024]{2,1,0:T(8,128)(2,1)}, bf16[3,128,1024]{2,1,0:T(8,128)(2,1)}, u32[]{:S(2)}, u32[]{:S(2)}) %collective-permute-start.19) | collective-permute-done | bytes 786464 | tf_op jit(solution)/shard_map/ppermute | solution.py:916
  257.2 1.7 bitcast_add_fusion
  258.9 1.1 slice_bitcast_fusion
  260.0 1.0 copy.34
  (121 shorter events, 10.7 us)
Async XLA Ops:
  7.2 106.9 %all-gather.7.cloned.1.call-start = ((), (), s32[]{:S(2)}) async-start(), calls=%async_computation.8 | async-start | bytes 1114112 | tf_op jit(solution)/shard_map/all_gather | solution.py:1002
  40.4 2.7 copy-start.1
  40.4 2.7 collective-permute-start
  43.1 1.0 copy-start.3
  44.1 9.1 %copy-start.30 = (bf16[128,512]{1,0:T(8,128)(2,1)S(1)}, bf16[128,512]{1,0:T(8,128)(2,1)}, u32[]{:S(2)}) copy-start(bf16[128,512]{1,0:T(8,128)(2,1)} %get-tuple-element.61) | copy-start | bytes 393220
  44.1 9.3 %copy-start.29 = (bf16[128,512]{1,0:T(8,128)(2,1)S(1)}, bf16[128,512]{1,0:T(8,128)(2,1)}, u32[]{:S(2)}) copy-start(bf16[128,512]{1,0:T(8,128)(2,1)} %get-tuple-element.62) | copy-start | bytes 393220
  44.1 11.4 %copy-start.28 = (bf16[128,512]{1,0:T(8,128)(2,1)S(1)}, bf16[128,512]{1,0:T(8,128)(2,1)}, u32[]{:S(2)}) copy-start(bf16[128,512]{1,0:T(8,128)(2,1)} %get-tuple-element.63) | copy-start | bytes 393220
  48.6 15.0 %all-to-all-start.1 = ((bf16[8,16,2048]{2,1,0:T(8,128)(2,1)}), bf16[8,16,2048]{2,1,0:T(8,128)(2,1)S(1)}, u32[]{:S(2)}, u32[]{:S(2)}) async-start(bf16[8,16,2048]{2,1,0:T(8,128)(2,1)} %bitcast.60), calls=%async_computation.1 | async-start | bytes 1048576 | tf_op jit(solution)/shard_map/all_to_all | solution.py:907
  53.1 122.0 %all-gather.11.cloned.1.call-start = ((), (), s32[]{:S(2)}) async-start(), calls=%async_computation.10 | async-start | bytes 3932160 | tf_op jit(solution)/shard_map/all_gather | solution.py:1009
  53.2 9.7 %collective-permute-start.1 = (bf16[128,512]{1,0:T(8,128)(2,1)S(1)}, bf16[128,512]{1,0:T(8,128)(2,1)S(1)}, u32[]{:S(2)}, u32[]{:S(2)}) collective-permute-start(bf16[128,512]{1,0:T(8,128)(2,1)S(1)} %copy-done.30), channel_id=1, source_target_pairs={{0,32},{32,64},{64,96},{96,0},{1,33},{33,65},{65,97},{97,1},{2,34}... | collective-permute-start | bytes 393224 | tf_op jit(solution)/shard_map/ppermute | solution.py:922
  53.4 9.5 %collective-permute-start.2 = (bf16[128,512]{1,0:T(8,128)(2,1)S(1)}, bf16[128,512]{1,0:T(8,128)(2,1)S(1)}, u32[]{:S(2)}, u32[]{:S(2)}) collective-permute-start(bf16[128,512]{1,0:T(8,128)(2,1)S(1)} %copy-done.29), channel_id=1, source_target_pairs={{0,64},{32,96},{64,0},{96,32},{1,65},{33,97},{65,1},{97,33},{2,66}... | collective-permute-start | bytes 393224 | tf_op jit(solution)/shard_map/ppermute | solution.py:922
  55.4 8.1 %collective-permute-start.3 = (bf16[128,512]{1,0:T(8,128)(2,1)S(1)}, bf16[128,512]{1,0:T(8,128)(2,1)S(1)}, u32[]{:S(2)}, u32[]{:S(2)}) collective-permute-start(bf16[128,512]{1,0:T(8,128)(2,1)S(1)} %copy-done.28), channel_id=1, source_target_pairs={{0,96},{32,0},{64,32},{96,64},{1,97},{33,1},{65,33},{97,65},{2,98}... | collective-permute-start | bytes 393224 | tf_op jit(solution)/shard_map/ppermute | solution.py:922
  63.5 0.8 copy-start.8
  96.2 3.8 %copy-start.33 = (bf16[128,512]{1,0:T(8,128)(2,1)S(1)}, bf16[128,512]{1,0:T(8,128)(2,1)}, u32[]{:S(2)}) copy-start(bf16[128,512]{1,0:T(8,128)(2,1)} %get-tuple-element.70) | copy-start | bytes 393220
  96.2 4.4 %copy-start.32 = (bf16[128,512]{1,0:T(8,128)(2,1)S(1)}, bf16[128,512]{1,0:T(8,128)(2,1)}, u32[]{:S(2)}) copy-start(bf16[128,512]{1,0:T(8,128)(2,1)} %get-tuple-element.71) | copy-start | bytes 393220
  96.2 9.0 %copy-start.31 = (bf16[128,512]{1,0:T(8,128)(2,1)S(1)}, bf16[128,512]{1,0:T(8,128)(2,1)}, u32[]{:S(2)}) copy-start(bf16[128,512]{1,0:T(8,128)(2,1)} %get-tuple-element.72) | copy-start | bytes 393220
  96.3 17.8 %all-to-all-start.3 = ((bf16[8,16,4096]{2,1,0:T(8,128)(2,1)}), bf16[8,16,4096]{2,1,0:T(8,128)(2,1)S(1)}, u32[]{:S(2)}, u32[]{:S(2)}) async-start(bf16[8,16,4096]{2,1,0:T(8,128)(2,1)} %bitcast.59), calls=%async_computation.3 | async-start | bytes 2097152 | tf_op jit(solution)/shard_map/all_to_all | solution.py:907
  100.0 8.2 %collective-permute-start.4 = (bf16[128,512]{1,0:T(8,128)(2,1)S(1)}, bf16[128,512]{1,0:T(8,128)(2,1)S(1)}, u32[]{:S(2)}, u32[]{:S(2)}) collective-permute-start(bf16[128,512]{1,0:T(8,128)(2,1)S(1)} %copy-done.33), channel_id=1, source_target_pairs={{0,32},{32,64},{64,96},{96,0},{1,33},{33,65},{65,97},{97,1},{2,34}... | collective-permute-start | bytes 393224 | tf_op jit(solution)/shard_map/ppermute | solution.py:922
  100.6 11.7 %collective-permute-start.5 = (bf16[128,512]{1,0:T(8,128)(2,1)S(1)}, bf16[128,512]{1,0:T(8,128)(2,1)S(1)}, u32[]{:S(2)}, u32[]{:S(2)}) collective-permute-start(bf16[128,512]{1,0:T(8,128)(2,1)S(1)} %copy-done.32), channel_id=1, source_target_pairs={{0,64},{32,96},{64,0},{96,32},{1,65},{33,97},{65,1},{97,33},{2,66}... | collective-permute-start | bytes 393224 | tf_op jit(solution)/shard_map/ppermute | solution.py:922
  105.3 8.8 %collective-permute-start.6 = (bf16[128,512]{1,0:T(8,128)(2,1)S(1)}, bf16[128,512]{1,0:T(8,128)(2,1)S(1)}, u32[]{:S(2)}, u32[]{:S(2)}) collective-permute-start(bf16[128,512]{1,0:T(8,128)(2,1)S(1)} %copy-done.31), channel_id=1, source_target_pairs={{0,96},{32,0},{64,32},{96,64},{1,97},{33,1},{65,33},{97,65},{2,98}... | collective-permute-start | bytes 393224 | tf_op jit(solution)/shard_map/ppermute | solution.py:922
  108.1 5.9 %copy-start.16 = (bf16[128,512]{1,0:T(8,128)(2,1)}, bf16[128,512]{1,0:T(8,128)(2,1)S(1)}, u32[]{:S(2)}) copy-start(bf16[128,512]{1,0:T(8,128)(2,1)S(1)} %collective-permute-done.4.refs_11_.refs_1_) | copy-start | bytes 393220
  112.3 1.8 copy-start.17
  114.0 1.0 copy-start.4
  115.0 7.9 %copy-start.27 = (bf16[128,512]{1,0:T(8,128)(2,1)S(1)}, bf16[128,512]{1,0:T(8,128)(2,1)}, u32[]{:S(2)}) copy-start(bf16[128,512]{1,0:T(8,128)(2,1)} %get-tuple-element.80) | copy-start | bytes 393220
  115.0 10.7 %copy-start.26 = (bf16[128,512]{1,0:T(8,128)(2,1)S(1)}, bf16[128,512]{1,0:T(8,128)(2,1)}, u32[]{:S(2)}) copy-start(bf16[128,512]{1,0:T(8,128)(2,1)} %get-tuple-element.78) | copy-start | bytes 393220
  115.0 10.7 %copy-start.25 = (bf16[128,512]{1,0:T(8,128)(2,1)S(1)}, bf16[128,512]{1,0:T(8,128)(2,1)}, u32[]{:S(2)}) copy-start(bf16[128,512]{1,0:T(8,128)(2,1)} %get-tuple-element.79) | copy-start | bytes 393220
  120.8 9.9 %collective-permute-start.7 = (bf16[64,2048]{1,0:T(8,128)(2,1)}, bf16[64,2048]{1,0:T(8,128)(2,1)S(1)}, u32[]{:S(2)}, u32[]{:S(2)}) collective-permute-start(bf16[64,2048]{1,0:T(8,128)(2,1)} %get-tuple-element.74), channel_id=1, source_target_pairs={{0,4},{4,0},{1,5},{5,1},{2,6},{6,2},{3,7},{7,3},{8,12},{12,8},{9,1... | collective-permute-start | bytes 786440 | tf_op jit(solution)/shard_map/ppermute | solution.py:916
  122.9 10.7 %collective-permute-start.10 = (bf16[128,512]{1,0:T(8,128)(2,1)S(1)}, bf16[128,512]{1,0:T(8,128)(2,1)S(1)}, u32[]{:S(2)}, u32[]{:S(2)}) collective-permute-start(bf16[128,512]{1,0:T(8,128)(2,1)S(1)} %copy-done.27), channel_id=1, source_target_pairs={{0,96},{32,0},{64,32},{96,64},{1,97},{33,1},{65,33},{97,65},{2,98}... | collective-permute-start | bytes 393224 | tf_op jit(solution)/shard_map/ppermute | solution.py:922
  125.7 11.9 %collective-permute-start.8 = (bf16[128,512]{1,0:T(8,128)(2,1)S(1)}, bf16[128,512]{1,0:T(8,128)(2,1)S(1)}, u32[]{:S(2)}, u32[]{:S(2)}) collective-permute-start(bf16[128,512]{1,0:T(8,128)(2,1)S(1)} %copy-done.26), channel_id=1, source_target_pairs={{0,32},{32,64},{64,96},{96,0},{1,33},{33,65},{65,97},{97,1},{2,34}... | collective-permute-start | bytes 393224 | tf_op jit(solution)/shard_map/ppermute | solution.py:922
  125.7 13.7 %collective-permute-start.9 = (bf16[128,512]{1,0:T(8,128)(2,1)S(1)}, bf16[128,512]{1,0:T(8,128)(2,1)S(1)}, u32[]{:S(2)}, u32[]{:S(2)}) collective-permute-start(bf16[128,512]{1,0:T(8,128)(2,1)S(1)} %copy-done.25), channel_id=1, source_target_pairs={{0,64},{32,96},{64,0},{96,32},{1,65},{33,97},{65,1},{97,33},{2,66}... | collective-permute-start | bytes 393224 | tf_op jit(solution)/shard_map/ppermute | solution.py:922
  127.2 12.8 %all-to-all-start.4 = ((bf16[8,16,2048]{2,1,0:T(8,128)(2,1)}), bf16[8,16,2048]{2,1,0:T(8,128)(2,1)S(1)}, u32[]{:S(2)}, u32[]{:S(2)}) async-start(bf16[8,16,2048]{2,1,0:T(8,128)(2,1)} %get-tuple-element.75), calls=%async_computation.4 | async-start | bytes 1048576 | tf_op jit(solution)/shard_map/all_to_all | solution.py:907
  133.6 6.4 %copy-start.22 = (bf16[128,512]{1,0:T(8,128)(2,1)}, bf16[128,512]{1,0:T(8,128)(2,1)S(1)}, u32[]{:S(2)}) copy-start(bf16[128,512]{1,0:T(8,128)(2,1)S(1)} %collective-permute-done.10.refs_3_.refs_7_) | copy-start | bytes 393220
  137.5 2.5 copy-start.23
  140.0 0.8 copy-start.2
  146.0 1.1 copy-start.15
  146.0 78.2 %all-gather.9.cloned.1.call-start = ((), (), s32[]{:S(2)}) async-start(), calls=%async_computation.9 | async-start | bytes 2621440 | tf_op jit(solution)/shard_map/all_gather | solution.py:1018
  161.8 2.0 copy-start.6
  161.8 2.0 collective-permute-start.11
  163.8 0.8 copy-start.14
  171.5 14.1 %all-to-all-start.6 = ((bf16[8,16,2048]{2,1,0:T(8,128)(2,1)}), bf16[8,16,2048]{2,1,0:T(8,128)(2,1)S(1)}, u32[]{:S(2)}, u32[]{:S(2)}) async-start(bf16[8,16,2048]{2,1,0:T(8,128)(2,1)} %bitcast.53), calls=%async_computation.6 | async-start | bytes 1048576 | tf_op jit(solution)/shard_map/all_to_all | solution.py:907
  182.0 51.9 %collective-permute-start.18 = (bf16[2,3,128,1024]{3,2,1,0:T(8,128)(2,1)}, bf16[2,3,128,1024]{3,2,1,0:T(8,128)(2,1)}, u32[]{:S(2)}, u32[]{:S(2)}) collective-permute-start(bf16[2,3,128,1024]{3,2,1,0:T(8,128)(2,1)} %get-tuple-element.102), channel_id=1, source_target_pairs={{0,8},{8,0},{1,9},{9,1},{2,10},{10,2},{3,11},{11,3},{4,12},{12,4},... | collective-permute-start | bytes 4718600 | tf_op jit(solution)/shard_map/ppermute | solution.py:916
  185.7 0.8 copy-start.7
  190.3 2.7 %copy-start.5 = (f32[9,16,128]{2,1,0:T(8,128)S(1)}, f32[9,16,128]{2,1,0:T(8,128)}, u32[]{:S(2)}) copy-start(f32[9,16,128]{2,1,0:T(8,128)} %get-tuple-element.92.refs_0_.refs_1_) | copy-start | bytes 221188
  190.3 2.7 %collective-permute-start.15 = (f32[9,16,128]{2,1,0:T(8,128)}, f32[9,16,128]{2,1,0:T(8,128)S(1)}, u32[]{:S(2)}, u32[]{:S(2)}) collective-permute-start(f32[9,16,128]{2,1,0:T(8,128)} %get-tuple-element.99), channel_id=1, source_target_pairs={{0,8},{8,0},{1,9},{9,1},{2,10},{10,2},{3,11},{11,3},{4,12},{12,4},... | collective-permute-start | bytes 221192 | tf_op jit(solution)/shard_map/ppermute | solution.py:916
  190.3 12.2 %collective-permute-start.14 = (bf16[128,1536]{1,0:T(8,128)(2,1)}, bf16[128,1536]{1,0:T(8,128)(2,1)S(1)}, u32[]{:S(2)}, u32[]{:S(2)}) collective-permute-start(bf16[128,1536]{1,0:T(8,128)(2,1)} %pin.9), channel_id=1, source_target_pairs={{0,96},{32,0},{64,32},{96,64},{1,97},{33,1},{65,33},{97,65},{2,98}... | collective-permute-start | bytes 1179656 | tf_op jit(solution)/shard_map/ppermute | solution.py:922
  191.5 13.7 %collective-permute-start.13 = (bf16[128,1536]{1,0:T(8,128)(2,1)}, bf16[128,1536]{1,0:T(8,128)(2,1)S(1)}, u32[]{:S(2)}, u32[]{:S(2)}) collective-permute-start(bf16[128,1536]{1,0:T(8,128)(2,1)} %pin.8), channel_id=1, source_target_pairs={{0,64},{32,96},{64,0},{96,32},{1,65},{33,97},{65,1},{97,33},{2,66}... | collective-permute-start | bytes 1179656 | tf_op jit(solution)/shard_map/ppermute | solution.py:922
  193.0 19.8 %collective-permute-start.12 = (bf16[128,1536]{1,0:T(8,128)(2,1)}, bf16[128,1536]{1,0:T(8,128)(2,1)S(1)}, u32[]{:S(2)}, u32[]{:S(2)}) collective-permute-start(bf16[128,1536]{1,0:T(8,128)(2,1)} %pin.7), channel_id=1, source_target_pairs={{0,32},{32,64},{64,96},{96,0},{1,33},{33,65},{65,97},{97,1},{2,34}... | collective-permute-start | bytes 1179656 | tf_op jit(solution)/shard_map/ppermute | solution.py:922
  193.1 1.6 copy-start.13
  193.1 5.9 %collective-permute-start.20 = (f32[5,16,128]{2,1,0:T(8,128)S(1)}, f32[5,16,128]{2,1,0:T(8,128)S(1)}, u32[]{:S(2)}, u32[]{:S(2)}) collective-permute-start(f32[5,16,128]{2,1,0:T(8,128)S(1)} %pad_maximum_fusion), channel_id=1, source_target_pairs={{0,16},{16,0},{1,17},{17,1},{2,18},{18,2},{3,19},{19,3},{4,20},{20... | collective-permute-start | bytes 122888 | tf_op jit(solution)/shard_map/ppermute | solution.py:916
  194.6 49.4 %all-to-all-start.7 = ((bf16[8,64,2048]{2,1,0:T(8,128)(2,1)}), bf16[8,64,2048]{2,1,0:T(8,128)(2,1)}, u32[]{:S(2)}, u32[]{:S(2)}) async-start(bf16[8,64,2048]{2,1,0:T(8,128)(2,1)} %get-tuple-element.93), calls=%async_computation.7 | async-start | bytes 4194304 | tf_op jit(solution)/shard_map/all_to_all | solution.py:907
  202.5 10.3 %copy-start.9 = (bf16[128,1536]{1,0:T(8,128)(2,1)}, bf16[128,1536]{1,0:T(8,128)(2,1)S(1)}, u32[]{:S(2)}) copy-start(bf16[128,1536]{1,0:T(8,128)(2,1)S(1)} %collective-permute-done.14.refs_3_.refs_11_) | copy-start | bytes 1179652
  205.2 7.6 %copy-start.10 = (bf16[128,1536]{1,0:T(8,128)(2,1)}, bf16[128,1536]{1,0:T(8,128)(2,1)S(1)}, u32[]{:S(2)}) copy-start(bf16[128,1536]{1,0:T(8,128)(2,1)S(1)} %collective-permute-done.13.refs_2_.refs_10_) | copy-start | bytes 1179652
  217.4 13.6 %collective-permute-start.16 = (bf16[2,4,128,256]{3,2,1,0:T(8,128)(2,1)}, bf16[2,4,128,256]{3,2,1,0:T(8,128)(2,1)}, u32[]{:S(2)}, u32[]{:S(2)}) collective-permute-start(bf16[2,4,128,256]{3,2,1,0:T(8,128)(2,1)} %get-tuple-element.101), channel_id=1, source_target_pairs={{0,8},{8,0},{1,9},{9,1},{2,10},{10,2},{3,11},{11,3},{4,12},{12,4},... | collective-permute-start | bytes 1572872 | tf_op jit(solution)/shard_map/ppermute | solution.py:916
  217.6 5.0 %collective-permute-start.21 = (f32[2,16,128]{2,1,0:T(8,128)S(1)}, f32[2,16,128]{2,1,0:T(8,128)S(1)}, u32[]{:S(2)}, u32[]{:S(2)}) collective-permute-start(f32[2,16,128]{2,1,0:T(8,128)S(1)} %get-tuple-element.141), channel_id=1, source_target_pairs={{0,32},{32,64},{64,96},{96,0},{1,33},{33,65},{65,97},{97,1},{2,34}... | collective-permute-start | bytes 49160 | tf_op jit(solution)/shard_map/ppermute | solution.py:922
  217.7 5.3 %collective-permute-start.22 = (f32[2,16,128]{2,1,0:T(8,128)S(1)}, f32[2,16,128]{2,1,0:T(8,128)S(1)}, u32[]{:S(2)}, u32[]{:S(2)}) collective-permute-start(f32[2,16,128]{2,1,0:T(8,128)S(1)} %get-tuple-element.142), channel_id=1, source_target_pairs={{0,64},{32,96},{64,0},{96,32},{1,65},{33,97},{65,1},{97,33},{2,66}... | collective-permute-start | bytes 49160 | tf_op jit(solution)/shard_map/ppermute | solution.py:922
  219.6 4.0 %collective-permute-start.23 = (f32[2,16,128]{2,1,0:T(8,128)S(1)}, f32[2,16,128]{2,1,0:T(8,128)S(1)}, u32[]{:S(2)}, u32[]{:S(2)}) collective-permute-start(f32[2,16,128]{2,1,0:T(8,128)S(1)} %get-tuple-element.143), channel_id=1, source_target_pairs={{0,96},{32,0},{64,32},{96,64},{1,97},{33,1},{65,33},{97,65},{2,98}... | collective-permute-start | bytes 49160 | tf_op jit(solution)/shard_map/ppermute | solution.py:922
  223.7 3.7 %collective-permute-start.24 = (f32[2,16,128]{2,1,0:T(8,128)S(1)}, f32[2,16,128]{2,1,0:T(8,128)S(1)}, u32[]{:S(2)}, u32[]{:S(2)}) collective-permute-start(f32[2,16,128]{2,1,0:T(8,128)S(1)} %fusion.5), channel_id=1, source_target_pairs={{0,4},{4,0},{1,5},{5,1},{2,6},{6,2},{3,7},{7,3},{8,12},{12,8},{9,1... | collective-permute-start | bytes 49160 | tf_op jit(solution)/shard_map/ppermute | solution.py:975
  224.2 9.7 %copy-start = (f32[2,3,128,1024]{3,2,1,0:T(8,128)S(1)}, f32[2,3,128,1024]{3,2,1,0:T(8,128)}, u32[]{:S(2)}) copy-start(f32[2,3,128,1024]{3,2,1,0:T(8,128)} %get-tuple-element.91.refs_9_) | copy-start | bytes 9437188
  227.4 10.7 %collective-permute-start.25 = (f32[2,16,128]{2,1,0:T(8,128)S(1)}, f32[2,16,128]{2,1,0:T(8,128)S(1)}, u32[]{:S(2)}, u32[]{:S(2)}) collective-permute-start(f32[2,16,128]{2,1,0:T(8,128)S(1)} %add.126), channel_id=1, source_target_pairs={{0,1},{1,2},{2,3},{3,0},{4,5},{5,6},{6,7},{7,4},{8,9},{9,10},{10,1... | collective-permute-start | bytes 49160 | tf_op jit(solution)/shard_map/ppermute | solution.py:975
  228.2 10.0 %collective-permute-start.26 = (f32[2,16,128]{2,1,0:T(8,128)S(1)}, f32[2,16,128]{2,1,0:T(8,128)S(1)}, u32[]{:S(2)}, u32[]{:S(2)}) collective-permute-start(f32[2,16,128]{2,1,0:T(8,128)S(1)} %add.126), channel_id=1, source_target_pairs={{0,2},{1,3},{2,0},{3,1},{4,6},{5,7},{6,4},{7,5},{8,10},{9,11},{10,... | collective-permute-start | bytes 49160 | tf_op jit(solution)/shard_map/ppermute | solution.py:975
  230.0 8.1 %collective-permute-start.27 = (f32[2,16,128]{2,1,0:T(8,128)S(1)}, f32[2,16,128]{2,1,0:T(8,128)S(1)}, u32[]{:S(2)}, u32[]{:S(2)}) collective-permute-start(f32[2,16,128]{2,1,0:T(8,128)S(1)} %add.126), channel_id=1, source_target_pairs={{0,3},{1,0},{2,1},{3,2},{4,7},{5,4},{6,5},{7,6},{8,11},{9,8},{10,9... | collective-permute-start | bytes 49160 | tf_op jit(solution)/shard_map/ppermute | solution.py:975
  230.9 10.6 %copy-start.12 = (f32[2,4,128,256]{3,2,1,0:T(8,128)S(1)}, f32[2,4,128,256]{3,2,1,0:T(8,128)}, u32[]{:S(2)}) copy-start(f32[2,4,128,256]{3,2,1,0:T(8,128)} %get-tuple-element.100) | copy-start | bytes 3145732
  232.2 9.3 %collective-permute-start.17 = (bf16[4,128,256]{2,1,0:T(8,128)(2,1)S(1)}, bf16[4,128,256]{2,1,0:T(8,128)(2,1)S(1)}, u32[]{:S(2)}, u32[]{:S(2)}) collective-permute-start(bf16[4,128,256]{2,1,0:T(8,128)(2,1)S(1)} %fusion.1), channel_id=1, source_target_pairs={{0,16},{16,0},{1,17},{17,1},{2,18},{18,2},{3,19},{19,3},{4,20},{20... | collective-permute-start | bytes 786440 | tf_op jit(solution)/shard_map/ppermute | solution.py:916
  236.2 21.0 %collective-permute-start.19 = (bf16[3,128,1024]{2,1,0:T(8,128)(2,1)}, bf16[3,128,1024]{2,1,0:T(8,128)(2,1)}, u32[]{:S(2)}, u32[]{:S(2)}) collective-permute-start(bf16[3,128,1024]{2,1,0:T(8,128)(2,1)} %fusion), channel_id=1, source_target_pairs={{0,16},{16,0},{1,17},{17,1},{2,18},{18,2},{3,19},{19,3},{4,20},{20... | collective-permute-start | bytes 2359304 | tf_op jit(solution)/shard_map/ppermute | solution.py:916
  (6 other events, 4.1 us)
Sparse Core Ops, SparseCore 0:
  48.7 43.1 all-gather.6
  96.4 44.9 all-gather.10
  149.1 27.2 all-gather.8
